TPU v7x, 32 devices: a whole 2x2x4 slice. The times are simulated.
32 devices in a mesh: seq: 2 (over y), fsdp: 16 (over z, x, core).
Axes of the slice: x: 2, y: 2, z: 4, core: 2. Of those that a mesh axis runs over, the one named last changes fastest.
Arguments:
- tokens: bfloat16 [2, 16, 256, 1792], P(None, 'fsdp', 'seq'), may hold values from -6 to 6
- seq_order: int32 [2, 16, 2, 128], P(None, 'fsdp', 'seq'), may hold values from 0 to 127, each once within a row
- seq_lengths: int32 [2, 16, 4], P(None, 'fsdp'), may hold values from 1 to 253, as said below
- valid_count: int32 [2, 16], P(None, 'fsdp'), may hold values from 32 to 246, as said below
- teacher: bfloat16 [2, 16, 256, 1792], P(None, 'fsdp', 'seq'), may hold values from -6 to 6
- norm_one: bfloat16 [1792], P('fsdp'), may hold values from 0.099609375 to 1.8984375
- w_query: bfloat16 [1792, 256], P('fsdp'), may hold values from -0.125 to 0.125
- w_key: bfloat16 [1792, 256], P('fsdp'), may hold values from -0.125 to 0.125
- w_value: bfloat16 [1792, 1792], P('fsdp'), may hold values from -0.125 to 0.125
- conv_taps: bfloat16 [3, 1792], P(None, 'fsdp'), may hold values from -3 to 3
- w_out: bfloat16 [1792, 1792], P('fsdp'), may hold values from -2 to 2
- norm_two: bfloat16 [1792], P('fsdp'), may hold values from 0.099609375 to 1.8984375
- w_gate: bfloat16 [1792, 4864], P('fsdp'), may hold values from -0.125 to 0.125
- w_up: bfloat16 [1792, 4864], P('fsdp'), may hold values from -0.125 to 0.125
- w_down: bfloat16 [4864, 1792], P('fsdp'), may hold values from -0.078125 to 0.078125
Outputs:
- output: bfloat16 [2, 16, 256, 1792], P(None, 'fsdp', 'seq')
- input_grad: bfloat16 [2, 16, 256, 1792], P(None, 'fsdp', 'seq')
- grad_norm_one: float32 [1792], P('fsdp')
- grad_w_query: float32 [1792, 256], P('fsdp')
- grad_w_key: float32 [1792, 256], P('fsdp')
- grad_w_value: float32 [1792, 1792], P('fsdp')
- grad_conv_taps: float32 [3, 1792], P(None, 'fsdp')
- grad_w_out: float32 [1792, 1792], P('fsdp')
- grad_norm_two: float32 [1792], P('fsdp')
- grad_w_gate: float32 [1792, 4864], P('fsdp')
- grad_w_up: float32 [1792, 4864], P('fsdp')
- grad_w_down: float32 [4864, 1792], P('fsdp')
- loss: float32 [], replicated
Inputs may be any that keep to these rules, and one draw needn't show every extreme that they name: `seq_lengths`: in each micro-batch and group the 4 lengths are positive and sum to 256; all but one of them are at most 10. `valid_count`: the loss counts, in each micro-batch and group, the tokens whose given position in the group is below this count. `seq_order`: each row of 128 entries is a permutation.
All inputs are finite; a program needn't handle non-finite values.
Results may differ from a plain program's by a relative error of at most 0.015.
Values may be sent and summed in bfloat16 or wider, within the bound.
No kernel may reach another device: no remote copies, remote signals or barrier semaphores. Data moves between devices by JAX's collectives and lax.ppermute only.
A program may use at most 384 MiB of HBM per device.

v0:
```python
from functools import partial

import jax
import jax.numpy as jnp
from jax import lax
from jax.sharding import PartitionSpec as P

HEADS = 16
FEAT = 16
HEAD_SIZE = 112


HIGHEST = lax.Precision.HIGHEST
TRIPLE = lax.Precision.HIGH
EPSILON = 1e-05
QUADRATIC = 0.1767766952966369


def shifted(value, axis, by):
    peers = lax.axis_size(axis)
    pairs = [(i, i + by) for i in range(peers) if 0 <= i + by < peers]
    return lax.ppermute(value, axis, pairs)


def carried_in(value, axis, combine, identity):
    peers, index = (lax.axis_size(axis), lax.axis_index(axis))
    everything = jax.tree.map(
        lambda part, kind: lax.all_gather(part.astype(kind), axis),
        value,
        (jnp.bfloat16, jnp.bfloat16, jnp.bfloat16),
    )
    start = jax.tree.map(
        lambda part, zero: jnp.broadcast_to(jnp.asarray(zero, part.dtype), part.shape),
        value,
        identity,
    )

    def carried_hop(k, before):
        reached = k < index
        new = combine(
            before, jax.tree.map(lambda part, own: part[k].astype(own.dtype), everything, value)
        )
        return jax.tree.map(lambda a, b: jnp.where(reached, a, b), new, before)

    return lax.fori_loop(0, peers, carried_hop, start)


def prefix(value, axis, combine, identity):
    peers, index = (lax.axis_size(axis), lax.axis_index(axis))
    everything = jax.tree.map(
        lambda part, kind: lax.all_gather(part.astype(kind), axis),
        value,
        jax.tree.map(lambda a: jnp.bfloat16 if a.dtype == jnp.float32 else a.dtype, value),
    )
    start = jax.tree.map(
        lambda part, zero: jnp.broadcast_to(jnp.asarray(zero, part.dtype), part.shape),
        value,
        identity,
    )

    def prefix_hop(k, before):
        at = peers - 1 - k
        reached = at > index
        new = combine(
            before, jax.tree.map(lambda part, own: part[at].astype(own.dtype), everything, value)
        )
        return jax.tree.map(lambda a, b: jnp.where(reached, a, b), new, before)

    return lax.fori_loop(0, peers, prefix_hop, start)


def rms_norm(values, gain):
    return values * lax.rsqrt(jnp.mean(values * values, axis=-1, keepdims=True) + EPSILON) * gain


def feature_map(vectors):
    leading = vectors.shape[:-1]
    feat_width = vectors.shape[-1]
    outer_prod = (vectors[..., :, None] * vectors[..., None, :]).reshape(
        leading + (feat_width * feat_width,)
    )
    return jnp.concatenate(
        [jnp.ones(leading + (1,), jnp.float32), 0.5 * vectors, QUADRATIC * outer_prod], axis=-1
    )


def segment_ids(seq_ends, positions):
    return jnp.sum((positions[:, None] >= seq_ends[None, :]).astype(jnp.int32), axis=1)


def project(left, weight):
    return jnp.dot(left, weight, preferred_element_type=jnp.float32)


def weight_grad(left, right):
    return lax.dot_general(
        left, right, (((0,), (0,)), ((), ())), preferred_element_type=jnp.float32
    )


def back_project(grads, weight):
    return lax.dot_general(
        grads, weight, (((1,), (1,)), ((), ())), preferred_element_type=jnp.float32
    )


def attend(scores, queries, value_heads, carry_state, carry_norm, allowed, continuing):
    kernel = (1.0 + scores + 0.5 * scores * scores) * allowed[None]
    features = feature_map(queries)
    numerator = jnp.einsum("htu,uhe->the", kernel, value_heads, precision=TRIPLE)
    numerator = numerator + continuing[:, None, None] * jnp.einsum(
        "thp,hpe->the", features, carry_state, precision=TRIPLE
    )
    denominator = jnp.transpose(jnp.sum(kernel, axis=2)) + continuing[:, None] * jnp.einsum(
        "thp,hp->th", features, carry_norm, precision=HIGHEST
    )
    return numerator / denominator[:, :, None]


def tail_summary(keys_rows, value_heads, tail_rows):
    features = feature_map(keys_rows) * tail_rows[:, None, None]
    return (
        jnp.einsum("thp,the->hpe", features, value_heads, precision=TRIPLE),
        jnp.sum(features, axis=0),
    )


def carry_combine(earlier, later):
    keep_part = 1.0 - later[2]
    return (
        later[0] + keep_part * earlier[0],
        later[1] + keep_part * earlier[1],
        jnp.maximum(earlier[2], later[2]),
    )


def short_conv(extended, taps, near_one, near_two):
    return (
        taps[0] * extended[2:]
        + taps[1] * extended[1:-1] * near_one[:, None]
        + taps[2] * extended[:-2] * near_two[:, None]
    )


def gate_mix(attended, conv_out):
    return attended * jax.nn.silu(conv_out)


def swiglu(gate_proj, up_proj):
    return jax.nn.silu(gate_proj) * up_proj


def gather_weights(shards):
    return (
        lax.all_gather(shards[0], "fsdp", axis=0, tiled=True),
        lax.all_gather(shards[1], "fsdp", axis=0, tiled=True),
        lax.all_gather(shards[2], "fsdp", axis=0, tiled=True),
        lax.all_gather(shards[3], "fsdp", axis=0, tiled=True),
        lax.all_gather(shards[4], "fsdp", axis=1, tiled=True),
        lax.all_gather(shards[5], "fsdp", axis=0, tiled=True),
        lax.all_gather(shards[6], "fsdp", axis=0, tiled=True),
        lax.all_gather(shards[7], "fsdp", axis=0, tiled=True),
        lax.all_gather(shards[8], "fsdp", axis=0, tiled=True),
        lax.all_gather(shards[9], "fsdp", axis=0, tiled=True),
    )


def on_device(
    tokens,
    seq_order,
    seq_lengths,
    valid_count,
    teacher,
    norm_one,
    w_query,
    w_key,
    w_value,
    conv_taps,
    w_out,
    norm_two,
    w_gate,
    w_up,
    w_down,
):
    shards = (norm_one, w_query, w_key, w_value, conv_taps, w_out, norm_two, w_gate, w_up, w_down)
    micro = tokens.shape[0]
    rows_dev = tokens.shape[2]
    model_width = tokens.shape[3]
    fsdp_size = lax.axis_size("fsdp")
    row_start = lax.axis_index("seq") * rows_dev
    positions = row_start + jnp.arange(rows_dev, dtype=jnp.int32)
    in_loss = (positions[None, :] < valid_count).astype(jnp.float32)
    total = lax.psum(jnp.sum(in_loss), ("seq", "fsdp"))
    slots = micro * fsdp_size * lax.axis_size("seq") * rows_dev
    scale = slots / total
    gathered_dims = (0, 0, 0, 0, 1, 0, 0, 0, 0, 0)
    grad_sums = []
    for weight_shard, shard_dim in zip(shards, gathered_dims):
        full_shape = list(weight_shard.shape)
        full_shape[shard_dim] = full_shape[shard_dim] * fsdp_size
        grad_sums.append(jnp.zeros(tuple(full_shape), jnp.float32))
    out_rows = []
    grad_rows = []
    squares = jnp.float32(0.0)
    ext_index = row_start - 2 + jnp.arange(rows_dev + 2, dtype=jnp.int32)
    local_index = jnp.arange(rows_dev, dtype=jnp.int32)
    for micro_step in range(micro):
        current = gather_weights(shards)
        gain_one, query_w, key_w, value_w, taps_w, out_w, gain_two, gate_w, up_w, down_w = current
        order_rows = seq_order[micro_step, 0, 0]
        inverse = jnp.zeros((rows_dev,), jnp.int32).at[order_rows].set(local_index)
        packed = tokens[micro_step, 0][order_rows].astype(jnp.float32)
        seq_ends = jnp.cumsum(seq_lengths[micro_step, 0])
        segment = segment_ids(seq_ends, positions)
        segment_ext = jnp.where(ext_index >= 0, segment_ids(seq_ends, ext_index), -1)
        near_one = (segment_ext[1:-1] == segment_ext[2:]).astype(jnp.float32)
        near_two = (segment_ext[:-2] == segment_ext[2:]).astype(jnp.float32)
        prev_segment = segment_ext[1]
        continuing = (segment == prev_segment).astype(jnp.float32)
        tail_rows = (segment == segment[rows_dev - 1]).astype(jnp.float32)
        start_flag = (segment[rows_dev - 1] != prev_segment).astype(jnp.float32)
        allowed = (
            (segment[:, None] == segment[None, :]) & (positions[:, None] >= positions[None, :])
        ).astype(jnp.float32)
        normed_one, norm_one_pull = jax.vjp(rms_norm, packed, gain_one.astype(jnp.float32))
        n_one = normed_one.astype(jnp.bfloat16)
        queries = project(n_one, query_w).astype(jnp.bfloat16)
        keys_rows = project(n_one, key_w).astype(jnp.bfloat16)
        values = project(n_one, value_w).astype(jnp.bfloat16)
        halo_rows = shifted(values[rows_dev - 2 :], "seq", 1)
        extended = jnp.concatenate([halo_rows, values], axis=0).astype(jnp.float32)
        conv_out, conv_pull = jax.vjp(
            partial(short_conv, near_one=near_one, near_two=near_two),
            extended,
            taps_w.astype(jnp.float32),
        )
        query_low_heads = queries.reshape(rows_dev, HEADS, FEAT)
        key_low_heads = keys_rows.reshape(rows_dev, HEADS, FEAT)
        query_heads = query_low_heads.astype(jnp.float32)
        key_heads = key_low_heads.astype(jnp.float32)
        value_heads = values.astype(jnp.float32).reshape(rows_dev, HEADS, HEAD_SIZE)
        scores = (
            jnp.einsum(
                "thf,uhf->htu", query_low_heads, key_low_heads, preferred_element_type=jnp.float32
            )
            * 0.25
        )
        summary, tail_pull = jax.vjp(
            partial(tail_summary, tail_rows=tail_rows), key_heads, value_heads
        )
        blank = (jnp.zeros_like(summary[0]), jnp.zeros_like(summary[1]), jnp.float32(0.0))
        carried = carried_in((summary[0], summary[1], start_flag), "seq", carry_combine, blank)
        attended, attend_pull = jax.vjp(
            partial(attend, allowed=allowed, continuing=continuing),
            scores,
            query_heads,
            value_heads,
            carried[0],
            carried[1],
        )
        mixed_rows, mix_pull = jax.vjp(gate_mix, attended.reshape(rows_dev, model_width), conv_out)
        mixed_low = mixed_rows.astype(jnp.bfloat16)
        residual = packed + project(mixed_low, out_w)
        normed_two, norm_two_pull = jax.vjp(rms_norm, residual, gain_two.astype(jnp.float32))
        n_two = normed_two.astype(jnp.bfloat16)
        hidden, glu_pull = jax.vjp(swiglu, project(n_two, gate_w), project(n_two, up_w))
        hidden_low = hidden.astype(jnp.bfloat16)
        result = (residual + project(hidden_low, down_w))[inverse]
        out_rows.append(result.astype(jnp.bfloat16))
        deviation = (result - teacher[micro_step, 0].astype(jnp.float32)) * in_loss[micro_step][
            :, None
        ]
        squares = squares + jnp.sum(deviation * deviation)
        grad_result = (scale * deviation)[order_rows]
        current = gather_weights(shards)
        gain_one, query_w, key_w, value_w, taps_w, out_w, gain_two, gate_w, up_w, down_w = current
        down_low = grad_result.astype(jnp.bfloat16)
        grad_sums[9] = grad_sums[9] + weight_grad(hidden_low, down_low)
        d_gate, d_up = glu_pull(back_project(down_low, down_w))
        gate_low = d_gate.astype(jnp.bfloat16)
        up_low = d_up.astype(jnp.bfloat16)
        grad_sums[7] = grad_sums[7] + weight_grad(n_two, gate_low)
        grad_sums[8] = grad_sums[8] + weight_grad(n_two, up_low)
        d_resid, d_gain_two = norm_two_pull(
            back_project(gate_low, gate_w) + back_project(up_low, up_w)
        )
        d_resid = d_resid + grad_result
        resid_low = d_resid.astype(jnp.bfloat16)
        grad_sums[5] = grad_sums[5] + weight_grad(mixed_low, resid_low)
        d_attended, d_conv = mix_pull(back_project(resid_low, out_w))
        d_scores, d_query_feat, d_value, d_state, d_norm = attend_pull(
            d_attended.reshape(rows_dev, HEADS, HEAD_SIZE)
        )
        d_query = d_query_feat + 0.25 * jnp.einsum(
            "htu,uhf->thf", d_scores, key_heads, precision=TRIPLE
        )
        d_key = 0.25 * jnp.einsum("htu,thf->uhf", d_scores, query_heads, precision=TRIPLE)
        back_carry = prefix((d_state, d_norm, start_flag), "seq", carry_combine, blank)
        d_key_tail, d_value_tail = tail_pull((back_carry[0], back_carry[1]))
        d_extended, d_taps = conv_pull(d_conv)
        spill = shifted(d_extended[:2], "seq", -1)
        d_value_all = (d_value + d_value_tail).reshape(rows_dev, model_width) + d_extended[2:]
        d_value_all = d_value_all + jnp.concatenate(
            [jnp.zeros((rows_dev - 2, model_width), jnp.float32), spill], axis=0
        )
        query_low = d_query.reshape(rows_dev, HEADS * FEAT).astype(jnp.bfloat16)
        key_low = (d_key + d_key_tail).reshape(rows_dev, HEADS * FEAT).astype(jnp.bfloat16)
        value_low = d_value_all.astype(jnp.bfloat16)
        grad_sums[1] = grad_sums[1] + weight_grad(n_one, query_low)
        grad_sums[2] = grad_sums[2] + weight_grad(n_one, key_low)
        grad_sums[3] = grad_sums[3] + weight_grad(n_one, value_low)
        d_normed = (
            back_project(query_low, query_w)
            + back_project(key_low, key_w)
            + back_project(value_low, value_w)
        )
        d_packed, d_gain_one = norm_one_pull(d_normed)
        d_packed = d_packed + d_resid
        grad_rows.append(d_packed[inverse].astype(jnp.bfloat16))
        grad_sums[0] = grad_sums[0] + d_gain_one
        grad_sums[4] = grad_sums[4] + d_taps
        grad_sums[6] = grad_sums[6] + d_gain_two
    summed = (
        lax.psum_scatter(
            grad_sums[0].astype(jnp.bfloat16), "fsdp", scatter_dimension=0, tiled=True
        ).astype(jnp.float32),
        lax.psum_scatter(
            grad_sums[1].astype(jnp.bfloat16), "fsdp", scatter_dimension=0, tiled=True
        ).astype(jnp.float32),
        lax.psum_scatter(
            grad_sums[2].astype(jnp.bfloat16), "fsdp", scatter_dimension=0, tiled=True
        ).astype(jnp.float32),
        lax.psum_scatter(
            grad_sums[3].astype(jnp.bfloat16), "fsdp", scatter_dimension=0, tiled=True
        ).astype(jnp.float32),
        lax.psum_scatter(
            grad_sums[4].astype(jnp.bfloat16), "fsdp", scatter_dimension=1, tiled=True
        ).astype(jnp.float32),
        lax.psum_scatter(
            grad_sums[5].astype(jnp.bfloat16), "fsdp", scatter_dimension=0, tiled=True
        ).astype(jnp.float32),
        lax.psum_scatter(
            grad_sums[6].astype(jnp.bfloat16), "fsdp", scatter_dimension=0, tiled=True
        ).astype(jnp.float32),
        lax.psum_scatter(
            grad_sums[7].astype(jnp.bfloat16), "fsdp", scatter_dimension=0, tiled=True
        ).astype(jnp.float32),
        lax.psum_scatter(
            grad_sums[8].astype(jnp.bfloat16), "fsdp", scatter_dimension=0, tiled=True
        ).astype(jnp.float32),
        lax.psum_scatter(
            grad_sums[9].astype(jnp.bfloat16), "fsdp", scatter_dimension=0, tiled=True
        ).astype(jnp.float32),
    )
    reduced = (
        lax.psum(summed[0].astype(jnp.bfloat16), "seq").astype(jnp.float32),
        lax.psum(summed[1].astype(jnp.bfloat16), "seq").astype(jnp.float32),
        lax.psum(summed[2].astype(jnp.bfloat16), "seq").astype(jnp.float32),
        lax.psum(summed[3].astype(jnp.bfloat16), "seq").astype(jnp.float32),
        lax.psum(summed[4].astype(jnp.bfloat16), "seq").astype(jnp.float32),
        lax.psum(summed[5].astype(jnp.bfloat16), "seq").astype(jnp.float32),
        lax.psum(summed[6].astype(jnp.bfloat16), "seq").astype(jnp.float32),
        lax.psum(summed[7].astype(jnp.bfloat16), "seq").astype(jnp.float32),
        lax.psum(summed[8].astype(jnp.bfloat16), "seq").astype(jnp.float32),
        lax.psum(summed[9].astype(jnp.bfloat16), "seq").astype(jnp.float32),
    )
    loss = lax.psum(squares, ("seq", "fsdp")) / (total * model_width)
    output = jnp.stack(out_rows)[:, None]
    input_grad = jnp.stack(grad_rows)[:, None]
    return (
        output,
        input_grad,
        reduced[0],
        reduced[1],
        reduced[2],
        reduced[3],
        reduced[4],
        reduced[5],
        reduced[6],
        reduced[7],
        reduced[8],
        reduced[9],
        loss,
    )


def solution(mesh):
    placed = (
        P(None, "fsdp", "seq", None),
        P(None, "fsdp", "seq", None),
        P(None, "fsdp", None),
        P(None, "fsdp"),
        P(None, "fsdp", "seq", None),
        P("fsdp"),
        P("fsdp", None),
        P("fsdp", None),
        P("fsdp", None),
        P(None, "fsdp"),
        P("fsdp", None),
        P("fsdp"),
        P("fsdp", None),
        P("fsdp", None),
        P("fsdp", None),
    )
    return jax.shard_map(
        on_device,
        mesh=mesh,
        in_specs=placed,
        out_specs=(
            P(None, "fsdp", "seq", None),
            P(None, "fsdp", "seq", None),
            P("fsdp"),
            P("fsdp", None),
            P("fsdp", None),
            P("fsdp", None),
            P(None, "fsdp"),
            P("fsdp", None),
            P("fsdp"),
            P("fsdp", None),
            P("fsdp", None),
            P("fsdp", None),
            P(),
        ),
        check_vma=False,
    )
```

profile of v0, /device:TPU:0, one launch (start us, length us, event | category | flops | bytes accessed | tf_op | source)
XLA Modules:
  0.0 1836.7 jit_solution(3418204324439645131)
XLA Ops:
  12.8 36.6 %all-reduce.22 = (bf16[1792]{0:T(1024)(128)(2,1)S(1)}, bf16[1792]{0:T(1024)(128)(2,1)}) all-reduce(bf16[1792]{0:T(1024)(128)(2,1)S(1)} %dynamic-update-slice, bf16[1792]{0:T(1024)(128)(2,1)S(1)} %dynamic-update-slice.2), channel_id=1, replica_groups=mesh['seq'=2,'fsdp'=16] {'fsdp'}, use_global_device_ids=true, to_apply=%add.14 | all-reduce | flops 3584 | bytes 14336
  52.5 24.6 %all_gather.117 = bf16[1792,256]{1,0:T(8,128)(2,1)S(1)} all-gather(bf16[112,256]{1,0:T(8,128)(2,1)S(1)} %copy-done.149), channel_id=1, replica_groups=mesh['seq'=2,'fsdp'=16] {'fsdp'}, dimensions={0}, use_global_device_ids=true | all-gather | bytes 974848 | tf_op jit(solution)/shard_map/all_gather | solution.py:157
  121.6 20.4 %all_gather.116 = bf16[1792,256]{1,0:T(8,128)(2,1)S(1)} all-gather(bf16[112,256]{1,0:T(8,128)(2,1)} %param.29), channel_id=1, replica_groups=mesh['seq'=2,'fsdp'=16] {'fsdp'}, dimensions={0}, use_global_device_ids=true | all-gather | bytes 974848 | tf_op jit(solution)/shard_map/all_gather | solution.py:156
  145.5 19.0 %all-gather.8 = bf16[16,112,3]{1,2,0:T(4,128)(2,1)S(1)} all-gather(bf16[1,112,3]{1,2,0:T(4,128)(2,1)} %bitcast.442), channel_id=1, replica_groups=mesh['seq'=2,'fsdp'=16] {'fsdp'}, dimensions={0}, use_global_device_ids=true | all-gather | bytes 11424 | tf_op jit(solution)/shard_map/all_gather | solution.py:159
  204.4 11.9 while.68
  227.5 11.1 while.69
  263.0 59.3 %all-gather.23.cloned.1.call-done = bf16[1792,4864]{1,0:T(8,128)(2,1)} async-done(((bf16[112,4864]{1,0:T(8,128)(2,1)}), bf16[1792,4864]{1,0:T(8,128)(2,1)}) %all-gather.23.cloned.1.call-update) | async-done | bytes 17432592 | tf_op jit(solution)/shard_map/all_gather | solution.py:162
  332.2 83.7 %all-gather.25.cloned.1.call-done = bf16[1792,4864]{1,0:T(8,128)(2,1)} async-done(((bf16[112,4864]{1,0:T(8,128)(2,1)}), bf16[1792,4864]{1,0:T(8,128)(2,1)}) %all-gather.25.cloned.1.call-update) | async-done | bytes 17432592 | tf_op jit(solution)/shard_map/all_gather | solution.py:163
  415.9 11.5 multiply_convert_fusion.3
  427.4 82.3 %all-gather.27.cloned.1.call-done = bf16[4864,1792]{1,0:T(8,128)(2,1)} async-done(((bf16[304,1792]{1,0:T(8,128)(2,1)}), bf16[4864,1792]{1,0:T(8,128)(2,1)}) %all-gather.27.cloned.1.call-update) | async-done | bytes 17432592 | tf_op jit(solution)/shard_map/all_gather | solution.py:164
  529.4 11.2 multiply_convert_fusion.2
  550.4 40.3 %all-reduce.20 = (f32[]{:T(128)}, f32[]{:T(128)}) all-reduce(f32[]{:T(128)} %fusion.136, f32[]{:T(128)S(6)} %add.588), channel_id=1, replica_groups=mesh['seq'=2,'fsdp'=16] {'seq','fsdp'}, use_global_device_ids=true, to_apply=%region_21.22 | all-reduce | flops 2 | bytes 16 | tf_op jit(solution)/shard_map/psum | solution.py:193
  600.7 11.7 multiply_convert_fusion
  612.4 13.0 fusion.165
  625.4 11.7 multiply_convert_fusion.1
  637.1 12.9 fusion.163
  649.9 13.1 convolution_add_fusion.4
  663.1 14.4 multiply_reduce_fusion.11
  826.0 14.0 fusion.167
  840.0 19.5 %add_convert_fusion.2 = bf16[1792,4864]{1,0:T(8,128)(2,1)} fusion(f32[1792,4864]{1,0:T(8,128)} %fusion.167, bf16[128,1792]{1,0:T(8,128)(2,1)S(1)} %copy-done.38, bf16[128,4864]{1,0:T(8,128)(2,1)S(1)} %copy-done.62), kind=kOutput, calls=%fused_computation.36 | convolution fusion | flops 2248802304 | bytes 54001664 | tf_op jit(solution)/shard_map/dot_general | solution.py:96
  860.8 13.8 fusion.168
  874.6 19.8 %add_convert_fusion.1 = bf16[1792,4864]{1,0:T(8,128)(2,1)} fusion(f32[1792,4864]{1,0:T(8,128)} %fusion.168, bf16[128,1792]{1,0:T(8,128)(2,1)S(1)} %copy-done.38, bf16[128,4864]{1,0:T(8,128)(2,1)S(1)} %copy-done.61), kind=kOutput, calls=%fused_computation.35 | convolution fusion | flops 2248802304 | bytes 54001664 | tf_op jit(solution)/shard_map/dot_general | solution.py:96
  895.6 15.2 fusion.94
  910.8 19.4 %add_convert_fusion = bf16[4864,1792]{1,0:T(8,128)(2,1)} fusion(f32[4864,1792]{1,0:T(8,128)} %fusion.94, bf16[128,4864]{1,0:T(8,128)(2,1)S(1)} %copy-done.56, f32[128,1792]{1,0:T(8,128)S(1)} %copy-done.39), kind=kOutput, calls=%fused_computation.34 | convolution fusion | flops 2249031680 | bytes 54460416 | tf_op jit(solution)/shard_map/dot_general | solution.py:96
  946.7 33.4 %all-reduce.21 = (bf16[1792]{0:T(1024)(128)(2,1)S(1)}, bf16[1792]{0:T(1024)(128)(2,1)S(1)}) all-reduce(bf16[1792]{0:T(1024)(128)(2,1)S(1)} %add_convert_fusion.7, bf16[1792]{0:T(1024)(128)(2,1)S(1)} %add_convert_fusion.6), channel_id=10, replica_groups=mesh['seq'=2,'fsdp'=16] {'fsdp'}, use_global_device_ids=true, to_apply=%region_42.43.clone | all-reduce | flops 3584 | bytes 14336
  981.4 53.3 %reduce-scatter.17.cloned.1.call-done = bf16[112,1792]{1,0:T(8,128)(2,1)} async-done(((bf16[1792,1792]{1,0:T(8,128)(2,1)}), bf16[112,1792]{1,0:T(8,128)(2,1)}) %reduce-scatter.17.cloned.1.call-update) | async-done | bytes 401424 | tf_op jit(solution)/shard_map/reduce_scatter | solution.py:339
  1034.7 89.1 %reduce-scatter.15.cloned.1.call-done = bf16[112,1792]{1,0:T(8,128)(2,1)} async-done(((bf16[1792,1792]{1,0:T(8,128)(2,1)}), bf16[112,1792]{1,0:T(8,128)(2,1)}) %reduce-scatter.15.cloned.1.call-update) | async-done | bytes 401424 | tf_op jit(solution)/shard_map/reduce_scatter | solution.py:333
  1123.7 187.4 %reduce-scatter.19.cloned.1.call-done = bf16[112,4864]{1,0:T(8,128)(2,1)} async-done(((bf16[1792,4864]{1,0:T(8,128)(2,1)}), bf16[112,4864]{1,0:T(8,128)(2,1)}) %reduce-scatter.19.cloned.1.call-update) | async-done | bytes 1089552 | tf_op jit(solution)/shard_map/reduce_scatter | solution.py:345
  1311.1 187.5 %reduce-scatter.21.cloned.1.call-done = bf16[112,4864]{1,0:T(8,128)(2,1)} async-done(((bf16[1792,4864]{1,0:T(8,128)(2,1)}), bf16[112,4864]{1,0:T(8,128)(2,1)}) %reduce-scatter.21.cloned.1.call-update) | async-done | bytes 1089552 | tf_op jit(solution)/shard_map/reduce_scatter | solution.py:348
  1498.7 187.6 %reduce-scatter.23.cloned.1.call-done = bf16[304,1792]{1,0:T(8,128)(2,1)} async-done(((bf16[4864,1792]{1,0:T(8,128)(2,1)}), bf16[304,1792]{1,0:T(8,128)(2,1)}) %reduce-scatter.23.cloned.1.call-update) | async-done | bytes 1089552 | tf_op jit(solution)/shard_map/reduce_scatter | solution.py:351
  1694.1 16.1 all-reduce.29.cloned.1.call-done
  1716.6 103.3 %all-reduce.31.cloned.1.call-done = (bf16[112,1792]{1,0:T(8,128)(2,1)}, bf16[112,1792]{1,0:T(8,128)(2,1)}, bf16[112,4864]{1,0:T(8,128)(2,1)}, bf16[112,4864]{1,0:T(8,128)(2,1)}, bf16[304,1792]{1,0:T(8,128)(2,1)}) async-done(((bf16[112,1792]{1,0:T(8,128)(2,1)}, bf16[112,1792]{1,0:T(8,128)(2,1)}, bf16[112,4864]{1,0:T(8,128)(2,1)}, bf16[112,4864]{1,0:T(8,128)(2,1)}, bf16[304,1792]{1,0:T(8,128)(2,1)}), ...) | async-done | bytes 4071440 | tf_op jit(solution)/shard_map/psum | solution.py:359
  (779 shorter events, 398.7 us)
Async XLA Ops:
  7.2 78.7 %all-gather.19.cloned.1.call-start = ((), (), s32[]{:S(2)}) async-start(), calls=%async_computation.8 | async-start | bytes 6823936 | tf_op jit(solution)/shard_map/all_gather | solution.py:158
  7.9 196.5 %all-gather.29.cloned.1.call-start = ((), (), s32[]{:S(2)}) async-start(), calls=%async_computation.20 | async-start | bytes 3354624 | tf_op jit(solution)/shard_map/all_gather | solution.py:28
  49.4 115.2 %copy-start.97 = (f32[1792]{0:T(1024)}, f32[1792]{0:T(1024)S(1)}, u32[]{:S(2)}) copy-start(f32[1792]{0:T(1024)S(1)} %convert_element_type.576) | copy-start | bytes 21508
  52.3 89.6 %copy-start.14 = (bf16[128,1792]{1,0:T(8,128)(2,1)}, bf16[128,1792]{1,0:T(8,128)(2,1)S(1)}, u32[]{:S(2)}) copy-start(bf16[128,1792]{1,0:T(8,128)(2,1)S(1)} %gather_fusion) | copy-start | bytes 1376260
  77.6 100.7 %copy-start.106 = (bf16[128,256]{0,1:T(8,128)(2,1)}, bf16[128,256]{0,1:T(8,128)(2,1)S(1)}, u32[]{:S(2)}) copy-start(bf16[128,256]{0,1:T(8,128)(2,1)S(1)} %copy.163) | copy-start | bytes 196612
  78.6 86.0 %copy-start.10 = (bf16[128,1792]{1,0:T(8,128)(2,1)}, bf16[128,1792]{1,0:T(8,128)(2,1)S(1)}, u32[]{:S(2)}) copy-start(bf16[128,1792]{1,0:T(8,128)(2,1)S(1)} %gather_fusion.2) | copy-start | bytes 1376260
  85.5 96.8 %copy-start.89 = (f32[128,16,16]{0,2,1:T(8,128)}, f32[128,16,16]{0,2,1:T(8,128)S(1)}, u32[]{:S(2)}) copy-start(f32[128,16,16]{0,2,1:T(8,128)S(1)} %get-tuple-element.1059) | copy-start | bytes 393220
  85.5 96.8 %copy-start.91 = (f32[128,16,16]{0,2,1:T(8,128)}, f32[128,16,16]{0,2,1:T(8,128)S(1)}, u32[]{:S(2)}) copy-start(f32[128,16,16]{0,2,1:T(8,128)S(1)} %get-tuple-element.1058) | copy-start | bytes 393220
  96.8 130.7 %all-gather.31.cloned.1.call-start = ((), (), s32[]{:S(2)}) async-start(), calls=%async_computation.21 | async-start | bytes 3354624 | tf_op jit(solution)/shard_map/all_gather | solution.py:28
  108.4 146.0 %all-gather.21.cloned.1.call-start = ((), (), s32[]{:S(2)}) async-start(), calls=%async_computation.9 | async-start | bytes 6823936 | tf_op jit(solution)/shard_map/all_gather | solution.py:160
  109.0 213.2 %all-gather.23.cloned.1.call-start = ((), (), s32[]{:S(2)}) async-start(), calls=%async_computation.10 | async-start | bytes 18522112 | tf_op jit(solution)/shard_map/all_gather | solution.py:162
  109.6 306.3 %all-gather.25.cloned.1.call-start = ((), (), s32[]{:S(2)}) async-start(), calls=%async_computation.11 | async-start | bytes 18522112 | tf_op jit(solution)/shard_map/all_gather | solution.py:163
  110.2 399.5 %all-gather.27.cloned.1.call-start = ((), (), s32[]{:S(2)}) async-start(), calls=%async_computation.12 | async-start | bytes 18522112 | tf_op jit(solution)/shard_map/all_gather | solution.py:164
  110.9 638.6 %all-gather.35.cloned.1.call-start = ((), (), s32[]{:S(2)}) async-start(), calls=%async_computation.23 | async-start | bytes 3354624 | tf_op jit(solution)/shard_map/all_gather | solution.py:51
  187.6 14.4 collective-permute-start
  200.1 3.2 collective-permute-start.1
  263.0 152.9 %copy-start.34 = (bf16[128,1792]{1,0:T(8,128)(2,1)}, bf16[128,1792]{1,0:T(8,128)(2,1)S(1)}, u32[]{:S(2)}) copy-start(bf16[128,1792]{1,0:T(8,128)(2,1)S(1)} %get-tuple-element.1018) | copy-start | bytes 1376260
  697.4 71.6 %all-gather.33.cloned.1.call-start = ((), (), s32[]{:S(2)}) async-start(), calls=%async_computation.22 | async-start | bytes 3354624 | tf_op jit(solution)/shard_map/all_gather | solution.py:51
  727.8 206.4 %reduce-scatter.25.cloned.1.call-start = ((), (), s32[]{:S(2)}) async-start(), calls=%async_computation.24 | async-start | bytes 487424
  735.8 245.5 %reduce-scatter.11.cloned.1.call-start = ((), (), s32[]{:S(2)}) async-start(), calls=%async_computation.13 | async-start | bytes 974848 | tf_op jit(solution)/shard_map/reduce_scatter | solution.py:327
  749.5 231.8 %reduce-scatter.13.cloned.1.call-start = ((), (), s32[]{:S(2)}) async-start(), calls=%async_computation.14 | async-start | bytes 974848 | tf_op jit(solution)/shard_map/reduce_scatter | solution.py:330
  786.4 248.3 %reduce-scatter.17.cloned.1.call-start = ((), (), s32[]{:S(2)}) async-start(), calls=%async_computation.16 | async-start | bytes 6823936 | tf_op jit(solution)/shard_map/reduce_scatter | solution.py:339
  794.4 329.3 %reduce-scatter.15.cloned.1.call-start = ((), (), s32[]{:S(2)}) async-start(), calls=%async_computation.15 | async-start | bytes 6823936 | tf_op jit(solution)/shard_map/reduce_scatter | solution.py:333
  797.0 16.3 collective-permute-start.3
  798.3 18.3 collective-permute-start.2
  824.6 486.5 %reduce-scatter.19.cloned.1.call-start = ((), (), s32[]{:S(2)}) async-start(), calls=%async_computation.17 | async-start | bytes 18522112 | tf_op jit(solution)/shard_map/reduce_scatter | solution.py:345
  859.5 639.2 %reduce-scatter.21.cloned.1.call-start = ((), (), s32[]{:S(2)}) async-start(), calls=%async_computation.18 | async-start | bytes 18522112 | tf_op jit(solution)/shard_map/reduce_scatter | solution.py:348
  894.4 791.9 %reduce-scatter.23.cloned.1.call-start = ((), (), s32[]{:S(2)}) async-start(), calls=%async_computation.19 | async-start | bytes 18522112 | tf_op jit(solution)/shard_map/reduce_scatter | solution.py:351
  930.2 779.9 %all-reduce.29.cloned.1.call-start = ((), (), s32[]{:S(2)}) async-start(), calls=%async_computation.25 | async-start | bytes 233472 | tf_op jit(solution)/shard_map/psum | solution.py:356
  946.7 741.0 %copy-start.93 = (bf16[1,128,1792]{2,1,0:T(8,128)(2,1)S(1)}, bf16[1,128,1792]{2,1,0:T(8,128)(2,1)}, u32[]{:S(2)}) copy-start(bf16[1,128,1792]{2,1,0:T(8,128)(2,1)} %get-tuple-element.998) | copy-start | bytes 1376260
  946.7 741.0 %copy-start.94 = (bf16[1,128,1792]{2,1,0:T(8,128)(2,1)S(1)}, bf16[1,128,1792]{2,1,0:T(8,128)(2,1)}, u32[]{:S(2)}) copy-start(bf16[1,128,1792]{2,1,0:T(8,128)(2,1)} %get-tuple-element.999) | copy-start | bytes 1376260
  981.3 838.6 %all-reduce.31.cloned.1.call-start = ((), (), s32[]{:S(2)}) async-start(), calls=%async_computation.26 | async-start | bytes 8142848 | tf_op jit(solution)/shard_map/psum | solution.py:359
  (223 other events, 1135.8 us)
Sparse Core Ops, SparseCore 0:
  10.3 73.5 all-gather.18
  96.9 32.1 all-gather.28
  130.7 34.6 all-gather.30
  167.5 62.4 all-gather.20
  231.5 90.7 all-gather.22
  323.7 92.1 all-gather.24
  417.5 92.1 all-gather.26
  697.5 34.7 all-gather.34
  733.9 35.0 all-gather.32
  772.3 53.4 reduce-scatter.24
  829.3 56.1 reduce-scatter.10
  889.4 55.9 reduce-scatter.12
  949.3 85.2 reduce-scatter.16
  1038.5 85.2 reduce-scatter.14
  1127.7 183.3 reduce-scatter.18
  1315.2 183.4 reduce-scatter.20
  1502.7 183.5 reduce-scatter.22
  1689.2 20.9 all-reduce.28
  1713.0 106.8 all-reduce.30
where the time goes:
time: 1850 us; the launch traced here: 1840 us
  waiting for transfers between devices  1060 us (57%)
  matrix products  362 us (20%)
  blocking collectives  198 us (11%)
  other arithmetic  90.2 us (5%)
  local copies, waits for them, and re-layouts  88.9 us (5%)
  between operations  25.8 us (1%)
    reduce_scatter x1, waiting for transfers between devices, on_device(): lax.psum_scatter(grad_sums[9].astype(jnp.bfloat16), 'fsdp', scatter_dimen...  188 us
    reduce_scatter x1, waiting for transfers between devices, on_device(): lax.psum_scatter(grad_sums[8].astype(jnp.bfloat16), 'fsdp', scatter_dimen...  188 us
    reduce_scatter x1, waiting for transfers between devices, on_device(): lax.psum_scatter(grad_sums[7].astype(jnp.bfloat16), 'fsdp', scatter_dimen...  187 us
    dot_general x14, matrix products, weight_grad(): lax.dot_general(left, right, (((0,), (0,)), ((), ())), preferred_element_...  120 us
    psum x1, waiting for transfers between devices, on_device(): lax.psum(summed[3].astype(jnp.bfloat16), 'seq').astype(jnp.float32)  103 us
    dot_general x14, matrix products, back_project(): lax.dot_general(grads, weight, (((1,), (1,)), ((), ())), preferred_elemen...  101 us
    reduce_scatter x1, waiting for transfers between devices, on_device(): lax.psum_scatter(grad_sums[3].astype(jnp.bfloat16), 'fsdp', scatter_dimen...  89.1 us
    all_gather x1, waiting for transfers between devices, gather_weights(): lax.all_gather(shards[8], 'fsdp', axis=0, tiled=True)  83.7 us
  transfers between devices with their start and end apart: 23, of which 12 were waited for; matrix products, arithmetic and copies ran while one was open for 19% of the time, Pallas kernels for 0%

commit v1 on v0

v1 whole, which is shorter than its diff:
```python
from functools import partial

import jax
import jax.numpy as jnp
from jax import lax
from jax.experimental import pallas as pl
from jax.experimental.pallas import tpu as pltpu
from jax.sharding import PartitionSpec as P

HEADS = 16
FEAT = 16
HEAD_SIZE = 112
Z_CHIPS = 4
CORES = 2
SMALL = 128
EPSILON = 1e-05
BF16 = jnp.bfloat16
F32 = jnp.float32


def dot(left, right, dims=((1,), (0,))):
    return lax.dot_general(left, right, (dims, ((), ())), preferred_element_type=F32)


def take(array, index, axis):
    return lax.dynamic_index_in_dim(array, index, axis, keepdims=False)


class Place:
    def __init__(self):
        self.seqs = lax.axis_size("seq")
        self.fsdp = lax.axis_size("fsdp")
        self.xs = self.fsdp // (Z_CHIPS * CORES)
        self.y = lax.axis_index("seq")
        self.p = lax.axis_index("fsdp")
        self.c = self.p % CORES
        self.x = (self.p // CORES) % self.xs
        self.z = self.p // (CORES * self.xs)
        self.z_low_size = Z_CHIPS // self.seqs
        self.z_high = self.z // self.z_low_size

    def index(self, z, x, c):
        return (z * self.xs + x) * CORES + c

    def everyone(self):
        for z in range(Z_CHIPS):
            for x in range(self.xs):
                for c in range(CORES):
                    yield z, x, c


def seq_pieces(place, value):
    got = [value]
    for k in range(1, place.seqs):
        pairs = [(i, (i + k) % place.seqs) for i in range(place.seqs)]
        got.append(lax.ppermute(value, "seq", pairs))
    if place.seqs == 2:
        first = place.y == 0
        return [jnp.where(first, got[0], got[1]), jnp.where(first, got[1], got[0])]
    stacked = jnp.stack(got)
    return [take(stacked, (place.y - j) % place.seqs, 0) for j in range(place.seqs)]


def seq_scatter(place, value, axis):
    total = take(value, place.y, axis).astype(F32)
    for k in range(1, place.seqs):
        pairs = [(i, (i + k) % place.seqs) for i in range(place.seqs)]
        sent = take(value, (place.y + k) % place.seqs, axis).astype(BF16)
        total = total + lax.ppermute(sent, "seq", pairs).astype(F32)
    return total


def add_low(*parts):
    total = parts[0].astype(F32)
    for part in parts[1:]:
        total = total + part.astype(F32)
    return total.astype(BF16)


def line_scatter(value, axis, count, index, pairs_of):
    if count == 2:
        got = lax.ppermute(take(value, 1 - index, axis), "fsdp", pairs_of([(0, 1), (1, 0)]))
        return add_low(take(value, index, axis), got)
    up = down = None
    for far in range(count - 1, 0, -1):
        send_up = take(value, (index + far) % count, axis)
        send_down = take(value, (index - far) % count, axis)
        if up is not None:
            send_up = add_low(send_up, up)
            send_down = add_low(send_down, down)
        up = lax.ppermute(
            send_up, "fsdp", pairs_of([(i, i + 1) for i in range(count - far)])
        )
        down = lax.ppermute(
            send_down, "fsdp", pairs_of([(i, i - 1) for i in range(far, count)])
        )
    return add_low(take(value, index, axis), up, down)


def grad_scatter(place, grad):
    def core_pairs(moves):
        return [
            (place.index(z, x, a), place.index(z, x, b))
            for a, b in moves
            for z in range(Z_CHIPS)
            for x in range(place.xs)
        ]

    def x_pairs(moves):
        return [
            (place.index(z, a, c), place.index(z, b, c))
            for a, b in moves
            for z in range(Z_CHIPS)
            for c in range(CORES)
        ]

    def z_pairs(moves):
        return [
            (place.index(a, x, c), place.index(b, x, c))
            for a, b in moves
            for x in range(place.xs)
            for c in range(CORES)
        ]

    one_core = line_scatter(grad, 2, CORES, place.c, core_pairs)
    one_x = line_scatter(one_core, 1, place.xs, place.x, x_pairs)
    return line_scatter(one_x, 0, Z_CHIPS, place.z, z_pairs)


def plane_pairs(place, k):
    pairs = []
    for y in range(place.seqs):
        for z, x, c in place.everyone():
            high, low = divmod(z, place.z_low_size)
            if high == y:
                other = ((y + k) % place.seqs) * place.z_low_size + low
                pairs.append(
                    (
                        y * place.fsdp + place.index(z, x, c),
                        y * place.fsdp + place.index(other, x, c),
                    )
                )
    return pairs


def spread_rows(place, shard):
    rows = shard.shape[0] // place.seqs
    pieces = shard.reshape(place.seqs, rows, shard.shape[1])
    part = take(pieces, place.y, 0)
    owner = place.z_high == place.y
    for k in range(1, place.seqs):
        sent = take(pieces, (place.y + k) % place.seqs, 0)
        got = lax.ppermute(sent, ("seq", "fsdp"), plane_pairs(place, k))
        part = jnp.where((place.z_high - place.y) % place.seqs == k, got, part)
    return part


def plane_rows(place, gathered):
    rows, columns = gathered.shape
    blocks = gathered.reshape(place.seqs, place.fsdp // place.seqs, -1, columns)
    return jnp.swapaxes(blocks, 0, 1).reshape(rows, columns)


def plane_grad_view(place, grad):
    rows, columns = grad.shape
    view = grad.reshape(place.z_low_size, place.xs, CORES, place.seqs, -1, columns)
    view = jnp.transpose(view, (3, 0, 1, 2, 4, 5))
    return view.reshape(Z_CHIPS, place.xs, CORES, -1, columns)


def unspread_rows(place, part):
    seqs = place.seqs
    rows, columns = part.shape
    shard = jnp.zeros((seqs, rows, columns), part.dtype)
    shard = lax.dynamic_update_index_in_dim(shard, part, place.y, 0)
    for k in range(1, seqs):
        pairs = [(b, a) for a, b in plane_pairs(place, k)]
        got = lax.ppermute(part, ("seq", "fsdp"), pairs)
        shard = lax.dynamic_update_index_in_dim(shard, got, (place.y + k) % seqs, 0)
    shard = shard.reshape(seqs * rows, columns)
    whole = shard
    for k in range(1, seqs):
        pairs = []
        for y in range(seqs):
            for z, x, c in place.everyone():
                if z // place.z_low_size == y:
                    pairs.append(
                        (
                            y * place.fsdp + place.index(z, x, c),
                            ((y + k) % seqs) * place.fsdp + place.index(z, x, c),
                        )
                    )
        got = lax.ppermute(shard, ("seq", "fsdp"), pairs)
        whole = jnp.where((place.y - place.z_high) % seqs == k, got, whole)
    return whole.astype(F32)


def sum_everywhere(place, value):
    for axis, count in (("fsdp", place.fsdp), ("seq", place.seqs)):
        bit = 1
        while bit < count:
            value = value + lax.ppermute(value, axis, [(i, i ^ bit) for i in range(count)])
            bit *= 2
    return value


def head_window(head):
    low = head * HEAD_SIZE // 128 * 128
    high = -(-(head + 1) * HEAD_SIZE // 128) * 128
    return low, high


def sigmoid(value):
    return 1.0 / (1.0 + jnp.exp(-value))


def conv_parts(values, taps_ref, seg_col):
    rows = values.shape[0]
    index = lax.broadcasted_iota(jnp.int32, (rows, 1), 0)
    near_one = (index >= 1) & (pltpu.roll(seg_col, 1, 0) == seg_col)
    near_two = (index >= 2) & (pltpu.roll(seg_col, 2, 0) == seg_col)
    prev_one = jnp.where(near_one, pltpu.roll(values, 1, 0), 0.0)
    prev_two = jnp.where(near_two, pltpu.roll(values, 2, 0), 0.0)
    conv = taps_ref[0:1] * values + taps_ref[1:2] * prev_one + taps_ref[2:3] * prev_two
    return conv, prev_one, prev_two, near_one, near_two


def masks(rows, seg_col, seg_row):
    at = lax.broadcasted_iota(jnp.int32, (rows, rows), 0)
    of = lax.broadcasted_iota(jnp.int32, (rows, rows), 1)
    return (seg_col == seg_row) & (at >= of)


def lanes_between(low, high, start, stop):
    lane = low + lax.broadcasted_iota(jnp.int32, (1, high - low), 1)
    return (lane >= start) & (lane < stop)


def mix_kernel(heads, qkv_ref, taps_ref, segc_ref, segr_ref, mixed_ref, att_ref):
    rows = qkv_ref.shape[0]
    qk_width = heads * FEAT
    width = heads * HEAD_SIZE
    seg_col = segc_ref[0]
    allowed = masks(rows, seg_col, segr_ref[0])
    queries = qkv_ref[:, 0:qk_width]
    keys = qkv_ref[:, qk_width : 2 * qk_width]
    for head in range(heads):
        mine = lanes_between(0, qk_width, head * FEAT, (head + 1) * FEAT)
        query = jnp.where(mine, queries, jnp.zeros_like(queries))
        scores = dot(query, keys, ((1,), (1,))) * 0.25
        kern = jnp.where(allowed, 1.0 + scores + 0.5 * scores * scores, 0.0)
        den = jnp.sum(kern, axis=1, keepdims=True)
        low, high = head_window(head)
        high = min(high, width)
        num = dot(kern.astype(BF16), qkv_ref[:, 2 * qk_width + low : 2 * qk_width + high])
        here = lanes_between(low, high, head * HEAD_SIZE, (head + 1) * HEAD_SIZE)
        att_ref[:, low:high] = jnp.where(here, num * (1.0 / den), att_ref[:, low:high])
    values = qkv_ref[:, 2 * qk_width : 2 * qk_width + width].astype(F32)
    conv = conv_parts(values, taps_ref, seg_col)[0]
    mixed_ref[...] = (att_ref[...] * conv * sigmoid(conv)).astype(BF16)


def mix_back_kernel(
    heads, qkv_ref, dmixed_ref, taps_ref, segc_ref, segr_ref, dqkv_ref, dtaps_ref,
    att_ref, silu_ref, dv_ref,
):
    rows = qkv_ref.shape[0]
    qk_width = heads * FEAT
    width = heads * HEAD_SIZE
    seg_col = segc_ref[0]
    allowed = masks(rows, seg_col, segr_ref[0])
    queries = qkv_ref[:, 0:qk_width]
    keys = qkv_ref[:, qk_width : 2 * qk_width]
    values = qkv_ref[:, 2 * qk_width : 2 * qk_width + width].astype(F32)
    conv, prev_one, prev_two, near_one, near_two = conv_parts(values, taps_ref, seg_col)
    sig = sigmoid(conv)
    silu_ref[...] = dmixed_ref[...] * conv * sig
    dv_ref[...] = jnp.zeros_like(dv_ref)
    dq = jnp.zeros((rows, qk_width), F32)
    dk = jnp.zeros((rows, qk_width), F32)
    for head in range(heads):
        mine = lanes_between(0, qk_width, head * FEAT, (head + 1) * FEAT)
        query = jnp.where(mine, queries, jnp.zeros_like(queries))
        scores = dot(query, keys, ((1,), (1,))) * 0.25
        kern = jnp.where(allowed, 1.0 + scores + 0.5 * scores * scores, 0.0)
        inv_den = 1.0 / jnp.sum(kern, axis=1, keepdims=True)
        kern_low = kern.astype(BF16)
        low, high = head_window(head)
        high = min(high, width)
        value = qkv_ref[:, 2 * qk_width + low : 2 * qk_width + high]
        att = dot(kern_low, value) * inv_den
        here = lanes_between(low, high, head * HEAD_SIZE, (head + 1) * HEAD_SIZE)
        att_ref[:, low:high] = jnp.where(here, att, att_ref[:, low:high])
        datt = jnp.where(here, silu_ref[:, low:high], 0.0) * inv_den
        row_dot = jnp.sum(datt * att, axis=1, keepdims=True)
        datt_low = datt.astype(BF16)
        dkern = dot(datt_low, value, ((1,), (1,))) - row_dot
        dscores = jnp.where(allowed, dkern * (0.25 + 0.25 * scores), 0.0).astype(BF16)
        dq = dq + jnp.where(mine, dot(dscores, keys), 0.0)
        dk = dk + dot(dscores, query, ((0,), (0,)))
        dv_ref[:, low:high] += dot(kern_low, datt_low, ((0,), (0,)))
    dconv = dmixed_ref[...] * att_ref[...] * sig * (1.0 + conv * (1.0 - sig))
    dtaps_ref[0, 0:1] = jnp.sum(dconv * values, axis=0, keepdims=True)
    dtaps_ref[0, 1:2] = jnp.sum(dconv * prev_one, axis=0, keepdims=True)
    dtaps_ref[0, 2:3] = jnp.sum(dconv * prev_two, axis=0, keepdims=True)
    dtaps_ref[0, 3:8] = jnp.zeros((5, width), F32)
    back_one = pltpu.roll(jnp.where(near_one, dconv, 0.0), rows - 1, 0)
    back_two = pltpu.roll(jnp.where(near_two, dconv, 0.0), rows - 2, 0)
    dv = (
        dv_ref[...]
        + taps_ref[0:1] * dconv
        + taps_ref[1:2] * back_one
        + taps_ref[2:3] * back_two
    )
    dqkv_ref[:, 0:qk_width] = dq.astype(BF16)
    dqkv_ref[:, qk_width : 2 * qk_width] = dk.astype(BF16)
    dqkv_ref[:, 2 * qk_width :] = dv.astype(BF16)


def seg_specs(rows):
    return [
        pl.BlockSpec((1, rows, 1), lambda m: (m, 0, 0)),
        pl.BlockSpec((1, 1, rows), lambda m: (m, 0, 0)),
    ]


def mix_forward(heads, micro, qkv, taps, segments):
    rows = qkv.shape[0] // micro
    width = heads * HEAD_SIZE
    return pl.pallas_call(
        partial(mix_kernel, heads),
        grid=(micro,),
        out_shape=jax.ShapeDtypeStruct((micro * rows, width), BF16),
        in_specs=[
            pl.BlockSpec((rows, qkv.shape[1]), lambda m: (m, 0)),
            pl.BlockSpec(taps.shape, lambda m: (0, 0)),
            *seg_specs(rows),
        ],
        out_specs=pl.BlockSpec((rows, width), lambda m: (m, 0)),
        scratch_shapes=[pltpu.VMEM((rows, width), F32)],
        compiler_params=pltpu.CompilerParams(vmem_limit_bytes=48 * 2**20),
    )(qkv, taps, segments[:, :, None], segments[:, None, :])


def mix_backward(heads, micro, qkv, dmixed, taps, segments):
    rows = qkv.shape[0] // micro
    width = heads * HEAD_SIZE
    return pl.pallas_call(
        partial(mix_back_kernel, heads),
        grid=(micro,),
        out_shape=(
            jax.ShapeDtypeStruct(qkv.shape, BF16),
            jax.ShapeDtypeStruct((micro, 8, width), F32),
        ),
        in_specs=[
            pl.BlockSpec((rows, qkv.shape[1]), lambda m: (m, 0)),
            pl.BlockSpec((rows, width), lambda m: (m, 0)),
            pl.BlockSpec(taps.shape, lambda m: (0, 0)),
            *seg_specs(rows),
        ],
        out_specs=(
            pl.BlockSpec((rows, qkv.shape[1]), lambda m: (m, 0)),
            pl.BlockSpec((1, 8, width), lambda m: (m, 0, 0)),
        ),
        scratch_shapes=[pltpu.VMEM((rows, width), F32)] * 3,
        compiler_params=pltpu.CompilerParams(vmem_limit_bytes=56 * 2**20),
    )(qkv, dmixed, taps, segments[:, :, None], segments[:, None, :])


def on_device(
    tokens,
    seq_order,
    seq_lengths,
    valid_count,
    teacher,
    norm_one,
    w_query,
    w_key,
    w_value,
    conv_taps,
    w_out,
    norm_two,
    w_gate,
    w_up,
    w_down,
):
    place = Place()
    seqs, y = place.seqs, place.y
    micro, rows_dev, model = tokens.shape[0], tokens.shape[2], tokens.shape[3]
    group = seqs * rows_dev
    rows = micro * group
    heads = HEADS // seqs
    qk_width = heads * FEAT
    width = heads * HEAD_SIZE
    slots = micro * place.fsdp * group

    def columns(weight):
        part = weight.shape[1] // seqs
        return lax.dynamic_slice_in_dim(weight, y * part, part, 1)

    shard_rows = w_query.shape[0]
    valid = valid_count[:, 0]
    coded = jnp.stack([valid // 16, valid % 16], axis=1).reshape(1, 2 * micro).astype(BF16)
    first_row = lax.broadcasted_iota(jnp.int32, (shard_rows, 2 * micro), 0) == 0
    small = jnp.concatenate(
        [
            norm_one[:, None],
            norm_two[:, None],
            conv_taps.T,
            jnp.where(first_row, coded, jnp.zeros_like(coded)),
        ],
        axis=1,
    )
    small = jnp.pad(small, ((0, 0), (0, SMALL - small.shape[1])))
    first_shard = jnp.concatenate(
        [columns(w_query), columns(w_key), columns(w_value), small], axis=1
    )
    first = lax.all_gather(first_shard, "fsdp", axis=0, tiled=True)
    out_part = spread_rows(place, w_out)
    down_part = spread_rows(place, w_down)
    out_w = plane_rows(place, lax.all_gather(out_part, "fsdp", axis=0, tiled=True))
    gate_w = lax.all_gather(columns(w_gate), "fsdp", axis=0, tiled=True)
    up_w = lax.all_gather(columns(w_up), "fsdp", axis=0, tiled=True)
    down_w = plane_rows(place, lax.all_gather(down_part, "fsdp", axis=0, tiled=True))

    qkv_width = 2 * qk_width + width
    qkv_w = first[:, :qkv_width]
    small_all = first[:, qkv_width : qkv_width + 16].astype(F32).T
    gain_one, gain_two = small_all[0], small_all[1]
    taps = lax.dynamic_slice_in_dim(small_all[2:5], y * width, width, 1)
    taps = jnp.pad(taps, ((0, 5), (0, 0)))
    coded_sum = jnp.sum(small_all[5 : 5 + 2 * micro], axis=1)
    total = 16.0 * jnp.sum(coded_sum[0::2]) + jnp.sum(coded_sum[1::2])
    scale = slots / total

    order = seq_order[:, 0, 0]
    order_all = jnp.stack(seq_pieces(place, order), axis=1)
    tokens_all = jnp.stack(seq_pieces(place, tokens[:, 0]), axis=1)
    local = jnp.arange(rows_dev, dtype=jnp.int32)
    pick_all = (order_all[..., None] == local).astype(BF16)
    packed = jnp.einsum("msij,msjd->msid", pick_all, tokens_all, preferred_element_type=BF16)
    packed = packed.reshape(rows, model)
    pick = (order[..., None] == local).astype(BF16)
    wanted = jnp.einsum("mij,mjd->mid", pick, teacher[:, 0], preferred_element_type=BF16)
    keep = (order + y * rows_dev < valid[:, None]).astype(F32)
    ends = jnp.cumsum(seq_lengths[:, 0], axis=1)
    positions = jnp.arange(group, dtype=jnp.int32)
    segments = jnp.sum((positions[None, :, None] >= ends[:, None, :]).astype(jnp.int32), axis=2)

    packed_f = packed.astype(F32)
    root_one = lax.rsqrt(jnp.mean(packed_f * packed_f, axis=1, keepdims=True) + EPSILON)
    n_one = (packed_f * root_one * gain_one).astype(BF16)
    qkv = dot(n_one, qkv_w).astype(BF16)
    mixed = mix_forward(heads, micro, qkv, taps, segments)

    def scatter(partial_rows):
        return seq_scatter(place, partial_rows.reshape(micro, seqs, rows_dev, model), 1)

    def gather(own_rows):
        return jnp.stack(seq_pieces(place, own_rows), axis=1).reshape(rows, model)

    packed_own = take(packed.reshape(micro, seqs, rows_dev, model), y, 1).astype(F32)
    resid = packed_own + scatter(dot(mixed, out_w))
    root_two = lax.rsqrt(jnp.mean(resid * resid, axis=2, keepdims=True) + EPSILON)
    n_two = gather((resid * root_two * gain_two).astype(BF16))
    gate = dot(n_two, gate_w)
    up = dot(n_two, up_w)
    sig = jax.nn.sigmoid(gate)
    hidden = (gate * sig * up).astype(BF16)
    result = resid + scatter(dot(hidden, down_w))
    output = jnp.einsum("mij,mid->mjd", pick, result.astype(BF16), preferred_element_type=BF16)
    error = (result - wanted.astype(F32)) * keep[..., None]
    squares = jnp.sum(error * error)
    loss = sum_everywhere(place, squares) / (total * model)

    d_result = scale * error
    d_low = gather(d_result.astype(BF16))
    grad_down = dot(hidden, d_low, ((0,), (0,))).astype(BF16)
    grad_down = grad_scatter(place, plane_grad_view(place, grad_down))
    d_hidden = dot(d_low, down_w, ((1,), (1,)))
    d_gate = (d_hidden * up * sig * (1.0 + gate * (1.0 - sig))).astype(BF16)
    d_up = (d_hidden * gate * sig).astype(BF16)

    def column_scatter(grad):
        view = grad.astype(BF16).reshape(Z_CHIPS, place.xs, CORES, shard_rows, grad.shape[1])
        return grad_scatter(place, view)

    grad_gate = column_scatter(dot(n_two, d_gate, ((0,), (0,))))
    grad_up = column_scatter(dot(n_two, d_up, ((0,), (0,))))
    d_n_two = scatter(dot(d_gate, gate_w, ((1,), (1,))) + dot(d_up, up_w, ((1,), (1,))))
    grad_norm_two = jnp.sum(d_n_two * resid * root_two, axis=(0, 1))
    d_scaled = d_n_two * gain_two
    d_resid = (
        d_result
        + root_two * d_scaled
        - resid * root_two**3 * jnp.mean(d_scaled * resid, axis=2, keepdims=True)
    )
    dm_low = gather(d_resid.astype(BF16))
    grad_out = dot(mixed, dm_low, ((0,), (0,))).astype(BF16)
    grad_out = grad_scatter(place, plane_grad_view(place, grad_out))
    d_mixed = dot(dm_low, out_w, ((1,), (1,)))
    d_qkv, d_taps = mix_backward(heads, micro, qkv, d_mixed, taps, segments)
    d_taps = jnp.sum(d_taps, axis=0)[:3]
    d_n_one_part = dot(d_qkv, qkv_w, ((1,), (1,)))
    grad_norm_one = jnp.sum(d_n_one_part * packed_f * root_one, axis=0)
    d_taps_wide = lax.dynamic_update_slice_in_dim(
        jnp.zeros((3, model), F32), d_taps, y * width, 1
    )
    extra = jnp.concatenate(
        [grad_norm_one[None], grad_norm_two[None], d_taps_wide, jnp.zeros((11, model), F32)]
    ).T
    extra = jnp.pad(extra.astype(BF16), ((0, 0), (0, SMALL - extra.shape[1])))
    grad_first = jnp.concatenate(
        [dot(n_one, d_qkv, ((0,), (0,))).astype(BF16), extra], axis=1
    )
    grad_first = column_scatter(grad_first)
    d_n_one = scatter(d_n_one_part)
    root_own = take(root_one.reshape(micro, seqs, rows_dev, 1), y, 1)
    d_scaled = d_n_one * gain_one
    d_packed = (
        d_resid
        + root_own * d_scaled
        - packed_own * root_own**3 * jnp.mean(d_scaled * packed_own, axis=2, keepdims=True)
    )
    input_grad = jnp.einsum(
        "mij,mid->mjd", pick, d_packed.astype(BF16), preferred_element_type=BF16
    )

    def join(parts):
        return jnp.concatenate(parts, axis=1).astype(F32)

    first_parts = seq_pieces(place, grad_first)
    extra_sum = sum(part[:, qkv_width:].astype(F32) for part in first_parts)
    return (
        output[:, None],
        input_grad[:, None],
        extra_sum[:, 0],
        join([part[:, :qk_width] for part in first_parts]),
        join([part[:, qk_width : 2 * qk_width] for part in first_parts]),
        join([part[:, 2 * qk_width : qkv_width] for part in first_parts]),
        extra_sum[:, 2:5].T,
        unspread_rows(place, grad_out),
        extra_sum[:, 1],
        join(seq_pieces(place, grad_gate)),
        join(seq_pieces(place, grad_up)),
        unspread_rows(place, grad_down),
        loss,
    )


def solution(mesh):
    rows = P(None, "fsdp", "seq", None)
    placed = (
        rows,
        rows,
        P(None, "fsdp", None),
        P(None, "fsdp"),
        rows,
        P("fsdp"),
        P("fsdp", None),
        P("fsdp", None),
        P("fsdp", None),
        P(None, "fsdp"),
        P("fsdp", None),
        P("fsdp"),
        P("fsdp", None),
        P("fsdp", None),
        P("fsdp", None),
    )
    return jax.shard_map(
        on_device,
        mesh=mesh,
        in_specs=placed,
        out_specs=(
            rows,
            rows,
            P("fsdp"),
            P("fsdp", None),
            P("fsdp", None),
            P("fsdp", None),
            P(None, "fsdp"),
            P("fsdp", None),
            P("fsdp"),
            P("fsdp", None),
            P("fsdp", None),
            P("fsdp", None),
            P(),
        ),
        check_vma=False,
    )
```

time: 1850 us -> 985 us (0.53)
  waiting for transfers between devices: 1060 us -> 534 us
  matrix products: 362 us -> 127 us
  blocking collectives: 198 us -> 0 us
  starting transfers between devices: 9.33 us -> 141 us
  other arithmetic: 90.2 us -> 58.6 us
    reduce_scatter x7 -> x0, waiting for transfers between devices: 705 us -> none  [the longest x1 188 us: on_device(): lax.psum_scatter(grad_sums[9].astype(jnp.bfloat16), 'fsdp', scatter_dimen...]
    ppermute x4 -> x63, waiting for transfers between devices: 0.28 us -> 335 us  [the longest x10 80.6 us: line_scatter(): lax.ppermute(take(value, 1 - index, axis), 'fsdp', pairs_of([(0, 1), (1,...]
    dot_general x70 -> x19, matrix products: 362 us -> 127 us  [the longest x15 115 us: dot(): lax.dot_general(left, right, (dims, ((), ())), preferred_element_type=F32)]
    ppermute x4 -> x63, starting transfers between devices: 8.1 us -> 141 us  [the longest x15 54.8 us: line_scatter(): lax.ppermute(send_up, 'fsdp', pairs_of([(i, i + 1) for i in range(count -...]
    psum x2 -> x0, waiting for transfers between devices: 119 us -> none  [the longest x1 103 us: on_device(): lax.psum(summed[3].astype(jnp.bfloat16), 'seq').astype(jnp.float32)]
    all_gather x7 -> x0, blocking collectives: 82.6 us -> none  [the longest x1 24.6 us: gather_weights(): lax.all_gather(shards[2], 'fsdp', axis=0, tiled=True)]
    unnamed x3 -> x0, blocking collectives: 75.6 us -> none
    psum x1 -> x0, blocking collectives: 40.3 us -> none  [on_device(): total = lax.psum(jnp.sum(in_loss), ('seq', 'fsdp'))]
  transfers between devices with their start and end apart: 23 -> 68, of which waited for: 12 -> 39; matrix products, arithmetic and copies ran while one was open for 19% -> 19% of each run, Pallas kernels for 0% -> 2%
where the time goes in v1:
time: 985 us; the launch traced here: 978 us
  waiting for transfers between devices  534 us (54%)
  starting transfers between devices  141 us (14%)
  matrix products  127 us (13%)
  local copies, waits for them, and re-layouts  80.6 us (8%)
  other arithmetic  58.6 us (6%)
  between operations  21.6 us (2%)
  Pallas kernels  15.4 us (2%)
    dot_general x15, matrix products, dot(): lax.dot_general(left, right, (dims, ((), ())), preferred_element_type=F32)  115 us
    ppermute x10, waiting for transfers between devices, line_scatter(): lax.ppermute(take(value, 1 - index, axis), 'fsdp', pairs_of([(0, 1), (1,...  80.6 us
    ppermute x8, waiting for transfers between devices, seq_pieces(): got.append(lax.ppermute(value, 'seq', pairs))  69.1 us
    all_gather x1, waiting for transfers between devices, on_device(): up_w = lax.all_gather(columns(w_up), 'fsdp', axis=0, tiled=True)  66.7 us
    all_gather x1, waiting for transfers between devices, on_device(): lax.all_gather(down_part, 'fsdp', axis=0, tiled=True)  64.5 us
    ppermute x15, starting transfers between devices, line_scatter(): lax.ppermute(send_up, 'fsdp', pairs_of([(i, i + 1) for i in range(count -...  54.8 us
    all_gather x1, waiting for transfers between devices, on_device(): first = lax.all_gather(first_shard, 'fsdp', axis=0, tiled=True)  49.4 us
    ppermute x4, waiting for transfers between devices, seq_scatter(): total = total + lax.ppermute(sent, 'seq', pairs).astype(F32)  41.1 us
  transfers between devices with their start and end apart: 68, of which 39 were waited for; matrix products, arithmetic and copies ran while one was open for 19% of the time, Pallas kernels for 2%

profile of v1, /device:TPU:0, one launch (start us, length us, event | category | flops | bytes accessed | tf_op | source)
XLA Modules:
  0.0 977.7 jit_solution(16743874121621828568)
XLA Ops:
  32.2 17.1 %collective-permute-done.5 = bf16[152,1792]{1,0:T(8,128)(2,1)S(1)} collective-permute-done((bf16[152,1792]{1,0:T(8,128)(2,1)S(1)}, bf16[152,1792]{1,0:T(8,128)(2,1)S(1)}, u32[]{:S(2)}, u32[]{:S(2)}) %collective-permute-start.5) | collective-permute-done | bytes 544800 | tf_op jit(solution)/shard_map/ppermute | solution.py:153
  50.2 15.2 %collective-permute-start.1 = (bf16[2,128,1792]{2,1,0:T(8,128)(2,1)S(1)}, bf16[2,128,1792]{2,1,0:T(8,128)(2,1)S(1)}, u32[]{:S(2)}, u32[]{:S(2)}) collective-permute-start(bf16[2,128,1792]{2,1,0:T(8,128)(2,1)S(1)} %bitcast.414), channel_id=1, source_target_pairs={{0,16},{16,0},{1,17},{17,1},{2,18},{18,2},{3,19},{19,3},{4,20},{20... | collective-permute-start | bytes 2752520 | tf_op jit(solution)/shard_map/ppermute | solution.py:56
  65.9 20.0 %collective-permute-done = s32[2,128]{1,0:T(2,128)S(1)} collective-permute-done((s32[2,128]{1,0:T(2,128)S(1)}, s32[2,128]{1,0:T(2,128)S(1)}, u32[]{:S(2)}, u32[]{:S(2)}) %collective-permute-start) | collective-permute-done | bytes 1056 | tf_op jit(solution)/shard_map/ppermute | solution.py:56
  91.4 49.4 %all-gather.6.cloned.1.call-done = bf16[1792,1280]{1,0:T(8,128)(2,1)} async-done(((bf16[112,1280]{1,0:T(8,128)(2,1)}), bf16[1792,1280]{1,0:T(8,128)(2,1)}) %all-gather.6.cloned.1.call-update) | async-done | bytes 4587536 | tf_op jit(solution)/shard_map/all_gather | solution.py:418
  155.3 21.0 %collective-permute-done.3 = bf16[2,128,1792]{2,1,0:T(8,128)(2,1)S(1)} collective-permute-done((bf16[2,128,1792]{2,1,0:T(8,128)(2,1)S(1)}, bf16[2,128,1792]{2,1,0:T(8,128)(2,1)S(1)}, u32[]{:S(2)}, u32[]{:S(2)}) %collective-permute-start.3) | collective-permute-done | bytes 917536 | tf_op jit(solution)/shard_map/ppermute | solution.py:69
  178.7 20.2 %collective-permute-done.4 = bf16[2,128,1792]{2,1,0:T(8,128)(2,1)S(1)} collective-permute-done((bf16[2,128,1792]{2,1,0:T(8,128)(2,1)S(1)}, bf16[2,128,1792]{2,1,0:T(8,128)(2,1)S(1)}, u32[]{:S(2)}, u32[]{:S(2)}) %collective-permute-start.4) | collective-permute-done | bytes 917536 | tf_op jit(solution)/shard_map/ppermute | solution.py:56
  200.9 18.2 %all-gather.10.cloned.1.call-done = bf16[1792,2432]{1,0:T(8,128)(2,1)} async-done(((bf16[112,2432]{1,0:T(8,128)(2,1)}), bf16[1792,2432]{1,0:T(8,128)(2,1)}) %all-gather.10.cloned.1.call-update) | async-done | bytes 8716304 | tf_op jit(solution)/shard_map/all_gather | solution.py:422
  219.1 11.1 %fusion.97 = f32[512,2432]{1,0:T(8,128)} fusion(bf16[512,1792]{1,0:T(8,128)(2,1)} %bitcast.403, bf16[1792,2432]{1,0:T(8,128)(2,1)} %all-gather.10.cloned.1.call-done), kind=kOutput, calls=%fused_computation.260 | convolution fusion | flops 4462739456 | bytes 15532032 | tf_op jit(solution)/shard_map/dot_general | solution.py:22
  230.2 66.7 %all-gather.12.cloned.1.call-done = bf16[1792,2432]{1,0:T(8,128)(2,1)} async-done(((bf16[112,2432]{1,0:T(8,128)(2,1)}), bf16[1792,2432]{1,0:T(8,128)(2,1)}) %all-gather.12.cloned.1.call-update) | async-done | bytes 8716304 | tf_op jit(solution)/shard_map/all_gather | solution.py:423
  296.9 13.3 %multiply_convert_fusion.2 = (bf16[512,2432]{1,0:T(8,128)(2,1)}, f32[512,2432]{1,0:T(8,128)}) fusion(f32[512,2432]{1,0:T(8,128)} %fusion.97, bf16[512,1792]{1,0:T(8,128)(2,1)} %bitcast.404, bf16[1792,2432]{1,0:T(8,128)(2,1)} %all-gather.12.cloned.1.call-done), kind=kOutput, calls=%fused_computation.14 | convolution fusion | flops 4470210560 | bytes 23003136 | tf_op jit(solution)/shard_map/dot_general | solution.py:22
  310.2 64.5 %all-gather.14.cloned.1.call-done = bf16[2432,1792]{1,0:T(8,128)(2,1)} async-done(((bf16[152,1792]{1,0:T(8,128)(2,1)}), bf16[2432,1792]{1,0:T(8,128)(2,1)}) %all-gather.14.cloned.1.call-update) | async-done | bytes 8716304 | tf_op jit(solution)/shard_map/all_gather | solution.py:424
  374.7 7.5 copy.203
  382.2 9.4 fusion.98
  398.9 18.4 %collective-permute-done.6 = bf16[2,128,1792]{2,1,0:T(8,128)(2,1)} collective-permute-done((bf16[2,128,1792]{2,1,0:T(8,128)(2,1)}, bf16[2,128,1792]{2,1,0:T(8,128)(2,1)}, u32[]{:S(2)}, u32[]{:S(2)}) %collective-permute-start.6) | collective-permute-done | bytes 917536 | tf_op jit(solution)/shard_map/ppermute | solution.py:69
  426.4 17.2 %collective-permute-done.7 = bf16[2,128,1792]{2,1,0:T(8,128)(2,1)} collective-permute-done((bf16[2,128,1792]{2,1,0:T(8,128)(2,1)}, bf16[2,128,1792]{2,1,0:T(8,128)(2,1)}, u32[]{:S(2)}, u32[]{:S(2)}) %collective-permute-start.7) | collective-permute-done | bytes 917536 | tf_op jit(solution)/shard_map/ppermute | solution.py:56
  445.5 13.1 %multiply_convert_fusion = (bf16[512,2432]{1,0:T(8,128)(2,1)}, bf16[512,2432]{1,0:T(8,128)(2,1)}) fusion(f32[512,2432]{1,0:T(8,128)} %fusion.97, f32[512,2432]{1,0:T(8,128)} %get-tuple-element.176, bf16[512,1792]{1,0:T(8,128)(2,1)S(1)} %bitcast.407, bf16[2432,1792]{1,0:T(8,128)(2,1)} %bitcast.386), kind=kOutput, calls=%fused_computation.12 | convolution fusion | flops 4478926848 | bytes 25493504 | tf_op jit(solution)/shard_map/dot_general | solution.py:22
  458.7 9.6 convolution_convert_fusion.2
  468.3 10.3 %fusion.99 = f32[512,1792]{1,0:T(8,128)} fusion(bf16[512,2432]{1,0:T(8,128)(2,1)S(1)} %copy-done.41, bf16[1792,2432]{1,0:T(8,128)(2,1)} %all-gather.10.cloned.1.call-done), kind=kOutput, calls=%fused_computation.262 | convolution fusion | flops 4462739456 | bytes 14876672 | tf_op jit(solution)/shard_map/dot_general | solution.py:22
  478.6 7.7 convolution_add_fusion
  498.8 7.8 convolution_convert_fusion
  520.7 11.7 %collective-permute-done.9 = bf16[2,128,1792]{2,1,0:T(8,128)(2,1)S(1)} collective-permute-done((bf16[2,128,1792]{2,1,0:T(8,128)(2,1)S(1)}, bf16[2,128,1792]{2,1,0:T(8,128)(2,1)S(1)}, u32[]{:S(2)}, u32[]{:S(2)}) %collective-permute-start.9) | collective-permute-done | bytes 917536 | tf_op jit(solution)/shard_map/ppermute | solution.py:56
  539.7 12.1 %shard_map.250 = (bf16[512,1152]{1,0:T(8,128)(2,1)}, f32[2,8,896]{2,1,0:T(8,128)}) custom-call(bf16[512,1152]{1,0:T(8,128)(2,1)} %copy-done.2, f32[512,896]{1,0:T(8,128)} %fusion.100.dmixed_ref, f32[8,896]{1,0:T(8,128)} %copy-done.4, s32[2,256,1]{2,1,0:T(8,128)} %copy-done.3, s32[2,1,256]{2,1,0:T(1,128)} %copy-done.5), custom_call_target="tpu_custom_call" | custom-call | tf_op jit(solution)/shard_map/pallas_call | solution.py:348
  637.5 16.3 %collective-permute-done.21 = bf16[4,56,1792]{2,1,0:T(8,128)(2,1)S(1)} collective-permute-done((bf16[4,56,1792]{2,1,0:T(8,128)(2,1)S(1)}, bf16[4,56,1792]{2,1,0:T(8,128)(2,1)S(1)}, u32[]{:S(2)}, u32[]{:S(2)}) %collective-permute-start.21) | collective-permute-done | bytes 802848 | tf_op jit(solution)/shard_map/ppermute | solution.py:82
  713.0 7.7 collective-permute-done.28
  746.2 25.6 %collective-permute-done.40 = bf16[4,112,2432]{2,1,0:T(8,128)(2,1)} collective-permute-done((bf16[4,112,2432]{2,1,0:T(8,128)(2,1)}, bf16[4,112,2432]{2,1,0:T(8,128)(2,1)}, u32[]{:S(2)}, u32[]{:S(2)}) %collective-permute-start.40) | collective-permute-done | bytes 2179104 | tf_op jit(solution)/shard_map/ppermute | solution.py:82
  778.8 38.7 %collective-permute-done.49 = bf16[4,152,1792]{2,1,0:T(8,128)(2,1)S(1)} collective-permute-done((bf16[4,152,1792]{2,1,0:T(8,128)(2,1)S(1)}, bf16[4,152,1792]{2,1,0:T(8,128)(2,1)S(1)}, u32[]{:S(2)}, u32[]{:S(2)}) %collective-permute-start.49) | collective-permute-done | bytes 2179104 | tf_op jit(solution)/shard_map/ppermute | solution.py:82
  884.4 10.4 %collective-permute-done.37 = bf16[112,2432]{1,0:T(8,128)(2,1)S(1)} collective-permute-done((bf16[112,2432]{1,0:T(8,128)(2,1)S(1)}, bf16[112,2432]{1,0:T(8,128)(2,1)S(1)}, u32[]{:S(2)}, u32[]{:S(2)}) %collective-permute-start.37) | collective-permute-done | bytes 544800 | tf_op jit(solution)/shard_map/ppermute | solution.py:94
  896.4 8.1 collective-permute-done.52
  904.5 9.7 collective-permute-done.55
  916.1 9.6 collective-permute-start.47
  925.6 19.9 %collective-permute-done.56 = bf16[152,1792]{1,0:T(8,128)(2,1)S(1)} collective-permute-done((bf16[152,1792]{1,0:T(8,128)(2,1)S(1)}, bf16[152,1792]{1,0:T(8,128)(2,1)S(1)}, u32[]{:S(2)}, u32[]{:S(2)}) %collective-permute-start.56) | collective-permute-done | bytes 544800 | tf_op jit(solution)/shard_map/ppermute | solution.py:178
  950.2 18.2 %collective-permute-done.57 = bf16[304,1792]{1,0:T(8,128)(2,1)S(1)} collective-permute-done((bf16[304,1792]{1,0:T(8,128)(2,1)S(1)}, bf16[304,1792]{1,0:T(8,128)(2,1)S(1)}, u32[]{:S(2)}, u32[]{:S(2)}) %collective-permute-start.57) | collective-permute-done | bytes 1089568 | tf_op jit(solution)/shard_map/ppermute | solution.py:193
  (394 shorter events, 350.4 us)
Async XLA Ops:
  7.2 79.7 %all-gather.8.cloned.1.call-start = ((), (), s32[]{:S(2)}) async-start(), calls=%async_computation.1 | async-start | bytes 3411968 | tf_op jit(solution)/shard_map/all_gather | solution.py:421
  20.2 120.6 %all-gather.6.cloned.1.call-start = ((), (), s32[]{:S(2)}) async-start(), calls=%async_computation | async-start | bytes 4874240 | tf_op jit(solution)/shard_map/all_gather | solution.py:418
  24.7 194.4 %all-gather.10.cloned.1.call-start = ((), (), s32[]{:S(2)}) async-start(), calls=%async_computation.2 | async-start | bytes 9261056 | tf_op jit(solution)/shard_map/all_gather | solution.py:422
  25.6 271.3 %all-gather.12.cloned.1.call-start = ((), (), s32[]{:S(2)}) async-start(), calls=%async_computation.3 | async-start | bytes 9261056 | tf_op jit(solution)/shard_map/all_gather | solution.py:423
  26.5 348.1 %all-gather.14.cloned.1.call-start = ((), (), s32[]{:S(2)}) async-start(), calls=%async_computation.4 | async-start | bytes 9261056 | tf_op jit(solution)/shard_map/all_gather | solution.py:424
  50.2 35.8 %collective-permute-start.1 = (bf16[2,128,1792]{2,1,0:T(8,128)(2,1)S(1)}, bf16[2,128,1792]{2,1,0:T(8,128)(2,1)S(1)}, u32[]{:S(2)}, u32[]{:S(2)}) collective-permute-start(bf16[2,128,1792]{2,1,0:T(8,128)(2,1)S(1)} %bitcast.414), channel_id=1, source_target_pairs={{0,16},{16,0},{1,17},{17,1},{2,18},{18,2},{3,19},{19,3},{4,20},{20... | collective-permute-start | bytes 2752520 | tf_op jit(solution)/shard_map/ppermute | solution.py:56
  497.5 159.2 %collective-permute-start.30 = (bf16[4,2,112,2432]{3,2,0,1:T(8,128)(2,1)}, bf16[4,2,112,2432]{3,2,0,1:T(8,128)(2,1)}, u32[]{:S(2)}, u32[]{:S(2)}) collective-permute-start(bf16[4,2,112,2432]{3,2,0,1:T(8,128)(2,1)} %bitcast.367), channel_id=1, source_target_pairs={{0,1},{2,3},{4,5},{6,7},{8,9},{10,11},{12,13},{14,15},{1,0},{3,2},... | collective-permute-start | bytes 13074440 | tf_op jit(solution)/shard_map/ppermute | solution.py:82
  565.4 59.4 %collective-permute-start.10 = (bf16[2,128,1792]{2,1,0:T(8,128)(2,1)}, bf16[2,128,1792]{2,1,0:T(8,128)(2,1)S(1)}, u32[]{:S(2)}, u32[]{:S(2)}) collective-permute-start(bf16[2,128,1792]{2,1,0:T(8,128)(2,1)} %fusion.57), channel_id=1, source_target_pairs={{0,16},{16,0},{1,17},{17,1},{2,18},{18,2},{3,19},{19,3},{4,20},{20... | collective-permute-start | bytes 2752520 | tf_op jit(solution)/shard_map/ppermute | solution.py:69
  580.7 53.0 %collective-permute-start.11 = (bf16[4,2,112,1280]{3,2,1,0:T(8,128)(2,1)}, bf16[4,2,112,1280]{3,2,1,0:T(8,128)(2,1)}, u32[]{:S(2)}, u32[]{:S(2)}) collective-permute-start(bf16[4,2,112,1280]{3,2,1,0:T(8,128)(2,1)} %dynamic-slice_bitcast_fusion.1), channel_id=1, source_target_pairs={{0,1},{2,3},{4,5},{6,7},{8,9},{10,11},{12,13},{14,15},{1,0},{3,2},... | collective-permute-start | bytes 6881288 | tf_op jit(solution)/shard_map/ppermute | solution.py:82
  582.3 48.7 %collective-permute-start.20 = (bf16[4,2,56,1792]{3,2,1,0:T(8,128)(2,1)}, bf16[4,2,56,1792]{3,2,1,0:T(8,128)(2,1)}, u32[]{:S(2)}, u32[]{:S(2)}) collective-permute-start(bf16[4,2,56,1792]{3,2,1,0:T(8,128)(2,1)} %dynamic-slice_bitcast_fusion.5), channel_id=1, source_target_pairs={{0,1},{2,3},{4,5},{6,7},{8,9},{10,11},{12,13},{14,15},{1,0},{3,2},... | collective-permute-start | bytes 4816904 | tf_op jit(solution)/shard_map/ppermute | solution.py:82
  624.1 40.1 %collective-permute-start.39 = (bf16[4,2,112,2432]{3,2,0,1:T(8,128)(2,1)}, bf16[4,2,112,2432]{3,2,0,1:T(8,128)(2,1)}, u32[]{:S(2)}, u32[]{:S(2)}) collective-permute-start(bf16[4,2,112,2432]{3,2,0,1:T(8,128)(2,1)} %bitcast.397), channel_id=1, source_target_pairs={{0,1},{2,3},{4,5},{6,7},{8,9},{10,11},{12,13},{14,15},{1,0},{3,2},... | collective-permute-start | bytes 13074440 | tf_op jit(solution)/shard_map/ppermute | solution.py:82
  624.8 45.2 %collective-permute-start.48 = (bf16[4,2,152,1792]{3,2,1,0:T(8,128)(2,1)}, bf16[4,2,152,1792]{3,2,1,0:T(8,128)(2,1)}, u32[]{:S(2)}, u32[]{:S(2)}) collective-permute-start(bf16[4,2,152,1792]{3,2,1,0:T(8,128)(2,1)} %dynamic-slice_bitcast_fusion), channel_id=1, source_target_pairs={{0,1},{2,3},{4,5},{6,7},{8,9},{10,11},{12,13},{14,15},{1,0},{3,2},... | collective-permute-start | bytes 13074440 | tf_op jit(solution)/shard_map/ppermute | solution.py:82
  636.4 44.1 %collective-permute-start.12 = (bf16[4,112,1280]{2,1,0:T(8,128)(2,1)S(1)}, bf16[4,112,1280]{2,1,0:T(8,128)(2,1)}, u32[]{:S(2)}, u32[]{:S(2)}) collective-permute-start(bf16[4,112,1280]{2,1,0:T(8,128)(2,1)S(1)} %dynamic-slice_bitcast_fusion.6), channel_id=1, source_target_pairs={{0,2},{1,3},{4,6},{5,7},{8,10},{9,11},{12,14},{13,15},{2,0},{3,1},... | collective-permute-start | bytes 3440648 | tf_op jit(solution)/shard_map/ppermute | solution.py:82
  664.2 74.3 %collective-permute-start.31 = (bf16[4,112,2432]{2,1,0:T(8,128)(2,1)}, bf16[4,112,2432]{2,1,0:T(8,128)(2,1)}, u32[]{:S(2)}, u32[]{:S(2)}) collective-permute-start(bf16[4,112,2432]{2,1,0:T(8,128)(2,1)} %dynamic-slice_bitcast_fusion.4), channel_id=1, source_target_pairs={{0,2},{1,3},{4,6},{5,7},{8,10},{9,11},{12,14},{13,15},{2,0},{3,1},... | collective-permute-start | bytes 6537224 | tf_op jit(solution)/shard_map/ppermute | solution.py:82
  670.0 101.8 %collective-permute-start.40 = (bf16[4,112,2432]{2,1,0:T(8,128)(2,1)}, bf16[4,112,2432]{2,1,0:T(8,128)(2,1)}, u32[]{:S(2)}, u32[]{:S(2)}) collective-permute-start(bf16[4,112,2432]{2,1,0:T(8,128)(2,1)} %dynamic-slice_bitcast_fusion.3), channel_id=1, source_target_pairs={{0,2},{1,3},{4,6},{5,7},{8,10},{9,11},{12,14},{13,15},{2,0},{3,1},... | collective-permute-start | bytes 6537224 | tf_op jit(solution)/shard_map/ppermute | solution.py:82
  676.5 141.0 %collective-permute-start.49 = (bf16[4,152,1792]{2,1,0:T(8,128)(2,1)S(1)}, bf16[4,152,1792]{2,1,0:T(8,128)(2,1)S(1)}, u32[]{:S(2)}, u32[]{:S(2)}) collective-permute-start(bf16[4,152,1792]{2,1,0:T(8,128)(2,1)S(1)} %dynamic-slice_bitcast_fusion.2), channel_id=1, source_target_pairs={{0,2},{1,3},{4,6},{5,7},{8,10},{9,11},{12,14},{13,15},{2,0},{3,1},... | collective-permute-start | bytes 6537224 | tf_op jit(solution)/shard_map/ppermute | solution.py:82
  736.0 84.7 %collective-permute-start.19 = (bf16[112,1280]{1,0:T(8,128)(2,1)S(1)}, bf16[112,1280]{1,0:T(8,128)(2,1)S(1)}, u32[]{:S(2)}, u32[]{:S(2)}) collective-permute-start(bf16[112,1280]{1,0:T(8,128)(2,1)S(1)} %fusion.72), channel_id=1, source_target_pairs={{0,16},{16,0},{1,17},{17,1},{2,18},{18,2},{3,19},{19,3},{4,20},{20... | collective-permute-start | bytes 860168 | tf_op jit(solution)/shard_map/ppermute | solution.py:56
  742.1 86.0 %collective-permute-start.32 = (bf16[112,2432]{1,0:T(8,128)(2,1)}, bf16[112,2432]{1,0:T(8,128)(2,1)}, u32[]{:S(2)}, u32[]{:S(2)}) collective-permute-start(bf16[112,2432]{1,0:T(8,128)(2,1)} %get-tuple-element.138), channel_id=1, source_target_pairs={{0,4},{1,5},{2,6},{3,7},{16,20},{17,21},{18,22},{19,23}} | collective-permute-start | bytes 1634312 | tf_op jit(solution)/shard_map/ppermute | solution.py:91
  744.8 97.4 %collective-permute-start.35 = (bf16[112,2432]{1,0:T(8,128)(2,1)}, bf16[112,2432]{1,0:T(8,128)(2,1)}, u32[]{:S(2)}, u32[]{:S(2)}) collective-permute-start(bf16[112,2432]{1,0:T(8,128)(2,1)} %get-tuple-element.139), channel_id=1, source_target_pairs={{12,8},{13,9},{14,10},{15,11},{28,24},{29,25},{30,26},{31,27}} | collective-permute-start | bytes 1634312 | tf_op jit(solution)/shard_map/ppermute | solution.py:94
  775.2 55.0 %collective-permute-start.41 = (bf16[112,2432]{1,0:T(8,128)(2,1)}, bf16[112,2432]{1,0:T(8,128)(2,1)}, u32[]{:S(2)}, u32[]{:S(2)}) collective-permute-start(bf16[112,2432]{1,0:T(8,128)(2,1)} %get-tuple-element.134), channel_id=1, source_target_pairs={{0,4},{1,5},{2,6},{3,7},{16,20},{17,21},{18,22},{19,23}} | collective-permute-start | bytes 1634312 | tf_op jit(solution)/shard_map/ppermute | solution.py:91
  817.5 32.6 %collective-permute-start.44 = (bf16[112,2432]{1,0:T(8,128)(2,1)}, bf16[112,2432]{1,0:T(8,128)(2,1)}, u32[]{:S(2)}, u32[]{:S(2)}) collective-permute-start(bf16[112,2432]{1,0:T(8,128)(2,1)} %get-tuple-element.135), channel_id=1, source_target_pairs={{12,8},{13,9},{14,10},{15,11},{28,24},{29,25},{30,26},{31,27}} | collective-permute-start | bytes 1634312 | tf_op jit(solution)/shard_map/ppermute | solution.py:94
  828.0 33.8 %collective-permute-start.53 = (bf16[152,1792]{1,0:T(8,128)(2,1)}, bf16[152,1792]{1,0:T(8,128)(2,1)S(1)}, u32[]{:S(2)}, u32[]{:S(2)}) collective-permute-start(bf16[152,1792]{1,0:T(8,128)(2,1)} %get-tuple-element.131), channel_id=1, source_target_pairs={{12,8},{13,9},{14,10},{15,11},{28,24},{29,25},{30,26},{31,27}} | collective-permute-start | bytes 1634312 | tf_op jit(solution)/shard_map/ppermute | solution.py:94
  836.5 23.2 %collective-permute-start.42 = (bf16[112,2432]{1,0:T(8,128)(2,1)S(1)}, bf16[112,2432]{1,0:T(8,128)(2,1)S(1)}, u32[]{:S(2)}, u32[]{:S(2)}) collective-permute-start(bf16[112,2432]{1,0:T(8,128)(2,1)S(1)} %fusion.44), channel_id=1, source_target_pairs={{0,4},{1,5},{2,6},{3,7},{4,8},{5,9},{6,10},{7,11},{16,20},{17,21},... | collective-permute-start | bytes 1634312 | tf_op jit(solution)/shard_map/ppermute | solution.py:91
  842.1 29.3 %collective-permute-start.51 = (bf16[152,1792]{1,0:T(8,128)(2,1)S(1)}, bf16[152,1792]{1,0:T(8,128)(2,1)S(1)}, u32[]{:S(2)}, u32[]{:S(2)}) collective-permute-start(bf16[152,1792]{1,0:T(8,128)(2,1)S(1)} %fusion.38), channel_id=1, source_target_pairs={{0,4},{1,5},{2,6},{3,7},{4,8},{5,9},{6,10},{7,11},{16,20},{17,21},... | collective-permute-start | bytes 1634312 | tf_op jit(solution)/shard_map/ppermute | solution.py:91
  850.1 33.0 %collective-permute-start.34 = (bf16[112,2432]{1,0:T(8,128)(2,1)S(1)}, bf16[112,2432]{1,0:T(8,128)(2,1)S(1)}, u32[]{:S(2)}, u32[]{:S(2)}) collective-permute-start(bf16[112,2432]{1,0:T(8,128)(2,1)S(1)} %get-tuple-element.136), channel_id=1, source_target_pairs={{0,4},{1,5},{2,6},{3,7},{4,8},{5,9},{6,10},{7,11},{8,12},{9,13},{1... | collective-permute-start | bytes 1634312 | tf_op jit(solution)/shard_map/ppermute | solution.py:91
  861.8 54.0 %collective-permute-start.43 = (bf16[112,2432]{1,0:T(8,128)(2,1)S(1)}, bf16[112,2432]{1,0:T(8,128)(2,1)S(1)}, u32[]{:S(2)}, u32[]{:S(2)}) collective-permute-start(bf16[112,2432]{1,0:T(8,128)(2,1)S(1)} %get-tuple-element.132), channel_id=1, source_target_pairs={{0,4},{1,5},{2,6},{3,7},{4,8},{5,9},{6,10},{7,11},{8,12},{9,13},{1... | collective-permute-start | bytes 1634312 | tf_op jit(solution)/shard_map/ppermute | solution.py:91
  872.4 32.1 %collective-permute-start.52 = (bf16[152,1792]{1,0:T(8,128)(2,1)S(1)}, bf16[152,1792]{1,0:T(8,128)(2,1)S(1)}, u32[]{:S(2)}, u32[]{:S(2)}) collective-permute-start(bf16[152,1792]{1,0:T(8,128)(2,1)S(1)} %get-tuple-element.128), channel_id=1, source_target_pairs={{0,4},{1,5},{2,6},{3,7},{4,8},{5,9},{6,10},{7,11},{8,12},{9,13},{1... | collective-permute-start | bytes 1634312 | tf_op jit(solution)/shard_map/ppermute | solution.py:91
  879.5 36.3 %collective-permute-start.46 = (bf16[112,2432]{1,0:T(8,128)(2,1)S(1)}, bf16[112,2432]{1,0:T(8,128)(2,1)S(1)}, u32[]{:S(2)}, u32[]{:S(2)}) collective-permute-start(bf16[112,2432]{1,0:T(8,128)(2,1)S(1)} %fusion.43), channel_id=1, source_target_pairs={{4,0},{5,1},{6,2},{7,3},{8,4},{9,5},{10,6},{11,7},{12,8},{13,9},{1... | collective-permute-start | bytes 1634312 | tf_op jit(solution)/shard_map/ppermute | solution.py:94
  883.1 31.1 %collective-permute-start.55 = (bf16[152,1792]{1,0:T(8,128)(2,1)S(1)}, bf16[152,1792]{1,0:T(8,128)(2,1)S(1)}, u32[]{:S(2)}, u32[]{:S(2)}) collective-permute-start(bf16[152,1792]{1,0:T(8,128)(2,1)S(1)} %fusion.37), channel_id=1, source_target_pairs={{4,0},{5,1},{6,2},{7,3},{8,4},{9,5},{10,6},{11,7},{12,8},{13,9},{1... | collective-permute-start | bytes 1634312 | tf_op jit(solution)/shard_map/ppermute | solution.py:94
  895.0 52.0 %collective-permute-start.38 = (bf16[112,2432]{1,0:T(8,128)(2,1)S(1)}, bf16[112,2432]{1,0:T(8,128)(2,1)S(1)}, u32[]{:S(2)}, u32[]{:S(2)}) collective-permute-start(bf16[112,2432]{1,0:T(8,128)(2,1)S(1)} %fusion.53), channel_id=1, source_target_pairs={{0,16},{16,0},{1,17},{17,1},{2,18},{18,2},{3,19},{19,3},{4,20},{20... | collective-permute-start | bytes 1634312 | tf_op jit(solution)/shard_map/ppermute | solution.py:56
  914.5 31.0 %collective-permute-start.56 = (bf16[152,1792]{1,0:T(8,128)(2,1)S(1)}, bf16[152,1792]{1,0:T(8,128)(2,1)S(1)}, u32[]{:S(2)}, u32[]{:S(2)}) collective-permute-start(bf16[152,1792]{1,0:T(8,128)(2,1)S(1)} %get-tuple-element.115), channel_id=1, source_target_pairs={{8,0},{9,1},{10,2},{11,3},{12,4},{13,5},{14,6},{15,7},{16,24},{17,... | collective-permute-start | bytes 1634312 | tf_op jit(solution)/shard_map/ppermute | solution.py:178
  916.1 31.0 %collective-permute-start.47 = (bf16[112,2432]{1,0:T(8,128)(2,1)S(1)}, bf16[112,2432]{1,0:T(8,128)(2,1)S(1)}, u32[]{:S(2)}, u32[]{:S(2)}) collective-permute-start(bf16[112,2432]{1,0:T(8,128)(2,1)S(1)} %fusion.47), channel_id=1, source_target_pairs={{0,16},{16,0},{1,17},{17,1},{2,18},{18,2},{3,19},{19,3},{4,20},{20... | collective-permute-start | bytes 1634312 | tf_op jit(solution)/shard_map/ppermute | solution.py:56
  (92 other events, 1404.3 us)
Sparse Core Ops, SparseCore 0:
  20.4 66.1 all-gather.7
  89.4 51.3 all-gather.5
  143.6 75.4 all-gather.9
  221.7 75.1 all-gather.11
  299.5 75.1 all-gather.13

commit v2 on v1

v2 whole, which is shorter than its diff:
```python
from functools import partial

import jax
import jax.numpy as jnp
from jax import lax
from jax.experimental import pallas as pl
from jax.experimental.pallas import tpu as pltpu
from jax.sharding import PartitionSpec as P

HEADS = 16
FEAT = 16
HEAD_SIZE = 112
Z_CHIPS = 4
CORES = 2
SMALL = 128
GATHER_TILES = 528
EPSILON = 1e-05
BF16 = jnp.bfloat16
F32 = jnp.float32


def dot(left, right, dims=((1,), (0,))):
    return lax.dot_general(left, right, (dims, ((), ())), preferred_element_type=F32)


def take(array, index, axis):
    return lax.dynamic_index_in_dim(array, index, axis, keepdims=False)


def fence(*values):
    return lax.optimization_barrier(values)


class Place:
    def __init__(self):
        self.seqs = lax.axis_size("seq")
        self.fsdp = lax.axis_size("fsdp")
        self.xs = self.fsdp // (Z_CHIPS * CORES)
        self.y = lax.axis_index("seq")
        self.p = lax.axis_index("fsdp")
        self.c = self.p % CORES
        self.x = (self.p // CORES) % self.xs
        self.z = self.p // (CORES * self.xs)
        self.z_low_size = Z_CHIPS // self.seqs
        self.z_high = self.z // self.z_low_size
        self.turn = jnp.zeros((1, 128), F32)

    def in_turn(self, *values):
        *values, self.turn = fence(*values, self.turn)
        return values

    def index(self, z, x, c):
        return (z * self.xs + x) * CORES + c

    def everyone(self):
        for z in range(Z_CHIPS):
            for x in range(self.xs):
                for c in range(CORES):
                    yield z, x, c


def seq_send(place, value, k):
    pairs = [(i, (i + k) % place.seqs) for i in range(place.seqs)]
    return lax.ppermute(value, "seq", pairs)


def gather_seq(place, value):
    return [value] + [seq_send(place, value, k) for k in range(1, place.seqs)]


def in_order(place, pieces):
    if place.seqs == 2:
        first = place.y == 0
        return [
            jnp.where(first, pieces[0], pieces[1]),
            jnp.where(first, pieces[1], pieces[0]),
        ]
    stacked = jnp.stack(pieces)
    return [take(stacked, (place.y - j) % place.seqs, 0) for j in range(place.seqs)]


class Reduction:
    def __init__(self, place, grad, labels, order):
        self.place = place
        self.order = list(order)
        self.mine = {}
        self.parts = [(grad, tuple(labels))]

    def bit(self, label):
        return (self.place.p >> label) & 1

    def total(self, chosen):
        total = None
        for part, labels in self.parts:
            starts = [chosen[b] if b in chosen else 0 for b in labels] + [0, 0]
            sizes = [1 if b in chosen else 2 for b in labels] + list(part.shape[-2:])
            piece = lax.dynamic_slice(part, starts, sizes)
            left = [2 for b in labels if b not in chosen] + list(part.shape[-2:])
            piece = piece.reshape(left)
            total = piece if total is None else total.astype(F32) + piece.astype(F32)
        return total.astype(BF16)

    def left(self):
        return tuple(b for b in self.parts[0][1] if b not in self.mine)

    def pick(self, label):
        return self.total({**self.mine, label: 1 - self.bit(label)})

    def send(self, label, sent):
        pairs = [(i, i ^ (1 << label)) for i in range(self.place.fsdp)]
        got = lax.ppermute(sent, "fsdp", pairs)
        self.mine[label] = self.bit(label)
        self.parts.append((got, self.left()))

    def after(self, *values):
        got, labels = self.parts[-1]
        got, *values = self.place.in_turn(got, *values)
        self.parts[-1] = (got, labels)
        return values

    def start(self, *values):
        *done, label = self.order.pop(0)
        for bit in done:
            self.send(bit, self.pick(bit))
        sent, *values = self.place.in_turn(self.pick(label), *values)
        self.send(label, sent)
        return values

    def result(self):
        return self.total(self.mine)


def plane_pairs(place, k):
    pairs = []
    for y in range(place.seqs):
        for z, x, c in place.everyone():
            high, low = divmod(z, place.z_low_size)
            if high == y:
                other = ((y + k) % place.seqs) * place.z_low_size + low
                pairs.append(
                    (
                        y * place.fsdp + place.index(z, x, c),
                        y * place.fsdp + place.index(other, x, c),
                    )
                )
    return pairs


def spread_rows(place, shard):
    rows = shard.shape[0] // place.seqs
    pieces = shard.reshape(place.seqs, rows, shard.shape[1])
    part = take(pieces, place.y, 0)
    owner = place.z_high == place.y
    for k in range(1, place.seqs):
        sent = take(pieces, (place.y + k) % place.seqs, 0)
        got = lax.ppermute(sent, ("seq", "fsdp"), plane_pairs(place, k))
        part = jnp.where((place.z_high - place.y) % place.seqs == k, got, part)
    return part


def plane_rows(place, gathered):
    rows, columns = gathered.shape
    blocks = gathered.reshape(place.seqs, place.fsdp // place.seqs, -1, columns)
    return jnp.swapaxes(blocks, 0, 1).reshape(rows, columns)


def unspread_start(place, part):
    return gather_seq(place, part)


def unspread_end(place, planes):
    seqs = place.seqs
    part = planes[0]
    by_plane = jnp.stack(planes)
    shard = jnp.zeros((seqs,) + part.shape, part.dtype)
    mine = take(by_plane, (place.y - place.z_high) % seqs, 0)
    shard = lax.dynamic_update_index_in_dim(shard, mine, place.z_high, 0)
    for k in range(1, seqs):
        pairs = []
        for z, x, c in place.everyone():
            high, low = divmod(z, place.z_low_size)
            other = ((high + k) % seqs) * place.z_low_size + low
            pairs.append((place.index(z, x, c), place.index(other, x, c)))
        sent = take(by_plane, (place.y - place.z_high - k) % seqs, 0)
        got = lax.ppermute(sent, "fsdp", pairs)
        shard = lax.dynamic_update_index_in_dim(shard, got, (place.z_high - k) % seqs, 0)
    return shard.reshape(-1, part.shape[1]).astype(F32)


def sum_everywhere(place, value):
    for axis, count in (("fsdp", place.fsdp), ("seq", place.seqs)):
        bit = 1
        while bit < count:
            value = value + lax.ppermute(value, axis, [(i, i ^ bit) for i in range(count)])
            bit *= 2
    return value


def head_window(head):
    low = head * HEAD_SIZE // 128 * 128
    high = -(-(head + 1) * HEAD_SIZE // 128) * 128
    return low, high


def sigmoid(value):
    return 1.0 / (1.0 + jnp.exp(-value))


def conv_parts(values, taps_ref, seg_col):
    rows = values.shape[0]
    index = lax.broadcasted_iota(jnp.int32, (rows, 1), 0)
    near_one = (index >= 1) & (pltpu.roll(seg_col, 1, 0) == seg_col)
    near_two = (index >= 2) & (pltpu.roll(seg_col, 2, 0) == seg_col)
    prev_one = jnp.where(near_one, pltpu.roll(values, 1, 0), 0.0)
    prev_two = jnp.where(near_two, pltpu.roll(values, 2, 0), 0.0)
    conv = taps_ref[0:1] * values + taps_ref[1:2] * prev_one + taps_ref[2:3] * prev_two
    return conv, prev_one, prev_two, near_one, near_two


def masks(rows, seg_col, seg_row):
    at = lax.broadcasted_iota(jnp.int32, (rows, rows), 0)
    of = lax.broadcasted_iota(jnp.int32, (rows, rows), 1)
    return (seg_col == seg_row) & (at >= of)


def lanes_between(low, high, start, stop):
    lane = low + lax.broadcasted_iota(jnp.int32, (1, high - low), 1)
    return (lane >= start) & (lane < stop)


def relative(y_ref, seqs, piece):
    return lax.rem(y_ref[0] - piece + seqs, seqs)


def read_pieces(y_ref, ref):
    seqs = ref.shape[0]
    return jnp.concatenate([ref[relative(y_ref, seqs, s), 0] for s in range(seqs)], axis=0)


def write_pieces(y_ref, ref, value, low, high):
    seqs, rows = ref.shape[0], ref.shape[2]
    for s in range(seqs):
        ref[relative(y_ref, seqs, s), 0, :, low:high] = value[s * rows : (s + 1) * rows]


def mix_kernel(heads, y_ref, qkv_in, taps_ref, segc_ref, segr_ref, mixed_ref, qkv_ref, att_ref):
    qkv_ref[...] = read_pieces(y_ref, qkv_in)
    rows = qkv_ref.shape[0]
    qk_width = heads * FEAT
    width = heads * HEAD_SIZE
    seg_col = segc_ref[0]
    allowed = masks(rows, seg_col, segr_ref[0])
    queries = qkv_ref[:, 0:qk_width]
    keys = qkv_ref[:, qk_width : 2 * qk_width]
    for head in range(heads):
        mine = lanes_between(0, qk_width, head * FEAT, (head + 1) * FEAT)
        query = jnp.where(mine, queries, jnp.zeros_like(queries))
        scores = dot(query, keys, ((1,), (1,))) * 0.25
        kern = jnp.where(allowed, 1.0 + scores + 0.5 * scores * scores, 0.0)
        den = jnp.sum(kern, axis=1, keepdims=True)
        low, high = head_window(head)
        high = min(high, width)
        num = dot(kern.astype(BF16), qkv_ref[:, 2 * qk_width + low : 2 * qk_width + high])
        here = lanes_between(low, high, head * HEAD_SIZE, (head + 1) * HEAD_SIZE)
        att_ref[:, low:high] = jnp.where(here, num * (1.0 / den), att_ref[:, low:high])
    values = qkv_ref[:, 2 * qk_width : 2 * qk_width + width].astype(F32)
    conv = conv_parts(values, taps_ref, seg_col)[0]
    mixed = (att_ref[...] * conv * sigmoid(conv)).astype(BF16)
    write_pieces(y_ref, mixed_ref, mixed, 0, width)


def mix_back_kernel(
    heads, y_ref, qkv_in, dmixed_in, taps_ref, segc_ref, segr_ref, dqkv_ref, dtaps_ref,
    qkv_ref, dmixed_ref, att_ref, silu_ref, dv_ref,
):
    qkv_ref[...] = read_pieces(y_ref, qkv_in)
    dmixed_ref[...] = read_pieces(y_ref, dmixed_in).astype(F32)
    rows = qkv_ref.shape[0]
    qk_width = heads * FEAT
    width = heads * HEAD_SIZE
    seg_col = segc_ref[0]
    allowed = masks(rows, seg_col, segr_ref[0])
    queries = qkv_ref[:, 0:qk_width]
    keys = qkv_ref[:, qk_width : 2 * qk_width]
    values = qkv_ref[:, 2 * qk_width : 2 * qk_width + width].astype(F32)
    conv, prev_one, prev_two, near_one, near_two = conv_parts(values, taps_ref, seg_col)
    sig = sigmoid(conv)
    silu_ref[...] = dmixed_ref[...] * conv * sig
    dv_ref[...] = jnp.zeros_like(dv_ref)
    dq = jnp.zeros((rows, qk_width), F32)
    dk = jnp.zeros((rows, qk_width), F32)
    for head in range(heads):
        mine = lanes_between(0, qk_width, head * FEAT, (head + 1) * FEAT)
        query = jnp.where(mine, queries, jnp.zeros_like(queries))
        scores = dot(query, keys, ((1,), (1,))) * 0.25
        kern = jnp.where(allowed, 1.0 + scores + 0.5 * scores * scores, 0.0)
        inv_den = 1.0 / jnp.sum(kern, axis=1, keepdims=True)
        kern_low = kern.astype(BF16)
        low, high = head_window(head)
        high = min(high, width)
        value = qkv_ref[:, 2 * qk_width + low : 2 * qk_width + high]
        att = dot(kern_low, value) * inv_den
        here = lanes_between(low, high, head * HEAD_SIZE, (head + 1) * HEAD_SIZE)
        att_ref[:, low:high] = jnp.where(here, att, att_ref[:, low:high])
        datt = jnp.where(here, silu_ref[:, low:high], 0.0) * inv_den
        row_dot = jnp.sum(datt * att, axis=1, keepdims=True)
        datt_low = datt.astype(BF16)
        dkern = dot(datt_low, value, ((1,), (1,))) - row_dot
        dscores = jnp.where(allowed, dkern * (0.25 + 0.25 * scores), 0.0).astype(BF16)
        dq = dq + jnp.where(mine, dot(dscores, keys), 0.0)
        dk = dk + dot(dscores, query, ((0,), (0,)))
        dv_ref[:, low:high] += dot(kern_low, datt_low, ((0,), (0,)))
    dconv = dmixed_ref[...] * att_ref[...] * sig * (1.0 + conv * (1.0 - sig))
    dtaps_ref[0, 0:1] = jnp.sum(dconv * values, axis=0, keepdims=True)
    dtaps_ref[0, 1:2] = jnp.sum(dconv * prev_one, axis=0, keepdims=True)
    dtaps_ref[0, 2:3] = jnp.sum(dconv * prev_two, axis=0, keepdims=True)
    dtaps_ref[0, 3:8] = jnp.zeros((5, width), F32)
    back_one = pltpu.roll(jnp.where(near_one, dconv, 0.0), rows - 1, 0)
    back_two = pltpu.roll(jnp.where(near_two, dconv, 0.0), rows - 2, 0)
    dv = (
        dv_ref[...]
        + taps_ref[0:1] * dconv
        + taps_ref[1:2] * back_one
        + taps_ref[2:3] * back_two
    )
    write_pieces(y_ref, dqkv_ref, dq.astype(BF16), 0, qk_width)
    write_pieces(y_ref, dqkv_ref, dk.astype(BF16), qk_width, 2 * qk_width)
    write_pieces(y_ref, dqkv_ref, dv.astype(BF16), 2 * qk_width, 2 * qk_width + width)
    write_pieces(y_ref, dqkv_ref, jnp.zeros((rows, SMALL), BF16), 2 * qk_width + width, None)


def seg_specs(rows):
    return [
        pl.BlockSpec((1, rows, 1), lambda m: (m, 0, 0)),
        pl.BlockSpec((1, 1, rows), lambda m: (m, 0, 0)),
    ]


def piece_spec(shape):
    seqs, _, rows, width = shape
    return pl.BlockSpec((seqs, 1, rows, width), lambda m: (0, m, 0, 0))


def mix_forward(heads, y, qkv, taps, segments):
    seqs, micro, rows, qkv_width = qkv.shape
    group = seqs * rows
    width = heads * HEAD_SIZE
    return pl.pallas_call(
        partial(mix_kernel, heads),
        grid=(micro,),
        out_shape=jax.ShapeDtypeStruct((seqs, micro, rows, width), BF16),
        in_specs=[
            pl.BlockSpec(memory_space=pltpu.SMEM),
            piece_spec(qkv.shape),
            pl.BlockSpec(taps.shape, lambda m: (0, 0)),
            *seg_specs(group),
        ],
        out_specs=piece_spec((seqs, micro, rows, width)),
        scratch_shapes=[pltpu.VMEM((group, qkv_width), BF16), pltpu.VMEM((group, width), F32)],
        compiler_params=pltpu.CompilerParams(vmem_limit_bytes=48 * 2**20),
    )(y.reshape(1), qkv, taps, segments[:, :, None], segments[:, None, :])


def mix_backward(heads, y, qkv, dmixed, taps, segments):
    seqs, micro, rows, qkv_width = qkv.shape
    group = seqs * rows
    width = heads * HEAD_SIZE
    return pl.pallas_call(
        partial(mix_back_kernel, heads),
        grid=(micro,),
        out_shape=(
            jax.ShapeDtypeStruct(qkv.shape, BF16),
            jax.ShapeDtypeStruct((micro, 8, width), F32),
        ),
        in_specs=[
            pl.BlockSpec(memory_space=pltpu.SMEM),
            piece_spec(qkv.shape),
            piece_spec(dmixed.shape),
            pl.BlockSpec(taps.shape, lambda m: (0, 0)),
            *seg_specs(group),
        ],
        out_specs=(
            piece_spec(qkv.shape),
            pl.BlockSpec((1, 8, width), lambda m: (m, 0, 0)),
        ),
        scratch_shapes=[pltpu.VMEM((group, qkv_width), BF16)]
        + [pltpu.VMEM((group, width), F32)] * 4,
        compiler_params=pltpu.CompilerParams(vmem_limit_bytes=56 * 2**20),
    )(y.reshape(1), qkv, dmixed, taps, segments[:, :, None], segments[:, None, :])


class Gather:
    def __init__(self, arrays):
        self.shapes = [a.shape for a in arrays]
        self.joined = not any(a.shape[0] % 8 or a.shape[1] % 128 for a in arrays)
        if not self.joined:
            self.raw = [lax.all_gather(a, "fsdp", axis=0, tiled=True) for a in arrays]
            return
        counts = [a.size // 1024 for a in arrays]
        buffer = jnp.zeros((max(GATHER_TILES, sum(counts)), 8, 128), arrays[0].dtype)
        at = 0
        for a, count in zip(arrays, counts):
            t = a.reshape(a.shape[0] // 8, 8, a.shape[1] // 128, 128)
            t = jnp.swapaxes(t, 1, 2).reshape(-1, 8, 128)
            buffer = lax.dynamic_update_slice(buffer, t, (at, 0, 0))
            at += count
        self.raw = [lax.all_gather(buffer, "fsdp", axis=0, tiled=False)]

    def after(self, *values):
        count = len(self.raw)
        values = fence(*self.raw, *values)
        self.raw = list(values[:count])
        return values[count:]

    def arrays(self):
        if not self.joined:
            return self.raw
        gathered = []
        at = 0
        for rows, columns in self.shapes:
            count = rows * columns // 1024
            t = self.raw[0][:, at : at + count]
            t = t.reshape(-1, rows // 8, columns // 128, 8, 128)
            gathered.append(jnp.swapaxes(t, 2, 3).reshape(-1, columns))
            at += count
        return gathered


def on_device(
    tokens,
    seq_order,
    seq_lengths,
    valid_count,
    teacher,
    norm_one,
    w_query,
    w_key,
    w_value,
    conv_taps,
    w_out,
    norm_two,
    w_gate,
    w_up,
    w_down,
):
    place = Place()
    seqs, y = place.seqs, place.y
    micro, rows_dev, model = tokens.shape[0], tokens.shape[2], tokens.shape[3]
    group = seqs * rows_dev
    own_rows = micro * rows_dev
    heads = HEADS // seqs
    qk_width = heads * FEAT
    width = heads * HEAD_SIZE
    slots = micro * place.fsdp * group
    bits = place.fsdp.bit_length() - 1
    seq_bits = seqs.bit_length() - 1

    def columns(weight):
        part = weight.shape[1] // seqs
        return lax.dynamic_slice_in_dim(weight, y * part, part, 1)

    shard_rows = w_query.shape[0]
    valid = valid_count[:, 0]
    coded = jnp.stack([valid // 16, valid % 16], axis=1).reshape(1, 2 * micro).astype(BF16)
    first_row = lax.broadcasted_iota(jnp.int32, (shard_rows, 2 * micro), 0) == 0
    small = jnp.concatenate(
        [
            norm_one[:, None],
            norm_two[:, None],
            conv_taps.T,
            jnp.where(first_row, coded, jnp.zeros_like(coded)),
        ],
        axis=1,
    )
    small = jnp.pad(small, ((0, 0), (0, SMALL - small.shape[1])))
    first_shard = jnp.concatenate(
        [columns(w_query), columns(w_key), columns(w_value), small], axis=1
    )
    out_part = spread_rows(place, w_out)
    first, gate_w, out_w = Gather([first_shard, columns(w_gate), out_part]).arrays()
    down_part = spread_rows(place, w_down)
    late = Gather([columns(w_up), down_part])
    out_w = plane_rows(place, out_w)

    qkv_width = 2 * qk_width + width
    wide = qkv_width + SMALL
    small_all = first[:, qkv_width : qkv_width + 16].astype(F32).T
    gain_one, gain_two = small_all[0], small_all[1]
    taps = lax.dynamic_slice_in_dim(small_all[2:5], y * width, width, 1)
    taps = jnp.pad(taps, ((0, 5), (0, 0)))
    coded_sum = jnp.sum(small_all[5 : 5 + 2 * micro], axis=1)
    total = 16.0 * jnp.sum(coded_sum[0::2]) + jnp.sum(coded_sum[1::2])
    scale = slots / total

    order = seq_order[:, 0, 0]
    local = jnp.arange(rows_dev, dtype=jnp.int32)
    order_k = gather_seq(place, order)
    tokens_k = gather_seq(place, tokens[:, 0])
    picks = [(o[..., None] == local).astype(BF16) for o in order_k]
    pick = picks[0]
    packed_k = [
        jnp.einsum("mij,mjd->mid", o, t, preferred_element_type=BF16).reshape(own_rows, model)
        for o, t in zip(picks, tokens_k)
    ]
    wanted = jnp.einsum("mij,mjd->mid", pick, teacher[:, 0], preferred_element_type=BF16)
    wanted = wanted.reshape(own_rows, model)
    keep = (order + y * rows_dev < valid[:, None]).astype(F32).reshape(own_rows, 1)
    ends = jnp.cumsum(seq_lengths[:, 0], axis=1)
    positions = jnp.arange(group, dtype=jnp.int32)
    segments = jnp.sum((positions[None, :, None] >= ends[:, None, :]).astype(jnp.int32), axis=2)

    packed = jnp.concatenate(packed_k, axis=0)
    packed_f = packed.astype(F32)
    root_one = lax.rsqrt(jnp.mean(packed_f * packed_f, axis=1, keepdims=True) + EPSILON)
    n_one = (packed_f * root_one * gain_one).astype(BF16)
    qkv = dot(n_one, first).astype(BF16).reshape(seqs, micro, rows_dev, wide)
    mixed = mix_forward(heads, y, qkv, taps, segments).reshape(seqs * own_rows, width)

    def pieces(value):
        return [value[k * own_rows : (k + 1) * own_rows] for k in range(seqs)]

    def scatter(parts):
        got = [seq_send(place, parts[k].astype(BF16), seqs - k) for k in range(1, seqs)]
        return parts[0], got

    def project(rows_k, weight, dims=((1,), (0,))):
        parts = [None] * seqs
        for k in list(range(1, seqs)) + [0]:
            parts[k] = dot(rows_k[k], weight, dims)
        return parts

    packed_own = packed_k[0].astype(F32)
    own, got = scatter(project(pieces(mixed), out_w))
    resid = packed_own + own
    for part in got:
        resid = resid + part.astype(F32)
    root_two = lax.rsqrt(jnp.mean(resid * resid, axis=1, keepdims=True) + EPSILON)
    n_two_k = gather_seq(place, (resid * root_two * gain_two).astype(BF16))
    gate_k = [dot(n, gate_w) for n in n_two_k]
    gate_k = list(late.after(*gate_k))
    up_w, down_w = late.arrays()
    down_w = plane_rows(place, down_w)
    up_k = [dot(n, up_w) for n in n_two_k]
    sig_k = [jax.nn.sigmoid(g) for g in gate_k]
    hidden_k = [(g * s * u).astype(BF16) for g, s, u in zip(gate_k, sig_k, up_k)]
    own, got = scatter(project(hidden_k, down_w))
    result = resid + own
    for part in got:
        result = result + part.astype(F32)
    error = (result - wanted.astype(F32)) * keep
    d_result = scale * error
    d_low = d_result.astype(BF16)
    d_low_k = gather_seq(place, d_low)
    squares = sum_everywhere(place, jnp.sum(error * error, axis=(0, 1), keepdims=True))

    def to_given(value):
        value = value.astype(BF16).reshape(micro, rows_dev, model)
        return jnp.einsum("mij,mid->mjd", pick, value, preferred_element_type=BF16)

    output = to_given(result)

    def ffn_back(k, d_low):
        d_hidden = dot(d_low, down_w, ((1,), (1,)))
        gate, up, sig = gate_k[k], up_k[k], sig_k[k]
        d_gate = (d_hidden * up * sig * (1.0 + gate * (1.0 - sig))).astype(BF16)
        d_up = (d_hidden * gate * sig).astype(BF16)
        return d_gate, d_up

    column_labels = list(range(bits - 1, -1, -1))
    row_labels = list(range(bits - 1 - seq_bits, -1, -1)) + list(
        range(bits - 1, bits - 1 - seq_bits, -1)
    )
    x_bits = list(range(1, bits - 2))
    x_first = [[0], x_bits, [bits - 2], [bits - 1]]

    def by_rows(grad, order):
        view = grad.reshape([2] * bits + [grad.shape[0] // place.fsdp, grad.shape[1]])
        return Reduction(place, view, row_labels, order)

    def by_columns(grad, order):
        view = grad.reshape([2] * bits + [grad.shape[0] // place.fsdp, grad.shape[1]])
        return Reduction(place, view, column_labels, order)

    def weight_grad(left, right):
        return dot(left, right, ((0,), (0,))).astype(BF16)

    d_gate_own, d_up_own = ffn_back(0, d_low)
    hidden = jnp.concatenate(hidden_k, axis=0)
    n_two = jnp.concatenate(n_two_k, axis=0)
    d_gate_own, d_up_own, squares, *d_low_others = fence(
        d_gate_own, d_up_own, squares, *d_low_k[1:]
    )
    down = by_rows(weight_grad(hidden, jnp.concatenate([d_low, *d_low_others])), x_first)
    d_low_others = down.start(*d_low_others)
    d_pairs = [(d_gate_own, d_up_own)] + [
        ffn_back(k + 1, d) for k, d in enumerate(d_low_others)
    ]
    d_gate_k = [a for a, b in d_pairs]
    d_up_k = [b for a, b in d_pairs]
    d_gate = jnp.concatenate(d_gate_k, axis=0)
    d_up = jnp.concatenate(d_up_k, axis=0)
    gate_grad = weight_grad(n_two, d_gate)
    gate_grad, d_up, *d_both = fence(gate_grad, d_up, *d_gate_k, *d_up_k)
    gate_sum = lax.psum_scatter(gate_grad, "fsdp", scatter_dimension=0, tiled=True)
    d_both = down.after(*d_both)
    d_both = down.start(*d_both)
    d_gate_k, d_up_k = d_both[:seqs], d_both[seqs:]

    def ffn_part(k):
        return dot(d_gate_k[k], gate_w, ((1,), (1,))) + dot(d_up_k[k], up_w, ((1,), (1,)))

    parts = [ffn_part(k).astype(BF16) for k in range(1, seqs)]
    d_both = place.in_turn(*parts, d_up, *d_gate_k, *d_up_k)
    parts, d_up = d_both[: seqs - 1], d_both[seqs - 1]
    d_gate_k, d_up_k = d_both[seqs:-seqs], d_both[-seqs:]
    got = [seq_send(place, part, seqs - 1 - k) for k, part in enumerate(parts)]
    up = by_columns(weight_grad(n_two, d_up), x_first)
    d_gate_k[0], d_up_k[0] = up.start(d_gate_k[0], d_up_k[0])
    own = ffn_part(0)
    own, = up.after(own)
    own, *got = place.in_turn(own, *got)
    d_n_two = own
    for part in got:
        d_n_two = d_n_two + part.astype(F32)
    grad_norm_two = jnp.sum(d_n_two * resid * root_two, axis=0)
    d_scaled = d_n_two * gain_two
    d_resid = (
        d_result
        + root_two * d_scaled
        - resid * root_two**3 * jnp.mean(d_scaled * resid, axis=1, keepdims=True)
    )
    dm_own, = place.in_turn(d_resid.astype(BF16))
    dm_k = gather_seq(place, dm_own)
    dm_own, = up.start(dm_own)
    d_mixed_own = dot(dm_own, out_w, ((1,), (1,)))
    d_mixed_own, *dm_others = place.in_turn(d_mixed_own, *dm_k[1:])
    out = by_rows(weight_grad(mixed, jnp.concatenate([dm_own, *dm_others])), x_first)
    dm_others = out.start(*dm_others)
    d_mixed = jnp.concatenate(
        [d_mixed_own] + [dot(d, out_w, ((1,), (1,))) for d in dm_others]
    ).reshape(seqs, micro, rows_dev, width)
    d_mixed, = down.after(d_mixed)
    d_mixed, = down.start(d_mixed)
    d_mixed, = out.after(d_mixed)
    d_mixed, = out.start(d_mixed)
    d_qkv, d_taps = mix_backward(heads, y, qkv, d_mixed, taps, segments)
    d_qkv = d_qkv.reshape(seqs * own_rows, wide)
    d_taps = jnp.sum(d_taps, axis=0)[:3]
    others = [dot(d, first, ((1,), (1,))) for d in pieces(d_qkv)[1:]]
    sent = [part.astype(BF16) for part in others]
    *sent, d_qkv = place.in_turn(*sent, d_qkv)
    got = [seq_send(place, part, seqs - 1 - k) for k, part in enumerate(sent)]
    own = dot(d_qkv[:own_rows], first, ((1,), (1,)))
    grad_norm_one = sum(
        jnp.sum(part * (p.astype(F32) * r), axis=0)
        for part, p, r in zip([own, *others], packed_k, pieces(root_one))
    )
    d_taps_wide = lax.dynamic_update_slice_in_dim(
        jnp.zeros((3, model), F32), d_taps, y * width, 1
    )
    extra = jnp.concatenate(
        [grad_norm_one[None], grad_norm_two[None], d_taps_wide, jnp.zeros((3, model), F32)]
    )
    extra = jnp.pad(extra.T, ((0, 0), (qkv_width, SMALL - extra.shape[0])))
    grad_first = (dot(n_one, d_qkv, ((0,), (0,))) + extra).astype(BF16)
    grad_first, own = fence(grad_first, own)
    first_sum = lax.psum_scatter(grad_first, "fsdp", scatter_dimension=0, tiled=True)
    own, = up.after(own)
    own, = up.start(own)
    own, *got = place.in_turn(own, *got)

    d_n_one = own
    for part in got:
        d_n_one = d_n_one + part.astype(F32)
    root_own = root_one[:own_rows]
    d_scaled = d_n_one * gain_one
    d_packed = (
        d_resid
        + root_own * d_scaled
        - packed_own * root_own**3 * jnp.mean(d_scaled * packed_own, axis=1, keepdims=True)
    )
    def join(parts):
        return jnp.concatenate(parts, axis=1).astype(F32)

    def all_pieces(value):
        return in_order(place, gather_seq(place, value))

    input_grad = to_given(d_packed)
    input_grad, = down.after(input_grad)
    input_grad, = down.start(input_grad)
    out.after()
    out.start()
    up.after()
    up.start()
    out.after()
    out.start()
    gate_sum, = place.in_turn(gate_sum)
    gate_k = gather_seq(place, gate_sum)
    down.after()
    down_k = unspread_start(place, down.result())
    up.after()
    up_k = gather_seq(place, up.result())
    out.after()
    out_k = unspread_start(place, out.result())
    gate_k = place.in_turn(*gate_k)
    grad_gate = join(in_order(place, gate_k))
    down_k = place.in_turn(*down_k)
    grad_down = unspread_end(place, down_k)
    up_k = place.in_turn(*up_k)
    grad_up = join(in_order(place, up_k))
    out_k = place.in_turn(*out_k)
    grad_out = unspread_end(place, out_k)
    first_sum, = place.in_turn(first_sum)
    first_parts = all_pieces(first_sum)
    loss = (squares[0, 0] + place.turn[0, 0]) / (total * model)
    extra_sum = sum(part[:, qkv_width:].astype(F32) for part in first_parts)
    return (
        output[:, None],
        input_grad[:, None],
        extra_sum[:, 0],
        join([part[:, :qk_width] for part in first_parts]),
        join([part[:, qk_width : 2 * qk_width] for part in first_parts]),
        join([part[:, 2 * qk_width : qkv_width] for part in first_parts]),
        extra_sum[:, 2:5].T,
        grad_out,
        extra_sum[:, 1],
        grad_gate,
        grad_up,
        grad_down,
        loss,
    )


def solution(mesh):
    rows = P(None, "fsdp", "seq", None)
    placed = (
        rows,
        rows,
        P(None, "fsdp", None),
        P(None, "fsdp"),
        rows,
        P("fsdp"),
        P("fsdp", None),
        P("fsdp", None),
        P("fsdp", None),
        P(None, "fsdp"),
        P("fsdp", None),
        P("fsdp"),
        P("fsdp", None),
        P("fsdp", None),
        P("fsdp", None),
    )
    return jax.shard_map(
        on_device,
        mesh=mesh,
        in_specs=placed,
        out_specs=(
            rows,
            rows,
            P("fsdp"),
            P("fsdp", None),
            P("fsdp", None),
            P("fsdp", None),
            P(None, "fsdp"),
            P("fsdp", None),
            P("fsdp"),
            P("fsdp", None),
            P("fsdp", None),
            P("fsdp", None),
            P(),
        ),
        check_vma=False,
    )
```

time: 985 us -> 661 us (0.67)
  waiting for transfers between devices: 534 us -> 278 us
  starting transfers between devices: 141 us -> 102 us
  local copies, waits for them, and re-layouts: 80.6 us -> 59.5 us
    all_gather x5 -> x2, waiting for transfers between devices: 199 us -> 57.7 us  [__init__(): self.raw = [lax.all_gather(buffer, 'fsdp', axis=0, tiled=False)]]
    ppermute x56 -> x28, waiting for transfers between devices: 306 us -> 199 us  [the longest x12 104 us: send(): got = lax.ppermute(sent, 'fsdp', pairs)]
    ppermute x56 -> x28, starting transfers between devices: 119 us -> 79.4 us  [the longest x14 60.5 us: seq_send(): return lax.ppermute(value, 'seq', pairs)]
    slice x0 -> x8, local copies, waits for them, and re-layouts: none -> 25.4 us  [the longest x5 24.1 us: arrays(): t = self.raw[0][:, at:at + count]]
    dynamic_slice x4 -> x0, local copies, waits for them, and re-layouts: 17.3 us -> none  [take(): return lax.dynamic_index_in_dim(array, index, axis, keepdims=False)]
    squeeze x15 -> x2, local copies, waits for them, and re-layouts: 17.6 us -> 1.75 us  [take(): return lax.dynamic_index_in_dim(array, index, axis, keepdims=False)]
    dot_general x15 -> x24, matrix products: 115 us -> 120 us  [dot(): lax.dot_general(left, right, (dims, ((), ())), preferred_element_type=F32)]
    convert_element_type x35 -> x18, other arithmetic: 36.4 us -> 37.8 us  [the longest x12 29.8 us: total(): return total.astype(BF16)]
  transfers between devices with their start and end apart: 68 -> 39, of which waited for: 39 -> 25; matrix products, arithmetic and copies ran while one was open for 19% -> 27% of each run, Pallas kernels for 2% -> 2%
where the time goes in v2:
time: 661 us; the launch traced here: 656 us
  waiting for transfers between devices  278 us (42%)
  matrix products  125 us (19%)
  starting transfers between devices  102 us (15%)
  local copies, waits for them, and re-layouts  59.5 us (9%)
  other arithmetic  54.4 us (8%)
  between operations  21.5 us (3%)
  Pallas kernels  15.3 us (2%)
    dot_general x24, matrix products, dot(): lax.dot_general(left, right, (dims, ((), ())), preferred_element_type=F32)  120 us
    ppermute x12, waiting for transfers between devices, send(): got = lax.ppermute(sent, 'fsdp', pairs)  104 us
    ppermute x14, waiting for transfers between devices, seq_send(): return lax.ppermute(value, 'seq', pairs)  91.6 us
    ppermute x14, starting transfers between devices, seq_send(): return lax.ppermute(value, 'seq', pairs)  60.5 us
    all_gather x2, waiting for transfers between devices, __init__(): self.raw = [lax.all_gather(buffer, 'fsdp', axis=0, tiled=False)]  57.7 us
    convert_element_type x12, other arithmetic, total(): return total.astype(BF16)  29.8 us
    slice x5, local copies, waits for them, and re-layouts, arrays(): t = self.raw[0][:, at:at + count]  24.1 us
    ppermute x12, starting transfers between devices, send(): got = lax.ppermute(sent, 'fsdp', pairs)  18.8 us
  transfers between devices with their start and end apart: 39, of which 25 were waited for; matrix products, arithmetic and copies ran while one was open for 27% of the time, Pallas kernels for 2%

profile of v2, /device:TPU:0, one launch (start us, length us, event | category | flops | bytes accessed | tf_op | source)
XLA Modules:
  0.0 655.7 jit_solution(17893008215809394025)
XLA Ops:
  9.0 5.9 collective-permute-start.2
  27.1 16.0 %collective-permute-done.4 = bf16[152,1792]{1,0:T(8,128)(2,1)S(1)} collective-permute-done((bf16[152,1792]{1,0:T(8,128)(2,1)S(1)}, bf16[152,1792]{1,0:T(8,128)(2,1)S(1)}, u32[]{:S(2)}, u32[]{:S(2)}) %collective-permute-start.4) | collective-permute-done | bytes 544800 | tf_op jit(solution)/shard_map/ppermute | solution.py:156
  44.3 20.3 %collective-permute-start.1 = (bf16[2,128,1792]{2,1,0:T(8,128)(2,1)S(1)}, bf16[2,128,1792]{2,1,0:T(8,128)(2,1)S(1)}, u32[]{:S(2)}, u32[]{:S(2)}) collective-permute-start(bf16[2,128,1792]{2,1,0:T(8,128)(2,1)S(1)} %bitcast.385), channel_id=1, source_target_pairs={{0,16},{16,0},{1,17},{17,1},{2,18},{18,2},{3,19},{19,3},{4,20},{20... | collective-permute-start | bytes 2752520 | tf_op jit(solution)/shard_map/ppermute | solution.py:64
  65.6 19.4 %collective-permute-done = s32[2,128]{1,0:T(2,128)S(1)} collective-permute-done((s32[2,128]{1,0:T(2,128)S(1)}, s32[2,128]{1,0:T(2,128)S(1)}, u32[]{:S(2)}, u32[]{:S(2)}) %collective-permute-start) | collective-permute-done | bytes 1056 | tf_op jit(solution)/shard_map/ppermute | solution.py:64
  85.9 32.0 %all-gather.4.cloned.1.call-done = bf16[16,528,8,128]{3,2,1,0:T(8,128)(2,1)} async-done(((bf16[1,528,8,128]{3,2,1,0:T(8,128)(2,1)}), bf16[16,528,8,128]{3,2,1,0:T(8,128)(2,1)}) %all-gather.4.cloned.1.call-update) | async-done | bytes 17301520 | tf_op jit(solution)/shard_map/all_gather | solution.py:407
  136.4 12.6 %collective-permute-start.3 = (bf16[256,1792]{1,0:T(8,128)(2,1)S(1)}, bf16[256,1792]{1,0:T(8,128)(2,1)S(1)}, u32[]{:S(2)}, u32[]{:S(2)}) collective-permute-start(bf16[256,1792]{1,0:T(8,128)(2,1)S(1)} %convolution_convert_fusion.6), channel_id=1, source_target_pairs={{0,16},{16,0},{1,17},{17,1},{2,18},{18,2},{3,19},{19,3},{4,20},{20... | collective-permute-start | bytes 2752520 | tf_op jit(solution)/shard_map/ppermute | solution.py:64
  150.4 19.4 %collective-permute-done.3 = bf16[256,1792]{1,0:T(8,128)(2,1)S(1)} collective-permute-done((bf16[256,1792]{1,0:T(8,128)(2,1)S(1)}, bf16[256,1792]{1,0:T(8,128)(2,1)S(1)}, u32[]{:S(2)}, u32[]{:S(2)}) %collective-permute-start.3) | collective-permute-done | bytes 917536 | tf_op jit(solution)/shard_map/ppermute | solution.py:64
  177.0 7.6 %slice.150 = bf16[16,266,8,128]{3,2,1,0:T(8,128)(2,1)} slice(bf16[16,528,8,128]{3,2,1,0:T(8,128)(2,1)} %all-gather.4.cloned.1.call-done), slice={[0:16], [140:406], [0:8], [0:128]} | slice | bytes 17432576 | tf_op jit(solution)/shard_map/slice | solution.py:422
  184.7 8.1 %fusion.76 = f32[256,2432]{1,0:T(8,128)} fusion(bf16[256,1792]{1,0:T(8,128)(2,1)} %multiply_convert_fusion.6, bf16[1792,2432]{1,0:T(8,128)(2,1)} %bitcast.337), kind=kOutput, calls=%fused_computation.215 | convolution fusion | flops 2231369728 | bytes 12124160 | tf_op jit(solution)/shard_map/dot_general | solution.py:23
  200.0 25.7 %all-gather.6.cloned.1.call-done = bf16[8512,8,128]{2,1,0:T(8,128)(2,1)} async-done(((bf16[532,8,128]{2,1,0:T(8,128)(2,1)}), bf16[8512,8,128]{2,1,0:T(8,128)(2,1)}) %all-gather.6.cloned.1.call-update) | async-done | bytes 17432592 | tf_op jit(solution)/shard_map/all_gather | solution.py:407
  225.7 12.0 %fusion.71 = (bf16[16,266,8,128]{3,2,1,0:T(8,128)(2,1)}, bf16[16,266,8,128]{3,2,1,0:T(8,128)(2,1)}) fusion(bf16[16,532,8,128]{3,2,1,0:T(8,128)(2,1)} %bitcast.326), kind=kLoop, calls=%fused_computation.210 | loop fusion | bytes 34865152 | tf_op jit(solution)/shard_map/slice | solution.py:422
  237.7 7.5 %copy.124 = bf16[8,2,152,1792]{3,2,1,0:T(8,128)(2,1)} copy(bf16[8,2,152,1792]{3,2,0,1:T(8,128)(2,1)} %bitcast.321) | data formatting | bytes 17432576 | tf_op jit(solution)/shard_map/transpose | solution.py:164
  245.2 8.8 %multiply_convert_fusion.4 = (bf16[256,2432]{1,0:T(8,128)(2,1)S(1)}, f32[256,2432]{1,0:T(8,128)}) fusion(f32[256,2432]{1,0:T(8,128)} %fusion.77, bf16[256,1792]{1,0:T(8,128)(2,1)} %collective-permute-done.5, bf16[1792,2432]{1,0:T(8,128)(2,1)} %bitcast.352), kind=kOutput, calls=%fused_computation.39 | convolution fusion | flops 2235105280 | bytes 15859712 | tf_op jit(solution)/shard_map/dot_general | solution.py:23
  263.6 15.7 %collective-permute-done.6 = bf16[256,1792]{1,0:T(8,128)(2,1)S(1)} collective-permute-done((bf16[256,1792]{1,0:T(8,128)(2,1)S(1)}, bf16[256,1792]{1,0:T(8,128)(2,1)S(1)}, u32[]{:S(2)}, u32[]{:S(2)}) %collective-permute-start.6) | collective-permute-done | bytes 917536 | tf_op jit(solution)/shard_map/ppermute | solution.py:64
  285.3 6.1 multiply_convert_fusion.2
  310.6 7.4 %convolution_convert_fusion.2 = bf16[2432,1792]{1,0:T(8,128)(2,1)S(1)} fusion(bf16[256,2432]{1,0:T(8,128)(2,1)} %copy-done.55, bf16[256,2432]{1,0:T(8,128)(2,1)S(1)} %get-tuple-element.378, bf16[256,1792]{1,0:T(8,128)(2,1)S(1)} %collective-permute-done.12, bf16[256,1792]{1,0:T(8,128)(2,1)S(1)} %get-tuple-element.352), kind=kOutput, calls=%fused_computation.2 | convolution fusion | flops 4475748352 | bytes 13041664 | tf_op jit(solution)/shard_map/dot_general | solution.py:23
  323.0 8.2 %multiply_convert_fusion = (bf16[256,2432]{1,0:T(8,128)(2,1)S(1)}, bf16[256,2432]{1,0:T(8,128)(2,1)S(1)}) fusion(f32[256,2432]{1,0:T(8,128)} %fusion.77, f32[256,2432]{1,0:T(8,128)} %get-tuple-element.381, bf16[256,1792]{1,0:T(8,128)(2,1)} %copy-done.49, bf16[2432,1792]{1,0:T(8,128)(2,1)} %bitcast.343), kind=kOutput, calls=%fused_computation.35 | convolution fusion | flops 2239463424 | bytes 17104896 | tf_op jit(solution)/shard_map/dot_general | solution.py:23
  333.5 8.8 %convolution_convert_fusion.1 = bf16[1792,2432]{1,0:T(8,128)(2,1)} fusion(bf16[256,2432]{1,0:T(8,128)(2,1)S(1)} %get-tuple-element.155, bf16[256,2432]{1,0:T(8,128)(2,1)S(1)} %copy-done.51, bf16[256,1792]{1,0:T(8,128)(2,1)} %collective-permute-done.5, bf16[256,1792]{1,0:T(8,128)(2,1)} %multiply_convert_fusion.6), kind=kOutput, calls=%fused_computation.1 | convolution fusion | flops 4475748352 | bytes 13041664 | tf_op jit(solution)/shard_map/dot_general | solution.py:23
  346.9 6.8 %fusion.78 = f32[256,1792]{1,0:T(8,128)S(1)} fusion(bf16[256,2432]{1,0:T(8,128)(2,1)S(1)} %copy-done.54, bf16[1792,2432]{1,0:T(8,128)(2,1)} %bitcast.338), kind=kOutput, calls=%fused_computation.217 | convolution fusion | flops 2231369728 | bytes 11796480 | tf_op jit(solution)/shard_map/dot_general | solution.py:23
  357.2 7.7 %convolution_convert_fusion = bf16[1792,2432]{1,0:T(8,128)(2,1)S(1)} fusion(bf16[512,2432]{1,0:T(8,128)(2,1)} %pad_maximum_fusion, bf16[256,1792]{1,0:T(8,128)(2,1)} %collective-permute-done.5, bf16[256,1792]{1,0:T(8,128)(2,1)} %multiply_convert_fusion.6), kind=kOutput, calls=%fused_computation | convolution fusion | flops 4470767616 | bytes 13041664 | tf_op jit(solution)/shard_map/dot_general | solution.py:23
  373.6 7.4 %convolution_add_fusion = f32[256,1792]{1,0:T(8,128)S(1)} fusion(f32[256,1792]{1,0:T(8,128)} %fusion.79, bf16[256,2432]{1,0:T(8,128)(2,1)S(1)} %copy-done.28, bf16[1792,2432]{1,0:T(8,128)(2,1)} %bitcast.353), kind=kOutput, calls=%fused_computation.21 | convolution fusion | flops 2231828480 | bytes 13631488 | tf_op jit(solution)/shard_map/dot_general | solution.py:23
  381.0 9.4 %collective-permute-done.16 = bf16[256,1792]{1,0:T(8,128)(2,1)S(1)} collective-permute-done((bf16[256,1792]{1,0:T(8,128)(2,1)}, bf16[256,1792]{1,0:T(8,128)(2,1)S(1)}, u32[]{:S(2)}, u32[]{:S(2)}) %collective-permute-start.16) | collective-permute-done | bytes 917536 | tf_op jit(solution)/shard_map/ppermute | solution.py:64
  400.4 15.0 %collective-permute-done.17 = bf16[256,1792]{1,0:T(8,128)(2,1)S(1)} collective-permute-done((bf16[256,1792]{1,0:T(8,128)(2,1)S(1)}, bf16[256,1792]{1,0:T(8,128)(2,1)S(1)}, u32[]{:S(2)}, u32[]{:S(2)}) %collective-permute-start.17) | collective-permute-done | bytes 917536 | tf_op jit(solution)/shard_map/ppermute | solution.py:64
  426.3 15.5 %collective-permute-done.14 = bf16[2,2,152,1792]{3,2,1,0:T(8,128)(2,1)} collective-permute-done((bf16[2,2,152,1792]{3,2,1,0:T(8,128)(2,1)}, bf16[2,2,152,1792]{3,2,1,0:T(8,128)(2,1)}, u32[]{:S(2)}, u32[]{:S(2)}) %collective-permute-start.14) | collective-permute-done | bytes 2179104 | tf_op jit(solution)/shard_map/ppermute | solution.py:111
  450.7 11.9 %shard_map.247 = (bf16[2,2,128,1280]{3,2,1,0:T(8,128)(2,1)}, f32[2,8,896]{2,1,0:T(8,128)}) custom-call(s32[1]{0:T(128)} %bitcast.3.y_ref, bf16[2,2,128,1280]{3,2,1,0:T(8,128)(2,1)} %bitcast.319, f32[2,2,128,896]{3,2,1,0:T(8,128)} %bitcast.360, f32[8,896]{1,0:T(8,128)} %copy-done.4, s32[2,256,1]{2,1,0:T(8,128)} %copy-done.3, s32[2,1,256]{2,1,0:T(1,128)} %copy-done.5), custom_call_target="tpu_custom_call" | custom-call | tf_op jit(solution)/shard_map/pallas_call | solution.py:368
  472.1 6.7 %add_convert_fusion = bf16[1792,1280]{1,0:T(8,128)(2,1)} fusion(f32[1792,8]{1,0:T(8,128)} %bitcast.387, bf16[512,1280]{1,0:T(8,128)(2,1)} %bitcast.395, f32[1792]{0:T(1024)S(1)} %copy-done.42, f32[512]{0:T(512)S(1)} %add_rsqrt_fusion, bf16[256,1792]{1,0:T(8,128)(2,1)} %bitcast.371, bf16[256,1792]{1,0:T(8,128)(2,1)S(1)} %bitcast.325), kind=kOutput, calls=%fused_computation.3 | convolution fusion | flops 2359820288 | bytes 7799808 | tf_op jit(solution)/shard_map/dot_general | solution.py:23
  478.8 16.1 %collective-permute-done.19 = bf16[2,2,112,2432]{3,2,1,0:T(8,128)(2,1)} collective-permute-done((bf16[2,2,112,2432]{3,2,1,0:T(8,128)(2,1)}, bf16[2,2,112,2432]{3,2,1,0:T(8,128)(2,1)}, u32[]{:S(2)}, u32[]{:S(2)}) %collective-permute-start.19) | collective-permute-done | bytes 2179104 | tf_op jit(solution)/shard_map/ppermute | solution.py:111
  517.6 30.8 %collective-permute-done.24 = bf16[2,112,2432]{2,1,0:T(8,128)(2,1)} collective-permute-done((bf16[2,112,2432]{2,1,0:T(8,128)(2,1)}, bf16[2,112,2432]{2,1,0:T(8,128)(2,1)}, u32[]{:S(2)}, u32[]{:S(2)}) %collective-permute-start.24) | collective-permute-done | bytes 1089568 | tf_op jit(solution)/shard_map/ppermute | solution.py:111
  569.3 21.1 %collective-permute-done.26 = bf16[112,2432]{1,0:T(8,128)(2,1)S(1)} collective-permute-done((bf16[112,2432]{1,0:T(8,128)(2,1)}, bf16[112,2432]{1,0:T(8,128)(2,1)S(1)}, u32[]{:S(2)}, u32[]{:S(2)}) %collective-permute-start.26) | collective-permute-done | bytes 544800 | tf_op jit(solution)/shard_map/ppermute | solution.py:111
  592.4 11.0 %collective-permute-done.25 = bf16[56,1792]{1,0:T(8,128)(2,1)S(1)} collective-permute-done((bf16[56,1792]{1,0:T(8,128)(2,1)}, bf16[56,1792]{1,0:T(8,128)(2,1)S(1)}, u32[]{:S(2)}, u32[]{:S(2)}) %collective-permute-start.25) | collective-permute-done | bytes 200736 | tf_op jit(solution)/shard_map/ppermute | solution.py:111
  603.4 16.0 %collective-permute-start.29 = (bf16[112,2432]{1,0:T(8,128)(2,1)S(1)}, bf16[112,2432]{1,0:T(8,128)(2,1)S(1)}, u32[]{:S(2)}, u32[]{:S(2)}) collective-permute-start(bf16[112,2432]{1,0:T(8,128)(2,1)S(1)} %fusion.32), channel_id=1, source_target_pairs={{0,16},{16,0},{1,17},{17,1},{2,18},{18,2},{3,19},{19,3},{4,20},{20... | collective-permute-start | bytes 1634312 | tf_op jit(solution)/shard_map/ppermute | solution.py:64
  621.2 5.5 collective-permute-done.29
  (330 shorter events, 211.7 us)
Async XLA Ops:
  7.2 110.7 %all-gather.4.cloned.1.call-start = ((), (), s32[]{:S(2)}) async-start(), calls=%async_computation.2 | async-start | bytes 18382848 | tf_op jit(solution)/shard_map/all_gather | solution.py:407
  9.0 10.5 %collective-permute-start.2 = (bf16[56,1792]{1,0:T(8,128)(2,1)}, bf16[56,1792]{1,0:T(8,128)(2,1)S(1)}, u32[]{:S(2)}, u32[]{:S(2)}) collective-permute-start(bf16[56,1792]{1,0:T(8,128)(2,1)} %dynamic-slice_bitcast_fusion.4), channel_id=1, source_target_pairs={{0,8},{1,9},{2,10},{3,11},{4,12},{5,13},{6,14},{7,15},{24,16},{25,... | collective-permute-start | bytes 602120 | tf_op jit(solution)/shard_map/ppermute | solution.py:156
  20.6 205.2 %all-gather.6.cloned.1.call-start = ((), (), s32[]{:S(2)}) async-start(), calls=%async_computation.5 | async-start | bytes 18522112 | tf_op jit(solution)/shard_map/all_gather | solution.py:407
  20.7 22.4 %collective-permute-start.4 = (bf16[152,1792]{1,0:T(8,128)(2,1)S(1)}, bf16[152,1792]{1,0:T(8,128)(2,1)S(1)}, u32[]{:S(2)}, u32[]{:S(2)}) collective-permute-start(bf16[152,1792]{1,0:T(8,128)(2,1)S(1)} %dynamic-slice_bitcast_fusion.3), channel_id=1, source_target_pairs={{0,8},{1,9},{2,10},{3,11},{4,12},{5,13},{6,14},{7,15},{24,16},{25,... | collective-permute-start | bytes 1634312 | tf_op jit(solution)/shard_map/ppermute | solution.py:156
  44.2 520.9 %reduce-scatter.5.cloned.1.call-start = ((), (), s32[]{:S(2)}) async-start(), calls=%async_computation.4 | async-start | bytes 9261056 | tf_op jit(solution)/shard_map/reduce_scatter | solution.py:604
  44.3 40.7 %collective-permute-start.1 = (bf16[2,128,1792]{2,1,0:T(8,128)(2,1)S(1)}, bf16[2,128,1792]{2,1,0:T(8,128)(2,1)S(1)}, u32[]{:S(2)}, u32[]{:S(2)}) collective-permute-start(bf16[2,128,1792]{2,1,0:T(8,128)(2,1)S(1)} %bitcast.385), channel_id=1, source_target_pairs={{0,16},{16,0},{1,17},{17,1},{2,18},{18,2},{3,19},{19,3},{4,20},{20... | collective-permute-start | bytes 2752520 | tf_op jit(solution)/shard_map/ppermute | solution.py:64
  64.6 20.4 %collective-permute-start = (s32[2,128]{1,0:T(2,128)S(1)}, s32[2,128]{1,0:T(2,128)S(1)}, u32[]{:S(2)}, u32[]{:S(2)}) collective-permute-start(s32[2,128]{1,0:T(2,128)S(1)} %bitcast.398), channel_id=1, source_target_pairs={{0,16},{16,0},{1,17},{17,1},{2,18},{18,2},{3,19},{19,3},{4,20},{20... | collective-permute-start | bytes 3080 | tf_op jit(solution)/shard_map/ppermute | solution.py:64
  136.4 33.4 %collective-permute-start.3 = (bf16[256,1792]{1,0:T(8,128)(2,1)S(1)}, bf16[256,1792]{1,0:T(8,128)(2,1)S(1)}, u32[]{:S(2)}, u32[]{:S(2)}) collective-permute-start(bf16[256,1792]{1,0:T(8,128)(2,1)S(1)} %convolution_convert_fusion.6), channel_id=1, source_target_pairs={{0,16},{16,0},{1,17},{17,1},{2,18},{18,2},{3,19},{19,3},{4,20},{20... | collective-permute-start | bytes 2752520 | tf_op jit(solution)/shard_map/ppermute | solution.py:64
  172.3 22.4 %collective-permute-start.5 = (bf16[256,1792]{1,0:T(8,128)(2,1)}, bf16[256,1792]{1,0:T(8,128)(2,1)}, u32[]{:S(2)}, u32[]{:S(2)}) collective-permute-start(bf16[256,1792]{1,0:T(8,128)(2,1)} %multiply_convert_fusion.6), channel_id=1, source_target_pairs={{0,16},{16,0},{1,17},{17,1},{2,18},{18,2},{3,19},{19,3},{4,20},{20... | collective-permute-start | bytes 2752520 | tf_op jit(solution)/shard_map/ppermute | solution.py:64
  256.6 22.6 %collective-permute-start.6 = (bf16[256,1792]{1,0:T(8,128)(2,1)S(1)}, bf16[256,1792]{1,0:T(8,128)(2,1)S(1)}, u32[]{:S(2)}, u32[]{:S(2)}) collective-permute-start(bf16[256,1792]{1,0:T(8,128)(2,1)S(1)} %convolution_convert_fusion.5), channel_id=1, source_target_pairs={{0,16},{16,0},{1,17},{17,1},{2,18},{18,2},{3,19},{19,3},{4,20},{20... | collective-permute-start | bytes 2752520 | tf_op jit(solution)/shard_map/ppermute | solution.py:64
  283.8 26.8 %collective-permute-start.12 = (bf16[256,1792]{1,0:T(8,128)(2,1)S(1)}, bf16[256,1792]{1,0:T(8,128)(2,1)S(1)}, u32[]{:S(2)}, u32[]{:S(2)}) collective-permute-start(bf16[256,1792]{1,0:T(8,128)(2,1)S(1)} %get-tuple-element.352), channel_id=1, source_target_pairs={{0,16},{16,0},{1,17},{17,1},{2,18},{18,2},{3,19},{19,3},{4,20},{20... | collective-permute-start | bytes 2752520 | tf_op jit(solution)/shard_map/ppermute | solution.py:64
  323.0 19.6 %collective-permute-start.13 = (bf16[2,2,2,152,1792]{4,3,2,1,0:T(8,128)(2,1)}, bf16[2,2,2,152,1792]{4,3,2,1,0:T(8,128)(2,1)}, u32[]{:S(2)}, u32[]{:S(2)}) collective-permute-start(bf16[2,2,2,152,1792]{4,3,2,1,0:T(8,128)(2,1)} %dynamic-slice_bitcast_fusion.1), channel_id=1, source_target_pairs={{0,1},{1,0},{2,3},{3,2},{4,5},{5,4},{6,7},{7,6},{8,9},{9,8},{10,11... | collective-permute-start | bytes 13074440 | tf_op jit(solution)/shard_map/ppermute | solution.py:111
  342.3 294.5 %reduce-scatter.3.cloned.1.call-start = ((), (), s32[]{:S(2)}) async-start(), calls=%async_computation.3 | async-start | bytes 4874240 | tf_op jit(solution)/shard_map/reduce_scatter | solution.py:667
  367.4 13.7 %collective-permute-start.15 = (bf16[2,2,2,112,2432]{4,3,2,1,0:T(8,128)(2,1)}, bf16[2,2,2,112,2432]{4,3,2,1,0:T(8,128)(2,1)}, u32[]{:S(2)}, u32[]{:S(2)}) collective-permute-start(bf16[2,2,2,112,2432]{4,3,2,1,0:T(8,128)(2,1)} %dynamic-slice_bitcast_fusion), channel_id=1, source_target_pairs={{0,1},{1,0},{2,3},{3,2},{4,5},{5,4},{6,7},{7,6},{8,9},{9,8},{10,11... | collective-permute-start | bytes 13074440 | tf_op jit(solution)/shard_map/ppermute | solution.py:111
  368.0 22.5 %collective-permute-start.16 = (bf16[256,1792]{1,0:T(8,128)(2,1)}, bf16[256,1792]{1,0:T(8,128)(2,1)S(1)}, u32[]{:S(2)}, u32[]{:S(2)}) collective-permute-start(bf16[256,1792]{1,0:T(8,128)(2,1)} %fusion.6), channel_id=1, source_target_pairs={{0,16},{16,0},{1,17},{17,1},{2,18},{18,2},{3,19},{19,3},{4,20},{20... | collective-permute-start | bytes 2752520 | tf_op jit(solution)/shard_map/ppermute | solution.py:64
  368.5 73.3 %collective-permute-start.14 = (bf16[2,2,152,1792]{3,2,1,0:T(8,128)(2,1)}, bf16[2,2,152,1792]{3,2,1,0:T(8,128)(2,1)}, u32[]{:S(2)}, u32[]{:S(2)}) collective-permute-start(bf16[2,2,152,1792]{3,2,1,0:T(8,128)(2,1)} %fusion.1), channel_id=1, source_target_pairs={{0,2},{1,3},{2,0},{3,1},{4,6},{5,7},{6,4},{7,5},{8,10},{9,11},{10,... | collective-permute-start | bytes 6537224 | tf_op jit(solution)/shard_map/ppermute | solution.py:111
  393.8 21.5 %collective-permute-start.17 = (bf16[256,1792]{1,0:T(8,128)(2,1)S(1)}, bf16[256,1792]{1,0:T(8,128)(2,1)S(1)}, u32[]{:S(2)}, u32[]{:S(2)}) collective-permute-start(bf16[256,1792]{1,0:T(8,128)(2,1)S(1)} %get-tuple-element.178), channel_id=1, source_target_pairs={{0,16},{16,0},{1,17},{17,1},{2,18},{18,2},{3,19},{19,3},{4,20},{20... | collective-permute-start | bytes 2752520 | tf_op jit(solution)/shard_map/ppermute | solution.py:64
  420.1 27.3 %collective-permute-start.20 = (bf16[2,2,2,56,1792]{4,3,2,1,0:T(8,128)(2,1)}, bf16[2,2,2,56,1792]{4,3,2,1,0:T(8,128)(2,1)S(1)}, u32[]{:S(2)}, u32[]{:S(2)}) collective-permute-start(bf16[2,2,2,56,1792]{4,3,2,1,0:T(8,128)(2,1)} %dynamic-slice_bitcast_fusion.2), channel_id=1, source_target_pairs={{0,1},{1,0},{2,3},{3,2},{4,5},{5,4},{6,7},{7,6},{8,9},{9,8},{10,11... | collective-permute-start | bytes 4816904 | tf_op jit(solution)/shard_map/ppermute | solution.py:111
  420.2 74.8 %collective-permute-start.19 = (bf16[2,2,112,2432]{3,2,1,0:T(8,128)(2,1)}, bf16[2,2,112,2432]{3,2,1,0:T(8,128)(2,1)}, u32[]{:S(2)}, u32[]{:S(2)}) collective-permute-start(bf16[2,2,112,2432]{3,2,1,0:T(8,128)(2,1)} %fusion), channel_id=1, source_target_pairs={{0,2},{1,3},{2,0},{3,1},{4,6},{5,7},{6,4},{7,5},{8,10},{9,11},{10,... | collective-permute-start | bytes 6537224 | tf_op jit(solution)/shard_map/ppermute | solution.py:111
  445.1 59.7 %collective-permute-start.18 = (bf16[2,152,1792]{2,1,0:T(8,128)(2,1)}, bf16[2,152,1792]{2,1,0:T(8,128)(2,1)}, u32[]{:S(2)}, u32[]{:S(2)}) collective-permute-start(bf16[2,152,1792]{2,1,0:T(8,128)(2,1)} %fusion.14), channel_id=1, source_target_pairs={{0,4},{1,5},{2,6},{3,7},{4,0},{5,1},{6,2},{7,3},{8,12},{9,13},{10,... | collective-permute-start | bytes 3268616 | tf_op jit(solution)/shard_map/ppermute | solution.py:111
  467.8 43.1 %collective-permute-start.22 = (bf16[2,2,56,1792]{3,2,1,0:T(8,128)(2,1)}, bf16[2,2,56,1792]{3,2,1,0:T(8,128)(2,1)}, u32[]{:S(2)}, u32[]{:S(2)}) collective-permute-start(bf16[2,2,56,1792]{3,2,1,0:T(8,128)(2,1)} %fusion.28), channel_id=1, source_target_pairs={{0,2},{1,3},{2,0},{3,1},{4,6},{5,7},{6,4},{7,5},{8,10},{9,11},{10,... | collective-permute-start | bytes 2408456 | tf_op jit(solution)/shard_map/ppermute | solution.py:111
  470.7 29.1 %collective-permute-start.21 = (bf16[256,1792]{1,0:T(8,128)(2,1)}, bf16[256,1792]{1,0:T(8,128)(2,1)}, u32[]{:S(2)}, u32[]{:S(2)}) collective-permute-start(bf16[256,1792]{1,0:T(8,128)(2,1)} %get-tuple-element.207), channel_id=1, source_target_pairs={{0,16},{16,0},{1,17},{17,1},{2,18},{18,2},{3,19},{19,3},{4,20},{20... | collective-permute-start | bytes 2752520 | tf_op jit(solution)/shard_map/ppermute | solution.py:64
  498.2 50.1 %collective-permute-start.24 = (bf16[2,112,2432]{2,1,0:T(8,128)(2,1)}, bf16[2,112,2432]{2,1,0:T(8,128)(2,1)}, u32[]{:S(2)}, u32[]{:S(2)}) collective-permute-start(bf16[2,112,2432]{2,1,0:T(8,128)(2,1)} %fusion.13), channel_id=1, source_target_pairs={{0,4},{1,5},{2,6},{3,7},{4,0},{5,1},{6,2},{7,3},{8,12},{9,13},{10,... | collective-permute-start | bytes 3268616 | tf_op jit(solution)/shard_map/ppermute | solution.py:111
  512.3 47.4 %collective-permute-start.23 = (bf16[2,56,1792]{2,1,0:T(8,128)(2,1)S(1)}, bf16[2,56,1792]{2,1,0:T(8,128)(2,1)S(1)}, u32[]{:S(2)}, u32[]{:S(2)}) collective-permute-start(bf16[2,56,1792]{2,1,0:T(8,128)(2,1)S(1)} %fusion.37), channel_id=1, source_target_pairs={{0,4},{1,5},{2,6},{3,7},{4,0},{5,1},{6,2},{7,3},{8,12},{9,13},{10,... | collective-permute-start | bytes 1204232 | tf_op jit(solution)/shard_map/ppermute | solution.py:111
  515.1 50.0 %collective-permute-start.27 = (bf16[152,1792]{1,0:T(8,128)(2,1)S(1)}, bf16[152,1792]{1,0:T(8,128)(2,1)}, u32[]{:S(2)}, u32[]{:S(2)}) collective-permute-start(bf16[152,1792]{1,0:T(8,128)(2,1)S(1)} %fusion.34), channel_id=1, source_target_pairs={{0,8},{1,9},{2,10},{3,11},{4,12},{5,13},{6,14},{7,15},{8,0},{9,1},... | collective-permute-start | bytes 1634312 | tf_op jit(solution)/shard_map/ppermute | solution.py:111
  551.0 39.5 %collective-permute-start.26 = (bf16[112,2432]{1,0:T(8,128)(2,1)}, bf16[112,2432]{1,0:T(8,128)(2,1)S(1)}, u32[]{:S(2)}, u32[]{:S(2)}) collective-permute-start(bf16[112,2432]{1,0:T(8,128)(2,1)} %fusion.33), channel_id=1, source_target_pairs={{0,8},{1,9},{2,10},{3,11},{4,12},{5,13},{6,14},{7,15},{8,0},{9,1},... | collective-permute-start | bytes 1634312 | tf_op jit(solution)/shard_map/ppermute | solution.py:111
  562.3 41.1 %collective-permute-start.25 = (bf16[56,1792]{1,0:T(8,128)(2,1)}, bf16[56,1792]{1,0:T(8,128)(2,1)S(1)}, u32[]{:S(2)}, u32[]{:S(2)}) collective-permute-start(bf16[56,1792]{1,0:T(8,128)(2,1)} %fusion.45), channel_id=1, source_target_pairs={{0,8},{1,9},{2,10},{3,11},{4,12},{5,13},{6,14},{7,15},{8,0},{9,1},... | collective-permute-start | bytes 602120 | tf_op jit(solution)/shard_map/ppermute | solution.py:111
  567.2 53.4 %collective-permute-start.30 = (bf16[152,1792]{1,0:T(8,128)(2,1)S(1)}, bf16[152,1792]{1,0:T(8,128)(2,1)S(1)}, u32[]{:S(2)}, u32[]{:S(2)}) collective-permute-start(bf16[152,1792]{1,0:T(8,128)(2,1)S(1)} %fusion.30), channel_id=1, source_target_pairs={{0,16},{16,0},{1,17},{17,1},{2,18},{18,2},{3,19},{19,3},{4,20},{20... | collective-permute-start | bytes 1634312 | tf_op jit(solution)/shard_map/ppermute | solution.py:64
  567.5 53.2 %collective-permute-start.31 = (bf16[112,2432]{1,0:T(8,128)(2,1)S(1)}, bf16[112,2432]{1,0:T(8,128)(2,1)S(1)}, u32[]{:S(2)}, u32[]{:S(2)}) collective-permute-start(bf16[112,2432]{1,0:T(8,128)(2,1)S(1)} %copy-done.35), channel_id=1, source_target_pairs={{0,16},{16,0},{1,17},{17,1},{2,18},{18,2},{3,19},{19,3},{4,20},{20... | collective-permute-start | bytes 1634312 | tf_op jit(solution)/shard_map/ppermute | solution.py:64
  603.4 23.4 %collective-permute-start.29 = (bf16[112,2432]{1,0:T(8,128)(2,1)S(1)}, bf16[112,2432]{1,0:T(8,128)(2,1)S(1)}, u32[]{:S(2)}, u32[]{:S(2)}) collective-permute-start(bf16[112,2432]{1,0:T(8,128)(2,1)S(1)} %fusion.32), channel_id=1, source_target_pairs={{0,16},{16,0},{1,17},{17,1},{2,18},{18,2},{3,19},{19,3},{4,20},{20... | collective-permute-start | bytes 1634312 | tf_op jit(solution)/shard_map/ppermute | solution.py:64
  620.5 8.4 %collective-permute-start.28 = (bf16[56,1792]{1,0:T(8,128)(2,1)S(1)}, bf16[56,1792]{1,0:T(8,128)(2,1)S(1)}, u32[]{:S(2)}, u32[]{:S(2)}) collective-permute-start(bf16[56,1792]{1,0:T(8,128)(2,1)S(1)} %fusion.47), channel_id=1, source_target_pairs={{0,16},{16,0},{1,17},{17,1},{2,18},{18,2},{3,19},{19,3},{4,20},{20... | collective-permute-start | bytes 602120 | tf_op jit(solution)/shard_map/ppermute | solution.py:64
  621.2 15.6 %collective-permute-start.34 = (bf16[152,1792]{1,0:T(8,128)(2,1)S(1)}, bf16[152,1792]{1,0:T(8,128)(2,1)S(1)}, u32[]{:S(2)}, u32[]{:S(2)}) collective-permute-start(bf16[152,1792]{1,0:T(8,128)(2,1)S(1)} %get-tuple-element.356), channel_id=1, source_target_pairs={{0,8},{1,9},{2,10},{3,11},{4,12},{5,13},{6,14},{7,15},{8,0},{9,1},... | collective-permute-start | bytes 1634312 | tf_op jit(solution)/shard_map/ppermute | solution.py:185
  (75 other events, 891.5 us)
Sparse Core Ops, SparseCore 0:
  20.7 97.1 all-gather.3
  120.0 105.6 all-gather.5
  342.4 142.4 reduce-scatter.4
  499.9 119.6 reduce-scatter.2

commit v3 on v2

--- a/solution.py
+++ b/solution.py
@@ -187,12 +187,11 @@
     return shard.reshape(-1, part.shape[1]).astype(F32)
 
 
-def sum_everywhere(place, value):
-    for axis, count in (("fsdp", place.fsdp), ("seq", place.seqs)):
-        bit = 1
-        while bit < count:
-            value = value + lax.ppermute(value, axis, [(i, i ^ bit) for i in range(count)])
-            bit *= 2
+def sum_over(axis, count, value):
+    bit = 1
+    while bit < count:
+        value = value + lax.ppermute(value, axis, [(i, i ^ bit) for i in range(count)])
+        bit *= 2
     return value
 
 
@@ -389,6 +388,56 @@
     )(y.reshape(1), qkv, dmixed, taps, segments[:, :, None], segments[:, None, :])
 
 
+def copy_kernel(source_ref, out_ref):
+    out_ref[...] = source_ref[...]
+
+
+def take_tiles(whole, part, parts, order):
+    shards, tiles = whole.shape[0], whole.shape[1] // parts
+    return pl.pallas_call(
+        copy_kernel,
+        grid=(shards,),
+        out_shape=jax.ShapeDtypeStruct((shards, tiles, 8, 128), whole.dtype),
+        in_specs=[pl.BlockSpec((1, tiles, 8, 128), lambda i: (order(i), part, 0, 0))],
+        out_specs=pl.BlockSpec((1, tiles, 8, 128), lambda i: (i, 0, 0, 0)),
+        compiler_params=pltpu.CompilerParams(vmem_limit_bytes=48 * 2**20),
+    )(whole)
+
+
+def up_kernel(rows_ref, tiles_ref, gate_ref, up_ref, hidden_ref):
+    count = tiles_ref.shape[2]
+    depth = rows_ref.shape[1]
+    weight = jnp.concatenate(
+        [tiles_ref[:, :, i].reshape(depth, 128) for i in range(count)], axis=1
+    )
+    up = dot(rows_ref[...], weight)
+    gate = gate_ref[...]
+    up_ref[...] = up
+    hidden_ref[...] = (gate * sigmoid(gate) * up).astype(BF16)
+
+
+def up_hidden(rows, whole, shape, gate, count=5):
+    row_tiles, columns = shape[0] // 8, shape[1]
+    tiles = whole.reshape(whole.shape[0], 2 * row_tiles, columns // 128, 8, 128)
+    block = (whole.shape[0], row_tiles, count, 8, 128)
+    wide = pl.BlockSpec((rows.shape[0], count * 128), lambda j: (0, j))
+    return pl.pallas_call(
+        up_kernel,
+        grid=(-(-columns // (count * 128)),),
+        out_shape=(
+            jax.ShapeDtypeStruct((rows.shape[0], columns), F32),
+            jax.ShapeDtypeStruct((rows.shape[0], columns), BF16),
+        ),
+        in_specs=[
+            pl.BlockSpec(rows.shape, lambda j: (0, 0)),
+            pl.BlockSpec(block, lambda j: (0, 0, j, 0, 0)),
+            wide,
+        ],
+        out_specs=(wide, wide),
+        compiler_params=pltpu.CompilerParams(vmem_limit_bytes=48 * 2**20),
+    )(rows, tiles, gate)
+
+
 class Gather:
     def __init__(self, arrays):
         self.shapes = [a.shape for a in arrays]
@@ -531,6 +580,7 @@
 
     packed_own = packed_k[0].astype(F32)
     own, got = scatter(project(pieces(mixed), out_w))
+    own, *got = fence(own, *got)
     resid = packed_own + own
     for part in got:
         resid = resid + part.astype(F32)
@@ -538,12 +588,29 @@
     n_two_k = gather_seq(place, (resid * root_two * gain_two).astype(BF16))
     gate_k = [dot(n, gate_w) for n in n_two_k]
     gate_k = list(late.after(*gate_k))
-    up_w, down_w = late.arrays()
-    down_w = plane_rows(place, down_w)
-    up_k = [dot(n, up_w) for n in n_two_k]
+    whole = late.raw[0]
+    direct = late.joined and whole.shape[1] == 2 * late.shapes[0][0] * late.shapes[0][1] // 1024
+    up_k, hidden_k = [None] * seqs, [None] * seqs
+    if direct:
+        for k in list(range(1, seqs)) + [0]:
+            up_k[k], hidden_k[k] = up_hidden(n_two_k[k], whole, late.shapes[0], gate_k[k])
+        per = place.fsdp // seqs
+        tiles = take_tiles(whole, 1, 2, lambda i: (i % seqs) * per + i // seqs)
+        rows_down, columns_down = late.shapes[1]
+        tiles = tiles.reshape(-1, rows_down // 8, columns_down // 128, 8, 128)
+        down_w = jnp.swapaxes(tiles, 2, 3).reshape(-1, columns_down)
+    else:
+        up_w, down_w = late.arrays()
+        down_w = plane_rows(place, down_w)
+        for k in range(seqs):
+            up_k[k] = dot(n_two_k[k], up_w)
+            hidden_k[k] = (gate_k[k] * jax.nn.sigmoid(gate_k[k]) * up_k[k]).astype(BF16)
     sig_k = [jax.nn.sigmoid(g) for g in gate_k]
-    hidden_k = [(g * s * u).astype(BF16) for g, s, u in zip(gate_k, sig_k, up_k)]
     own, got = scatter(project(hidden_k, down_w))
+    if direct:
+        late.raw[0], own = fence(late.raw[0], own)
+        up_w, _ = late.arrays()
+    own, up_w, *got = fence(own, up_w, *got)
     result = resid + own
     for part in got:
         result = result + part.astype(F32)
@@ -551,7 +618,7 @@
     d_result = scale * error
     d_low = d_result.astype(BF16)
     d_low_k = gather_seq(place, d_low)
-    squares = sum_everywhere(place, jnp.sum(error * error, axis=(0, 1), keepdims=True))
+    squares = sum_over("fsdp", place.fsdp, jnp.sum(error * error, axis=(0, 1), keepdims=True))
 
     def to_given(value):
         value = value.astype(BF16).reshape(micro, rows_dev, model)
@@ -633,7 +700,8 @@
     dm_k = gather_seq(place, dm_own)
     dm_own, = up.start(dm_own)
     d_mixed_own = dot(dm_own, out_w, ((1,), (1,)))
-    d_mixed_own, *dm_others = place.in_turn(d_mixed_own, *dm_k[1:])
+    squares = sum_over("seq", seqs, squares)
+    d_mixed_own, squares, *dm_others = place.in_turn(d_mixed_own, squares, *dm_k[1:])
     out = by_rows(weight_grad(mixed, jnp.concatenate([dm_own, *dm_others])), x_first)
     dm_others = out.start(*dm_others)
     d_mixed = jnp.concatenate(
@@ -665,8 +733,6 @@
     grad_first = (dot(n_one, d_qkv, ((0,), (0,))) + extra).astype(BF16)
     grad_first, own = fence(grad_first, own)
     first_sum = lax.psum_scatter(grad_first, "fsdp", scatter_dimension=0, tiled=True)
-    own, = up.after(own)
-    own, = up.start(own)
     own, *got = place.in_turn(own, *got)
 
     d_n_one = own
@@ -682,36 +748,36 @@
     def join(parts):
         return jnp.concatenate(parts, axis=1).astype(F32)
 
-    def all_pieces(value):
-        return in_order(place, gather_seq(place, value))
-
+    d_packed, = up.after(d_packed)
+    d_packed, = up.start(d_packed)
+    d_packed, gate_sum = place.in_turn(d_packed, gate_sum)
+    gate_k = gather_seq(place, gate_sum)
     input_grad = to_given(d_packed)
-    input_grad, = down.after(input_grad)
-    input_grad, = down.start(input_grad)
+    down.after()
+    down.start()
     out.after()
     out.start()
     up.after()
     up.start()
+    down.after()
+    down_k = unspread_start(place, down.result())
+    gate_k = place.in_turn(*gate_k)
+    grad_gate = join(in_order(place, gate_k))
     out.after()
     out.start()
-    gate_sum, = place.in_turn(gate_sum)
-    gate_k = gather_seq(place, gate_sum)
-    down.after()
-    down_k = unspread_start(place, down.result())
+    down_k = place.in_turn(*down_k)
+    grad_down = unspread_end(place, down_k)
     up.after()
     up_k = gather_seq(place, up.result())
     out.after()
     out_k = unspread_start(place, out.result())
-    gate_k = place.in_turn(*gate_k)
-    grad_gate = join(in_order(place, gate_k))
-    down_k = place.in_turn(*down_k)
-    grad_down = unspread_end(place, down_k)
+    first_sum, = place.in_turn(first_sum)
+    first_k = gather_seq(place, first_sum)
+    out_k = place.in_turn(*out_k)
+    grad_out = unspread_end(place, out_k)
     up_k = place.in_turn(*up_k)
     grad_up = join(in_order(place, up_k))
-    out_k = place.in_turn(*out_k)
-    grad_out = unspread_end(place, out_k)
-    first_sum, = place.in_turn(first_sum)
-    first_parts = all_pieces(first_sum)
+    first_parts = in_order(place, first_k)
     loss = (squares[0, 0] + place.turn[0, 0]) / (total * model)
     extra_sum = sum(part[:, qkv_width:].astype(F32) for part in first_parts)
     return (

time: 661 us -> 649 us (0.982)
  Pallas kernels: 15.3 us -> 41.6 us
  starting transfers between devices: 102 us -> 80.3 us
  matrix products: 125 us -> 112 us
  local copies, waits for them, and re-layouts: 59.5 us -> 50.7 us
    pallas_call x0 -> x3, Pallas kernels: none -> 26.3 us  [the longest x2 14.2 us: up_hidden(): pl.pallas_call(up_kernel, grid=(-(-columns // (count * 128)),), out_shape...]
    ppermute x14, waiting for transfers between devices: 91.6 us -> 70.5 us  [seq_send(): return lax.ppermute(value, 'seq', pairs)]
    ppermute x14, starting transfers between devices: 60.5 us -> 46 us  [seq_send(): return lax.ppermute(value, 'seq', pairs)]
    dot_general x24 -> x22, matrix products: 120 us -> 106 us  [dot(): lax.dot_general(left, right, (dims, ((), ())), preferred_element_type=F32)]
    ppermute x2, waiting for transfers between devices: 3.38 us -> 14.3 us  [unspread_end(): got = lax.ppermute(sent, 'fsdp', pairs)]
    transpose x2 -> x1, local copies, waits for them, and re-layouts: 9.39 us -> 0.21 us  [plane_rows(): return jnp.swapaxes(blocks, 0, 1).reshape(rows, columns)]
    ppermute x12, starting transfers between devices: 18.8 us -> 11.3 us  [send(): got = lax.ppermute(sent, 'fsdp', pairs)]
    unnamed x137 -> x141, local copies, waits for them, and re-layouts: 10.8 us -> 16.5 us
  transfers between devices with their start and end apart: 39 -> 39, of which waited for: 25 -> 23; matrix products, arithmetic and copies ran while one was open for 27% -> 28% of each run, Pallas kernels for 2% -> 3%
where the time goes in v3:
time: 649 us; the launch traced here: 640 us
  waiting for transfers between devices  275 us (42%)
  matrix products  112 us (17%)
  starting transfers between devices  80.3 us (12%)
  other arithmetic  58.5 us (9%)
  local copies, waits for them, and re-layouts  50.7 us (8%)
  Pallas kernels  41.6 us (6%)
  between operations  21.7 us (3%)
    ppermute x12, waiting for transfers between devices, send(): got = lax.ppermute(sent, 'fsdp', pairs)  110 us
    dot_general x22, matrix products, dot(): lax.dot_general(left, right, (dims, ((), ())), preferred_element_type=F32)  106 us
    ppermute x14, waiting for transfers between devices, seq_send(): return lax.ppermute(value, 'seq', pairs)  70.5 us
    all_gather x2, waiting for transfers between devices, __init__(): self.raw = [lax.all_gather(buffer, 'fsdp', axis=0, tiled=False)]  58.8 us
    ppermute x14, starting transfers between devices, seq_send(): return lax.ppermute(value, 'seq', pairs)  46 us
    convert_element_type x12, other arithmetic, total(): return total.astype(BF16)  28.5 us
    slice x5, local copies, waits for them, and re-layouts, arrays(): t = self.raw[0][:, at:at + count]  19.7 us
    ppermute x2, waiting for transfers between devices, spread_rows(): got = lax.ppermute(sent, ('seq', 'fsdp'), plane_pairs(place, k))  17.4 us
  transfers between devices with their start and end apart: 39, of which 23 were waited for; matrix products, arithmetic and copies ran while one was open for 28% of the time, Pallas kernels for 3%

profile of v3, /device:TPU:0, one launch (start us, length us, event | category | flops | bytes accessed | tf_op | source)
XLA Modules:
  0.0 640.2 jit_solution(7034908049316578690)
XLA Ops:
  9.0 5.9 collective-permute-start.2
  27.1 16.0 %collective-permute-done.4 = bf16[152,1792]{1,0:T(8,128)(2,1)S(1)} collective-permute-done((bf16[152,1792]{1,0:T(8,128)(2,1)S(1)}, bf16[152,1792]{1,0:T(8,128)(2,1)S(1)}, u32[]{:S(2)}, u32[]{:S(2)}) %collective-permute-start.4) | collective-permute-done | bytes 544800 | tf_op jit(solution)/shard_map/ppermute | solution.py:156
  44.6 20.2 %collective-permute-start.1 = (bf16[2,128,1792]{2,1,0:T(8,128)(2,1)S(1)}, bf16[2,128,1792]{2,1,0:T(8,128)(2,1)}, u32[]{:S(2)}, u32[]{:S(2)}) collective-permute-start(bf16[2,128,1792]{2,1,0:T(8,128)(2,1)S(1)} %bitcast.373), channel_id=1, source_target_pairs={{0,16},{16,0},{1,17},{17,1},{2,18},{18,2},{3,19},{19,3},{4,20},{20... | collective-permute-start | bytes 2752520 | tf_op jit(solution)/shard_map/ppermute | solution.py:64
  65.8 19.5 %collective-permute-done = s32[2,128]{1,0:T(2,128)S(1)} collective-permute-done((s32[2,128]{1,0:T(2,128)S(1)}, s32[2,128]{1,0:T(2,128)S(1)}, u32[]{:S(2)}, u32[]{:S(2)}) %collective-permute-start) | collective-permute-done | bytes 1056 | tf_op jit(solution)/shard_map/ppermute | solution.py:64
  87.5 30.4 %all-gather.4.cloned.1.call-done = bf16[16,528,8,128]{3,2,1,0:T(8,128)(2,1)} async-done(((bf16[1,528,8,128]{3,2,1,0:T(8,128)(2,1)}), bf16[16,528,8,128]{3,2,1,0:T(8,128)(2,1)}) %all-gather.4.cloned.1.call-update) | async-done | bytes 17301520 | tf_op jit(solution)/shard_map/all_gather | solution.py:456
  135.8 12.6 %collective-permute-start.3 = (bf16[256,1792]{1,0:T(8,128)(2,1)S(1)}, bf16[256,1792]{1,0:T(8,128)(2,1)S(1)}, u32[]{:S(2)}, u32[]{:S(2)}) collective-permute-start(bf16[256,1792]{1,0:T(8,128)(2,1)S(1)} %convolution_convert_fusion.6), channel_id=1, source_target_pairs={{0,16},{16,0},{1,17},{17,1},{2,18},{18,2},{3,19},{19,3},{4,20},{20... | collective-permute-start | bytes 2752520 | tf_op jit(solution)/shard_map/ppermute | solution.py:64
  150.9 18.3 %collective-permute-done.3 = bf16[256,1792]{1,0:T(8,128)(2,1)S(1)} collective-permute-done((bf16[256,1792]{1,0:T(8,128)(2,1)S(1)}, bf16[256,1792]{1,0:T(8,128)(2,1)S(1)}, u32[]{:S(2)}, u32[]{:S(2)}) %collective-permute-start.3) | collective-permute-done | bytes 917536 | tf_op jit(solution)/shard_map/ppermute | solution.py:64
  173.0 7.6 %slice.146 = bf16[16,266,8,128]{3,2,1,0:T(8,128)(2,1)} slice(bf16[16,528,8,128]{3,2,1,0:T(8,128)(2,1)} %all-gather.4.cloned.1.call-done), slice={[0:16], [140:406], [0:8], [0:128]} | slice | bytes 17432576 | tf_op jit(solution)/shard_map/slice | solution.py:471
  180.6 7.9 %fusion.77.gate_ref = f32[256,2432]{1,0:T(8,128)} fusion(bf16[256,1792]{1,0:T(8,128)(2,1)S(1)} %multiply_convert_fusion.4.rows_ref, bf16[1792,2432]{1,0:T(8,128)(2,1)} %bitcast.338), kind=kOutput, calls=%fused_computation.212 | convolution fusion | flops 2231369728 | bytes 12124160 | tf_op jit(solution)/shard_map/dot_general | solution.py:23
  197.3 28.4 %all-gather.6.cloned.1.call-done = bf16[8512,8,128]{2,1,0:T(8,128)(2,1)} async-done(((bf16[532,8,128]{2,1,0:T(8,128)(2,1)}), bf16[8512,8,128]{2,1,0:T(8,128)(2,1)}) %all-gather.6.cloned.1.call-update) | async-done | bytes 17432592 | tf_op jit(solution)/shard_map/all_gather | solution.py:456
  225.7 12.0 %shard_map.248 = bf16[16,266,8,128]{3,2,1,0:T(8,128)(2,1)} custom-call(bf16[16,532,8,128]{3,2,1,0:T(8,128)(2,1)} %bitcast.312), custom_call_target="tpu_custom_call" | custom-call | tf_op jit(solution)/shard_map/pallas_call | solution.py:397
  237.8 7.2 %shard_map.249 = (f32[256,2432]{1,0:T(8,128)S(1)}, bf16[256,2432]{1,0:T(8,128)(2,1)S(1)}) custom-call(bf16[256,1792]{1,0:T(8,128)(2,1)S(1)} %collective-permute-done.5.rows_ref, bf16[16,28,19,8,128]{4,3,2,1,0:T(8,128)(2,1)} %bitcast.313, f32[256,2432]{1,0:T(8,128)} %fusion.78.gate_ref), custom_call_target="tpu_custom_call" | custom-call | tf_op jit(solution)/shard_map/pallas_call | solution.py:424
  252.9 7.0 %shard_map.247 = (f32[256,2432]{1,0:T(8,128)S(1)}, bf16[256,2432]{1,0:T(8,128)(2,1)S(1)}) custom-call(bf16[256,1792]{1,0:T(8,128)(2,1)S(1)} %multiply_convert_fusion.4.rows_ref, bf16[16,28,19,8,128]{4,3,2,1,0:T(8,128)(2,1)} %bitcast.314, f32[256,2432]{1,0:T(8,128)} %fusion.77.gate_ref), custom_call_target="tpu_custom_call" | custom-call | tf_op jit(solution)/shard_map/pallas_call | solution.py:424
  261.4 7.3 %fusion.79 = f32[256,1792]{1,0:T(8,128)} fusion(bf16[256,2432]{1,0:T(8,128)(2,1)S(1)} %get-tuple-element.150, bf16[2432,1792]{1,0:T(8,128)(2,1)} %bitcast.324), kind=kOutput, calls=%fused_computation.214 | convolution fusion | flops 2231369728 | bytes 11796480 | tf_op jit(solution)/shard_map/dot_general | solution.py:23
  268.6 7.5 %slice.115 = bf16[16,266,8,128]{3,2,1,0:T(8,128)(2,1)} slice(bf16[16,532,8,128]{3,2,1,0:T(8,128)(2,1)} %bitcast.315), slice={[0:16], [0:266], [0:8], [0:128]} | slice | bytes 17432576 | tf_op jit(solution)/shard_map/slice | solution.py:471
  283.3 8.0 %multiply_convert_fusion.2 = (bf16[256,2432]{1,0:T(8,128)(2,1)}, bf16[256,2432]{1,0:T(8,128)(2,1)}) fusion(f32[256,2432]{1,0:T(8,128)S(1)} %copy-done.35, f32[256,2432]{1,0:T(8,128)S(1)} %copy-done.9, bf16[256,1792]{1,0:T(8,128)(2,1)S(1)} %multiply_convert_fusion.5, bf16[2432,1792]{1,0:T(8,128)(2,1)} %bitcast.325), kind=kOutput, calls=%fused_computation.36 | convolution fusion | flops 2239463424 | bytes 17104896 | tf_op jit(solution)/shard_map/dot_general | solution.py:23
  306.1 5.8 convolution_convert_fusion.2
  316.7 6.5 %fusion.80 = f32[256,2432]{1,0:T(8,128)S(1)} fusion(bf16[256,1792]{1,0:T(8,128)(2,1)} %copy-done.56, bf16[2432,1792]{1,0:T(8,128)(2,1)} %bitcast.326), kind=kOutput, calls=%fused_computation.215 | convolution fusion | flops 2231369728 | bytes 12124160 | tf_op jit(solution)/shard_map/dot_general | solution.py:23
  327.0 7.2 %convolution_convert_fusion.1 = bf16[1792,2432]{1,0:T(8,128)(2,1)} fusion(bf16[256,2432]{1,0:T(8,128)(2,1)S(1)} %get-tuple-element.175, bf16[256,2432]{1,0:T(8,128)(2,1)S(1)} %copy-done.59, bf16[256,1792]{1,0:T(8,128)(2,1)S(1)} %collective-permute-done.5.rows_ref, bf16[256,1792]{1,0:T(8,128)(2,1)S(1)} %multiply_convert_fusion.4.rows_ref), kind=kOutput, calls=%fused_computation.1 | convolution fusion | flops 4475748352 | bytes 13041664 | tf_op jit(solution)/shard_map/dot_general | solution.py:23
  338.6 6.8 %fusion.81 = f32[256,1792]{1,0:T(8,128)S(1)} fusion(bf16[256,2432]{1,0:T(8,128)(2,1)S(1)} %copy-done.39, bf16[1792,2432]{1,0:T(8,128)(2,1)} %bitcast.339), kind=kOutput, calls=%fused_computation.216 | convolution fusion | flops 2231369728 | bytes 11796480 | tf_op jit(solution)/shard_map/dot_general | solution.py:23
  349.0 7.5 %convolution_convert_fusion = bf16[1792,2432]{1,0:T(8,128)(2,1)S(1)} fusion(bf16[512,2432]{1,0:T(8,128)(2,1)} %pad_maximum_fusion, bf16[256,1792]{1,0:T(8,128)(2,1)S(1)} %collective-permute-done.5.rows_ref, bf16[256,1792]{1,0:T(8,128)(2,1)S(1)} %multiply_convert_fusion.4.rows_ref), kind=kOutput, calls=%fused_computation | convolution fusion | flops 4470767616 | bytes 13041664 | tf_op jit(solution)/shard_map/dot_general | solution.py:23
  369.7 6.6 %convolution_add_fusion = f32[256,1792]{1,0:T(8,128)S(1)} fusion(f32[256,1792]{1,0:T(8,128)} %fusion.82, bf16[256,2432]{1,0:T(8,128)(2,1)S(1)} %copy-done.37, bf16[1792,2432]{1,0:T(8,128)(2,1)} %bitcast.344), kind=kOutput, calls=%fused_computation.21 | convolution fusion | flops 2231828480 | bytes 13631488 | tf_op jit(solution)/shard_map/dot_general | solution.py:23
  376.3 8.6 %collective-permute-done.14 = bf16[256,1792]{1,0:T(8,128)(2,1)S(1)} collective-permute-done((bf16[256,1792]{1,0:T(8,128)(2,1)S(1)}, bf16[256,1792]{1,0:T(8,128)(2,1)S(1)}, u32[]{:S(2)}, u32[]{:S(2)}) %collective-permute-start.14) | collective-permute-done | bytes 917536 | tf_op jit(solution)/shard_map/ppermute | solution.py:64
  393.0 13.9 %collective-permute-done.17 = bf16[256,1792]{1,0:T(8,128)(2,1)S(1)} collective-permute-done((bf16[256,1792]{1,0:T(8,128)(2,1)S(1)}, bf16[256,1792]{1,0:T(8,128)(2,1)S(1)}, u32[]{:S(2)}, u32[]{:S(2)}) %collective-permute-start.17) | collective-permute-done | bytes 917536 | tf_op jit(solution)/shard_map/ppermute | solution.py:64
  418.8 21.6 %collective-permute-done.19 = bf16[2,2,152,1792]{3,2,1,0:T(8,128)(2,1)} collective-permute-done((bf16[2,2,152,1792]{3,2,1,0:T(8,128)(2,1)}, bf16[2,2,152,1792]{3,2,1,0:T(8,128)(2,1)}, u32[]{:S(2)}, u32[]{:S(2)}) %collective-permute-start.19) | collective-permute-done | bytes 2179104 | tf_op jit(solution)/shard_map/ppermute | solution.py:111
  447.7 11.7 %shard_map.250 = (bf16[2,2,128,1280]{3,2,1,0:T(8,128)(2,1)}, f32[2,8,896]{2,1,0:T(8,128)}) custom-call(s32[1]{0:T(128)} %bitcast.3.y_ref, bf16[2,2,128,1280]{3,2,1,0:T(8,128)(2,1)} %bitcast.310, f32[2,2,128,896]{3,2,1,0:T(8,128)} %bitcast.348, f32[8,896]{1,0:T(8,128)} %copy-done.6, s32[2,256,1]{2,1,0:T(8,128)} %copy-done.5, s32[2,1,256]{2,1,0:T(1,128)} %copy-done.7), custom_call_target="tpu_custom_call" | custom-call | tf_op jit(solution)/shard_map/pallas_call | solution.py:367
  472.1 6.7 %add_convert_fusion = bf16[1792,1280]{1,0:T(8,128)(2,1)} fusion(f32[1792,8]{1,0:T(8,128)} %bitcast.374, bf16[512,1280]{1,0:T(8,128)(2,1)} %bitcast.383, f32[1792]{0:T(1024)S(1)} %copy-done.48, f32[512]{0:T(512)S(1)} %add_rsqrt_fusion, bf16[256,1792]{1,0:T(8,128)(2,1)} %bitcast.359, bf16[256,1792]{1,0:T(8,128)(2,1)S(1)} %bitcast.318), kind=kOutput, calls=%fused_computation.3 | convolution fusion | flops 2359820288 | bytes 7799808 | tf_op jit(solution)/shard_map/dot_general | solution.py:23
  501.3 8.0 %collective-permute-done.21 = bf16[2,2,56,1792]{3,2,1,0:T(8,128)(2,1)} collective-permute-done((bf16[2,2,56,1792]{3,2,1,0:T(8,128)(2,1)}, bf16[2,2,56,1792]{3,2,1,0:T(8,128)(2,1)}, u32[]{:S(2)}, u32[]{:S(2)}) %collective-permute-start.21) | collective-permute-done | bytes 802848 | tf_op jit(solution)/shard_map/ppermute | solution.py:111
  517.4 37.6 %collective-permute-done.26 = bf16[2,112,2432]{2,1,0:T(8,128)(2,1)S(1)} collective-permute-done((bf16[2,112,2432]{2,1,0:T(8,128)(2,1)}, bf16[2,112,2432]{2,1,0:T(8,128)(2,1)S(1)}, u32[]{:S(2)}, u32[]{:S(2)}) %collective-permute-start.26) | collective-permute-done | bytes 1089568 | tf_op jit(solution)/shard_map/ppermute | solution.py:111
  559.9 10.5 %collective-permute-done.23 = bf16[2,56,1792]{2,1,0:T(8,128)(2,1)S(1)} collective-permute-done((bf16[2,56,1792]{2,1,0:T(8,128)(2,1)S(1)}, bf16[2,56,1792]{2,1,0:T(8,128)(2,1)S(1)}, u32[]{:S(2)}, u32[]{:S(2)}) %collective-permute-start.23) | collective-permute-done | bytes 401440 | tf_op jit(solution)/shard_map/ppermute | solution.py:111
  573.4 27.6 %collective-permute-done.28 = bf16[112,2432]{1,0:T(8,128)(2,1)S(1)} collective-permute-done((bf16[112,2432]{1,0:T(8,128)(2,1)S(1)}, bf16[112,2432]{1,0:T(8,128)(2,1)S(1)}, u32[]{:S(2)}, u32[]{:S(2)}) %collective-permute-start.28) | collective-permute-done | bytes 544800 | tf_op jit(solution)/shard_map/ppermute | solution.py:111
  608.0 11.0 %collective-permute-done.34 = bf16[152,1792]{1,0:T(8,128)(2,1)S(1)} collective-permute-done((bf16[152,1792]{1,0:T(8,128)(2,1)S(1)}, bf16[152,1792]{1,0:T(8,128)(2,1)S(1)}, u32[]{:S(2)}, u32[]{:S(2)}) %collective-permute-start.34) | collective-permute-done | bytes 544800 | tf_op jit(solution)/shard_map/ppermute | solution.py:185
  (337 shorter events, 204.9 us)
Async XLA Ops:
  7.2 110.7 %all-gather.4.cloned.1.call-start = ((), (), s32[]{:S(2)}) async-start(), calls=%async_computation.2 | async-start | bytes 18382848 | tf_op jit(solution)/shard_map/all_gather | solution.py:456
  9.0 10.5 %collective-permute-start.2 = (bf16[56,1792]{1,0:T(8,128)(2,1)}, bf16[56,1792]{1,0:T(8,128)(2,1)S(1)}, u32[]{:S(2)}, u32[]{:S(2)}) collective-permute-start(bf16[56,1792]{1,0:T(8,128)(2,1)} %dynamic-slice_bitcast_fusion.4), channel_id=1, source_target_pairs={{0,8},{1,9},{2,10},{3,11},{4,12},{5,13},{6,14},{7,15},{24,16},{25,... | collective-permute-start | bytes 602120 | tf_op jit(solution)/shard_map/ppermute | solution.py:156
  20.6 205.2 %all-gather.6.cloned.1.call-start = ((), (), s32[]{:S(2)}) async-start(), calls=%async_computation.5 | async-start | bytes 18522112 | tf_op jit(solution)/shard_map/all_gather | solution.py:456
  20.7 22.4 %collective-permute-start.4 = (bf16[152,1792]{1,0:T(8,128)(2,1)S(1)}, bf16[152,1792]{1,0:T(8,128)(2,1)S(1)}, u32[]{:S(2)}, u32[]{:S(2)}) collective-permute-start(bf16[152,1792]{1,0:T(8,128)(2,1)S(1)} %dynamic-slice_bitcast_fusion.3), channel_id=1, source_target_pairs={{0,8},{1,9},{2,10},{3,11},{4,12},{5,13},{6,14},{7,15},{24,16},{25,... | collective-permute-start | bytes 1634312 | tf_op jit(solution)/shard_map/ppermute | solution.py:156
  44.3 454.9 %reduce-scatter.3.cloned.1.call-start = ((), (), s32[]{:S(2)}) async-start(), calls=%async_computation.3 | async-start | bytes 9261056 | tf_op jit(solution)/shard_map/reduce_scatter | solution.py:671
  44.6 40.7 %collective-permute-start.1 = (bf16[2,128,1792]{2,1,0:T(8,128)(2,1)S(1)}, bf16[2,128,1792]{2,1,0:T(8,128)(2,1)}, u32[]{:S(2)}, u32[]{:S(2)}) collective-permute-start(bf16[2,128,1792]{2,1,0:T(8,128)(2,1)S(1)} %bitcast.373), channel_id=1, source_target_pairs={{0,16},{16,0},{1,17},{17,1},{2,18},{18,2},{3,19},{19,3},{4,20},{20... | collective-permute-start | bytes 2752520 | tf_op jit(solution)/shard_map/ppermute | solution.py:64
  64.9 20.5 %collective-permute-start = (s32[2,128]{1,0:T(2,128)S(1)}, s32[2,128]{1,0:T(2,128)S(1)}, u32[]{:S(2)}, u32[]{:S(2)}) collective-permute-start(s32[2,128]{1,0:T(2,128)S(1)} %bitcast.385), channel_id=1, source_target_pairs={{0,16},{16,0},{1,17},{17,1},{2,18},{18,2},{3,19},{19,3},{4,20},{20... | collective-permute-start | bytes 3080 | tf_op jit(solution)/shard_map/ppermute | solution.py:64
  135.8 33.4 %collective-permute-start.3 = (bf16[256,1792]{1,0:T(8,128)(2,1)S(1)}, bf16[256,1792]{1,0:T(8,128)(2,1)S(1)}, u32[]{:S(2)}, u32[]{:S(2)}) collective-permute-start(bf16[256,1792]{1,0:T(8,128)(2,1)S(1)} %convolution_convert_fusion.6), channel_id=1, source_target_pairs={{0,16},{16,0},{1,17},{17,1},{2,18},{18,2},{3,19},{19,3},{4,20},{20... | collective-permute-start | bytes 2752520 | tf_op jit(solution)/shard_map/ppermute | solution.py:64
  171.1 22.2 %collective-permute-start.5 = (bf16[256,1792]{1,0:T(8,128)(2,1)S(1)}, bf16[256,1792]{1,0:T(8,128)(2,1)S(1)}, u32[]{:S(2)}, u32[]{:S(2)}) collective-permute-start(bf16[256,1792]{1,0:T(8,128)(2,1)S(1)} %multiply_convert_fusion.4.rows_ref), channel_id=1, source_target_pairs={{0,16},{16,0},{1,17},{17,1},{2,18},{18,2},{3,19},{19,3},{4,20},{20... | collective-permute-start | bytes 2752520 | tf_op jit(solution)/shard_map/ppermute | solution.py:64
  248.5 27.7 %collective-permute-start.6 = (bf16[256,1792]{1,0:T(8,128)(2,1)}, bf16[256,1792]{1,0:T(8,128)(2,1)}, u32[]{:S(2)}, u32[]{:S(2)}) collective-permute-start(bf16[256,1792]{1,0:T(8,128)(2,1)} %convolution_convert_fusion.5), channel_id=1, source_target_pairs={{0,16},{16,0},{1,17},{17,1},{2,18},{18,2},{3,19},{19,3},{4,20},{20... | collective-permute-start | bytes 2752520 | tf_op jit(solution)/shard_map/ppermute | solution.py:64
  281.1 25.0 %collective-permute-start.11 = (bf16[256,1792]{1,0:T(8,128)(2,1)S(1)}, bf16[256,1792]{1,0:T(8,128)(2,1)S(1)}, u32[]{:S(2)}, u32[]{:S(2)}) collective-permute-start(bf16[256,1792]{1,0:T(8,128)(2,1)S(1)} %multiply_convert_fusion.5), channel_id=1, source_target_pairs={{0,16},{16,0},{1,17},{17,1},{2,18},{18,2},{3,19},{19,3},{4,20},{20... | collective-permute-start | bytes 2752520 | tf_op jit(solution)/shard_map/ppermute | solution.py:64
  316.7 17.6 %collective-permute-start.12 = (bf16[2,2,2,152,1792]{4,3,2,1,0:T(8,128)(2,1)}, bf16[2,2,2,152,1792]{4,3,2,1,0:T(8,128)(2,1)}, u32[]{:S(2)}, u32[]{:S(2)}) collective-permute-start(bf16[2,2,2,152,1792]{4,3,2,1,0:T(8,128)(2,1)} %dynamic-slice_bitcast_fusion.1), channel_id=1, source_target_pairs={{0,1},{1,0},{2,3},{3,2},{4,5},{5,4},{6,7},{7,6},{8,9},{9,8},{10,11... | collective-permute-start | bytes 13074440 | tf_op jit(solution)/shard_map/ppermute | solution.py:111
  334.2 286.3 %reduce-scatter.5.cloned.1.call-start = ((), (), s32[]{:S(2)}) async-start(), calls=%async_computation.4 | async-start | bytes 4874240 | tf_op jit(solution)/shard_map/reduce_scatter | solution.py:735
  358.9 17.4 %collective-permute-start.13 = (bf16[2,2,2,112,2432]{4,3,2,1,0:T(8,128)(2,1)}, bf16[2,2,2,112,2432]{4,3,2,1,0:T(8,128)(2,1)}, u32[]{:S(2)}, u32[]{:S(2)}) collective-permute-start(bf16[2,2,2,112,2432]{4,3,2,1,0:T(8,128)(2,1)} %dynamic-slice_bitcast_fusion), channel_id=1, source_target_pairs={{0,1},{1,0},{2,3},{3,2},{4,5},{5,4},{6,7},{7,6},{8,9},{9,8},{10,11... | collective-permute-start | bytes 13074440 | tf_op jit(solution)/shard_map/ppermute | solution.py:111
  363.5 21.4 %collective-permute-start.14 = (bf16[256,1792]{1,0:T(8,128)(2,1)S(1)}, bf16[256,1792]{1,0:T(8,128)(2,1)S(1)}, u32[]{:S(2)}, u32[]{:S(2)}) collective-permute-start(bf16[256,1792]{1,0:T(8,128)(2,1)S(1)} %copy-done.58), channel_id=1, source_target_pairs={{0,16},{16,0},{1,17},{17,1},{2,18},{18,2},{3,19},{19,3},{4,20},{20... | collective-permute-start | bytes 2752520 | tf_op jit(solution)/shard_map/ppermute | solution.py:64
  368.4 72.0 %collective-permute-start.19 = (bf16[2,2,152,1792]{3,2,1,0:T(8,128)(2,1)}, bf16[2,2,152,1792]{3,2,1,0:T(8,128)(2,1)}, u32[]{:S(2)}, u32[]{:S(2)}) collective-permute-start(bf16[2,2,152,1792]{3,2,1,0:T(8,128)(2,1)} %fusion.1), channel_id=1, source_target_pairs={{0,2},{1,3},{2,0},{3,1},{4,6},{5,7},{6,4},{7,5},{8,10},{9,11},{10,... | collective-permute-start | bytes 6537224 | tf_op jit(solution)/shard_map/ppermute | solution.py:111
  386.3 20.5 %collective-permute-start.17 = (bf16[256,1792]{1,0:T(8,128)(2,1)S(1)}, bf16[256,1792]{1,0:T(8,128)(2,1)S(1)}, u32[]{:S(2)}, u32[]{:S(2)}) collective-permute-start(bf16[256,1792]{1,0:T(8,128)(2,1)S(1)} %get-tuple-element.200), channel_id=1, source_target_pairs={{0,16},{16,0},{1,17},{17,1},{2,18},{18,2},{3,19},{19,3},{4,20},{20... | collective-permute-start | bytes 2752520 | tf_op jit(solution)/shard_map/ppermute | solution.py:64
  411.8 33.5 %collective-permute-start.18 = (bf16[2,2,2,56,1792]{4,3,2,1,0:T(8,128)(2,1)}, bf16[2,2,2,56,1792]{4,3,2,1,0:T(8,128)(2,1)}, u32[]{:S(2)}, u32[]{:S(2)}) collective-permute-start(bf16[2,2,2,56,1792]{4,3,2,1,0:T(8,128)(2,1)} %dynamic-slice_bitcast_fusion.2), channel_id=1, source_target_pairs={{0,1},{1,0},{2,3},{3,2},{4,5},{5,4},{6,7},{7,6},{8,9},{9,8},{10,11... | collective-permute-start | bytes 4816904 | tf_op jit(solution)/shard_map/ppermute | solution.py:111
  411.8 81.1 %collective-permute-start.15 = (bf16[2,2,112,2432]{3,2,1,0:T(8,128)(2,1)}, bf16[2,2,112,2432]{3,2,1,0:T(8,128)(2,1)}, u32[]{:S(2)}, u32[]{:S(2)}) collective-permute-start(bf16[2,2,112,2432]{3,2,1,0:T(8,128)(2,1)} %fusion), channel_id=1, source_target_pairs={{0,2},{1,3},{2,0},{3,1},{4,6},{5,7},{6,4},{7,5},{8,10},{9,11},{10,... | collective-permute-start | bytes 6537224 | tf_op jit(solution)/shard_map/ppermute | solution.py:111
  443.9 55.3 %collective-permute-start.22 = (bf16[2,152,1792]{2,1,0:T(8,128)(2,1)}, bf16[2,152,1792]{2,1,0:T(8,128)(2,1)}, u32[]{:S(2)}, u32[]{:S(2)}) collective-permute-start(bf16[2,152,1792]{2,1,0:T(8,128)(2,1)} %fusion.13), channel_id=1, source_target_pairs={{0,4},{1,5},{2,6},{3,7},{4,0},{5,1},{6,2},{7,3},{8,12},{9,13},{10,... | collective-permute-start | bytes 3268616 | tf_op jit(solution)/shard_map/ppermute | solution.py:111
  464.2 20.7 %collective-permute-start.20 = (bf16[256,1792]{1,0:T(8,128)(2,1)}, bf16[256,1792]{1,0:T(8,128)(2,1)}, u32[]{:S(2)}, u32[]{:S(2)}) collective-permute-start(bf16[256,1792]{1,0:T(8,128)(2,1)} %get-tuple-element.224), channel_id=1, source_target_pairs={{0,16},{16,0},{1,17},{17,1},{2,18},{18,2},{3,19},{19,3},{4,20},{20... | collective-permute-start | bytes 2752520 | tf_op jit(solution)/shard_map/ppermute | solution.py:64
  478.7 30.6 %collective-permute-start.21 = (bf16[2,2,56,1792]{3,2,1,0:T(8,128)(2,1)}, bf16[2,2,56,1792]{3,2,1,0:T(8,128)(2,1)}, u32[]{:S(2)}, u32[]{:S(2)}) collective-permute-start(bf16[2,2,56,1792]{3,2,1,0:T(8,128)(2,1)} %fusion.27), channel_id=1, source_target_pairs={{0,2},{1,3},{2,0},{3,1},{4,6},{5,7},{6,4},{7,5},{8,10},{9,11},{10,... | collective-permute-start | bytes 2408456 | tf_op jit(solution)/shard_map/ppermute | solution.py:111
  496.4 58.7 %collective-permute-start.26 = (bf16[2,112,2432]{2,1,0:T(8,128)(2,1)}, bf16[2,112,2432]{2,1,0:T(8,128)(2,1)S(1)}, u32[]{:S(2)}, u32[]{:S(2)}) collective-permute-start(bf16[2,112,2432]{2,1,0:T(8,128)(2,1)} %fusion.12), channel_id=1, source_target_pairs={{0,4},{1,5},{2,6},{3,7},{4,0},{5,1},{6,2},{7,3},{8,12},{9,13},{10,... | collective-permute-start | bytes 3268616 | tf_op jit(solution)/shard_map/ppermute | solution.py:111
  509.3 47.5 %collective-permute-start.25 = (bf16[152,1792]{1,0:T(8,128)(2,1)S(1)}, bf16[152,1792]{1,0:T(8,128)(2,1)S(1)}, u32[]{:S(2)}, u32[]{:S(2)}) collective-permute-start(bf16[152,1792]{1,0:T(8,128)(2,1)S(1)} %fusion.33), channel_id=1, source_target_pairs={{0,8},{1,9},{2,10},{3,11},{4,12},{5,13},{6,14},{7,15},{8,0},{9,1},... | collective-permute-start | bytes 1634312 | tf_op jit(solution)/shard_map/ppermute | solution.py:111
  513.1 46.8 %collective-permute-start.24 = (bf16[112,2432]{1,0:T(8,128)(2,1)S(1)}, bf16[112,2432]{1,0:T(8,128)(2,1)S(1)}, u32[]{:S(2)}, u32[]{:S(2)}) collective-permute-start(bf16[112,2432]{1,0:T(8,128)(2,1)S(1)} %copy-done.44), channel_id=1, source_target_pairs={{0,16},{16,0},{1,17},{17,1},{2,18},{18,2},{3,19},{19,3},{4,20},{20... | collective-permute-start | bytes 1634312 | tf_op jit(solution)/shard_map/ppermute | solution.py:64
  514.6 55.8 %collective-permute-start.23 = (bf16[2,56,1792]{2,1,0:T(8,128)(2,1)S(1)}, bf16[2,56,1792]{2,1,0:T(8,128)(2,1)S(1)}, u32[]{:S(2)}, u32[]{:S(2)}) collective-permute-start(bf16[2,56,1792]{2,1,0:T(8,128)(2,1)S(1)} %fusion.36), channel_id=1, source_target_pairs={{0,4},{1,5},{2,6},{3,7},{4,0},{5,1},{6,2},{7,3},{8,12},{9,13},{10,... | collective-permute-start | bytes 1204232 | tf_op jit(solution)/shard_map/ppermute | solution.py:111
  556.7 44.3 %collective-permute-start.28 = (bf16[112,2432]{1,0:T(8,128)(2,1)S(1)}, bf16[112,2432]{1,0:T(8,128)(2,1)S(1)}, u32[]{:S(2)}, u32[]{:S(2)}) collective-permute-start(bf16[112,2432]{1,0:T(8,128)(2,1)S(1)} %fusion.32), channel_id=1, source_target_pairs={{0,8},{1,9},{2,10},{3,11},{4,12},{5,13},{6,14},{7,15},{8,0},{9,1},... | collective-permute-start | bytes 1634312 | tf_op jit(solution)/shard_map/ppermute | solution.py:111
  558.8 14.7 %collective-permute-start.29 = (bf16[152,1792]{1,0:T(8,128)(2,1)S(1)}, bf16[152,1792]{1,0:T(8,128)(2,1)S(1)}, u32[]{:S(2)}, u32[]{:S(2)}) collective-permute-start(bf16[152,1792]{1,0:T(8,128)(2,1)S(1)} %fusion.31), channel_id=1, source_target_pairs={{0,16},{16,0},{1,17},{17,1},{2,18},{18,2},{3,19},{19,3},{4,20},{20... | collective-permute-start | bytes 1634312 | tf_op jit(solution)/shard_map/ppermute | solution.py:64
  571.6 33.7 %collective-permute-start.27 = (bf16[56,1792]{1,0:T(8,128)(2,1)S(1)}, bf16[56,1792]{1,0:T(8,128)(2,1)S(1)}, u32[]{:S(2)}, u32[]{:S(2)}) collective-permute-start(bf16[56,1792]{1,0:T(8,128)(2,1)S(1)} %fusion.46), channel_id=1, source_target_pairs={{0,8},{1,9},{2,10},{3,11},{4,12},{5,13},{6,14},{7,15},{8,0},{9,1},... | collective-permute-start | bytes 602120 | tf_op jit(solution)/shard_map/ppermute | solution.py:111
  601.6 17.4 %collective-permute-start.34 = (bf16[152,1792]{1,0:T(8,128)(2,1)S(1)}, bf16[152,1792]{1,0:T(8,128)(2,1)S(1)}, u32[]{:S(2)}, u32[]{:S(2)}) collective-permute-start(bf16[152,1792]{1,0:T(8,128)(2,1)S(1)} %get-tuple-element.376), channel_id=1, source_target_pairs={{0,8},{1,9},{2,10},{3,11},{4,12},{5,13},{6,14},{7,15},{8,0},{9,1},... | collective-permute-start | bytes 1634312 | tf_op jit(solution)/shard_map/ppermute | solution.py:185
  603.4 17.1 %collective-permute-start.33 = (bf16[112,2432]{1,0:T(8,128)(2,1)S(1)}, bf16[112,2432]{1,0:T(8,128)(2,1)S(1)}, u32[]{:S(2)}, u32[]{:S(2)}) collective-permute-start(bf16[112,2432]{1,0:T(8,128)(2,1)S(1)} %fusion.29), channel_id=1, source_target_pairs={{0,16},{16,0},{1,17},{17,1},{2,18},{18,2},{3,19},{19,3},{4,20},{20... | collective-permute-start | bytes 1634312 | tf_op jit(solution)/shard_map/ppermute | solution.py:64
  606.6 13.9 %collective-permute-start.31 = (bf16[56,1792]{1,0:T(8,128)(2,1)S(1)}, bf16[56,1792]{1,0:T(8,128)(2,1)S(1)}, u32[]{:S(2)}, u32[]{:S(2)}) collective-permute-start(bf16[56,1792]{1,0:T(8,128)(2,1)S(1)} %fusion.45), channel_id=1, source_target_pairs={{0,16},{16,0},{1,17},{17,1},{2,18},{18,2},{3,19},{19,3},{4,20},{20... | collective-permute-start | bytes 602120 | tf_op jit(solution)/shard_map/ppermute | solution.py:64
  (77 other events, 889.3 us)
Sparse Core Ops, SparseCore 0:
  20.7 97.1 all-gather.3
  120.0 105.6 all-gather.5
  334.4 142.2 reduce-scatter.2
  480.4 118.6 reduce-scatter.4

commit v4 on v3

--- a/solution.py
+++ b/solution.py
@@ -700,8 +700,7 @@
     dm_k = gather_seq(place, dm_own)
     dm_own, = up.start(dm_own)
     d_mixed_own = dot(dm_own, out_w, ((1,), (1,)))
-    squares = sum_over("seq", seqs, squares)
-    d_mixed_own, squares, *dm_others = place.in_turn(d_mixed_own, squares, *dm_k[1:])
+    d_mixed_own, *dm_others = place.in_turn(d_mixed_own, *dm_k[1:])
     out = by_rows(weight_grad(mixed, jnp.concatenate([dm_own, *dm_others])), x_first)
     dm_others = out.start(*dm_others)
     d_mixed = jnp.concatenate(
@@ -751,6 +750,9 @@
     d_packed, = up.after(d_packed)
     d_packed, = up.start(d_packed)
     d_packed, gate_sum = place.in_turn(d_packed, gate_sum)
+    squares, d_packed = place.in_turn(squares, d_packed)
+    squares = sum_over("seq", seqs, squares)
+    squares, gate_sum = place.in_turn(squares, gate_sum)
     gate_k = gather_seq(place, gate_sum)
     input_grad = to_given(d_packed)
     down.after()

time: 649 us -> 650 us (level)
    ppermute x14, waiting for transfers between devices: 70.5 us -> 77.1 us  [seq_send(): return lax.ppermute(value, 'seq', pairs)]
where the time goes in v4:
time: 650 us; the launch traced here: 644 us
  waiting for transfers between devices  275 us (42%)
  matrix products  113 us (17%)
  starting transfers between devices  83.7 us (13%)
  other arithmetic  58.3 us (9%)
  local copies, waits for them, and re-layouts  50.7 us (8%)
  Pallas kernels  41.6 us (6%)
  between operations  21.6 us (3%)
    ppermute x12, waiting for transfers between devices, send(): got = lax.ppermute(sent, 'fsdp', pairs)  108 us
    dot_general x22, matrix products, dot(): lax.dot_general(left, right, (dims, ((), ())), preferred_element_type=F32)  107 us
    ppermute x14, waiting for transfers between devices, seq_send(): return lax.ppermute(value, 'seq', pairs)  77.1 us
    all_gather x2, waiting for transfers between devices, __init__(): self.raw = [lax.all_gather(buffer, 'fsdp', axis=0, tiled=False)]  58.8 us
    ppermute x14, starting transfers between devices, seq_send(): return lax.ppermute(value, 'seq', pairs)  46.8 us
    convert_element_type x12, other arithmetic, total(): return total.astype(BF16)  28.3 us
    slice x5, local copies, waits for them, and re-layouts, arrays(): t = self.raw[0][:, at:at + count]  19.7 us
    ppermute x2, waiting for transfers between devices, spread_rows(): got = lax.ppermute(sent, ('seq', 'fsdp'), plane_pairs(place, k))  17.4 us
  transfers between devices with their start and end apart: 39, of which 23 were waited for; matrix products, arithmetic and copies ran while one was open for 28% of the time, Pallas kernels for 3%

profile of v4, /device:TPU:0, one launch (start us, length us, event | category | flops | bytes accessed | tf_op | source)
XLA Modules:
  0.0 644.3 jit_solution(14494251975328731203)
XLA Ops:
  9.0 5.9 collective-permute-start.2
  27.1 16.0 %collective-permute-done.4 = bf16[152,1792]{1,0:T(8,128)(2,1)S(1)} collective-permute-done((bf16[152,1792]{1,0:T(8,128)(2,1)S(1)}, bf16[152,1792]{1,0:T(8,128)(2,1)S(1)}, u32[]{:S(2)}, u32[]{:S(2)}) %collective-permute-start.4) | collective-permute-done | bytes 544800 | tf_op jit(solution)/shard_map/ppermute | solution.py:156
  44.6 20.2 %collective-permute-start.1 = (bf16[2,128,1792]{2,1,0:T(8,128)(2,1)S(1)}, bf16[2,128,1792]{2,1,0:T(8,128)(2,1)}, u32[]{:S(2)}, u32[]{:S(2)}) collective-permute-start(bf16[2,128,1792]{2,1,0:T(8,128)(2,1)S(1)} %bitcast.373), channel_id=1, source_target_pairs={{0,16},{16,0},{1,17},{17,1},{2,18},{18,2},{3,19},{19,3},{4,20},{20... | collective-permute-start | bytes 2752520 | tf_op jit(solution)/shard_map/ppermute | solution.py:64
  65.8 19.5 %collective-permute-done = s32[2,128]{1,0:T(2,128)S(1)} collective-permute-done((s32[2,128]{1,0:T(2,128)S(1)}, s32[2,128]{1,0:T(2,128)S(1)}, u32[]{:S(2)}, u32[]{:S(2)}) %collective-permute-start) | collective-permute-done | bytes 1056 | tf_op jit(solution)/shard_map/ppermute | solution.py:64
  87.5 30.4 %all-gather.4.cloned.1.call-done = bf16[16,528,8,128]{3,2,1,0:T(8,128)(2,1)} async-done(((bf16[1,528,8,128]{3,2,1,0:T(8,128)(2,1)}), bf16[16,528,8,128]{3,2,1,0:T(8,128)(2,1)}) %all-gather.4.cloned.1.call-update) | async-done | bytes 17301520 | tf_op jit(solution)/shard_map/all_gather | solution.py:456
  135.8 12.6 %collective-permute-start.3 = (bf16[256,1792]{1,0:T(8,128)(2,1)S(1)}, bf16[256,1792]{1,0:T(8,128)(2,1)S(1)}, u32[]{:S(2)}, u32[]{:S(2)}) collective-permute-start(bf16[256,1792]{1,0:T(8,128)(2,1)S(1)} %convolution_convert_fusion.6), channel_id=1, source_target_pairs={{0,16},{16,0},{1,17},{17,1},{2,18},{18,2},{3,19},{19,3},{4,20},{20... | collective-permute-start | bytes 2752520 | tf_op jit(solution)/shard_map/ppermute | solution.py:64
  150.9 18.3 %collective-permute-done.3 = bf16[256,1792]{1,0:T(8,128)(2,1)S(1)} collective-permute-done((bf16[256,1792]{1,0:T(8,128)(2,1)S(1)}, bf16[256,1792]{1,0:T(8,128)(2,1)S(1)}, u32[]{:S(2)}, u32[]{:S(2)}) %collective-permute-start.3) | collective-permute-done | bytes 917536 | tf_op jit(solution)/shard_map/ppermute | solution.py:64
  173.0 7.6 %slice.146 = bf16[16,266,8,128]{3,2,1,0:T(8,128)(2,1)} slice(bf16[16,528,8,128]{3,2,1,0:T(8,128)(2,1)} %all-gather.4.cloned.1.call-done), slice={[0:16], [140:406], [0:8], [0:128]} | slice | bytes 17432576 | tf_op jit(solution)/shard_map/slice | solution.py:471
  180.6 7.9 %fusion.77.gate_ref = f32[256,2432]{1,0:T(8,128)} fusion(bf16[256,1792]{1,0:T(8,128)(2,1)S(1)} %multiply_convert_fusion.4.rows_ref, bf16[1792,2432]{1,0:T(8,128)(2,1)} %bitcast.338), kind=kOutput, calls=%fused_computation.212 | convolution fusion | flops 2231369728 | bytes 12124160 | tf_op jit(solution)/shard_map/dot_general | solution.py:23
  197.3 28.4 %all-gather.6.cloned.1.call-done = bf16[8512,8,128]{2,1,0:T(8,128)(2,1)} async-done(((bf16[532,8,128]{2,1,0:T(8,128)(2,1)}), bf16[8512,8,128]{2,1,0:T(8,128)(2,1)}) %all-gather.6.cloned.1.call-update) | async-done | bytes 17432592 | tf_op jit(solution)/shard_map/all_gather | solution.py:456
  225.7 12.0 %shard_map.248 = bf16[16,266,8,128]{3,2,1,0:T(8,128)(2,1)} custom-call(bf16[16,532,8,128]{3,2,1,0:T(8,128)(2,1)} %bitcast.312), custom_call_target="tpu_custom_call" | custom-call | tf_op jit(solution)/shard_map/pallas_call | solution.py:397
  237.8 7.2 %shard_map.249 = (f32[256,2432]{1,0:T(8,128)S(1)}, bf16[256,2432]{1,0:T(8,128)(2,1)S(1)}) custom-call(bf16[256,1792]{1,0:T(8,128)(2,1)S(1)} %collective-permute-done.5.rows_ref, bf16[16,28,19,8,128]{4,3,2,1,0:T(8,128)(2,1)} %bitcast.313, f32[256,2432]{1,0:T(8,128)} %fusion.78.gate_ref), custom_call_target="tpu_custom_call" | custom-call | tf_op jit(solution)/shard_map/pallas_call | solution.py:424
  252.9 7.0 %shard_map.247 = (f32[256,2432]{1,0:T(8,128)S(1)}, bf16[256,2432]{1,0:T(8,128)(2,1)S(1)}) custom-call(bf16[256,1792]{1,0:T(8,128)(2,1)S(1)} %multiply_convert_fusion.4.rows_ref, bf16[16,28,19,8,128]{4,3,2,1,0:T(8,128)(2,1)} %bitcast.314, f32[256,2432]{1,0:T(8,128)} %fusion.77.gate_ref), custom_call_target="tpu_custom_call" | custom-call | tf_op jit(solution)/shard_map/pallas_call | solution.py:424
  261.4 7.3 %fusion.79 = f32[256,1792]{1,0:T(8,128)} fusion(bf16[256,2432]{1,0:T(8,128)(2,1)S(1)} %get-tuple-element.155, bf16[2432,1792]{1,0:T(8,128)(2,1)} %bitcast.324), kind=kOutput, calls=%fused_computation.214 | convolution fusion | flops 2231369728 | bytes 11796480 | tf_op jit(solution)/shard_map/dot_general | solution.py:23
  268.6 7.5 %slice.115 = bf16[16,266,8,128]{3,2,1,0:T(8,128)(2,1)} slice(bf16[16,532,8,128]{3,2,1,0:T(8,128)(2,1)} %bitcast.315), slice={[0:16], [0:266], [0:8], [0:128]} | slice | bytes 17432576 | tf_op jit(solution)/shard_map/slice | solution.py:471
  283.3 8.0 %multiply_convert_fusion.2 = (bf16[256,2432]{1,0:T(8,128)(2,1)}, bf16[256,2432]{1,0:T(8,128)(2,1)}) fusion(f32[256,2432]{1,0:T(8,128)S(1)} %copy-done.35, f32[256,2432]{1,0:T(8,128)S(1)} %copy-done.9, bf16[256,1792]{1,0:T(8,128)(2,1)S(1)} %multiply_convert_fusion.5, bf16[2432,1792]{1,0:T(8,128)(2,1)} %bitcast.325), kind=kOutput, calls=%fused_computation.36 | convolution fusion | flops 2239463424 | bytes 17104896 | tf_op jit(solution)/shard_map/dot_general | solution.py:23
  316.7 6.5 %fusion.80 = f32[256,2432]{1,0:T(8,128)S(1)} fusion(bf16[256,1792]{1,0:T(8,128)(2,1)} %copy-done.56, bf16[2432,1792]{1,0:T(8,128)(2,1)} %bitcast.326), kind=kOutput, calls=%fused_computation.215 | convolution fusion | flops 2231369728 | bytes 12124160 | tf_op jit(solution)/shard_map/dot_general | solution.py:23
  327.0 7.2 %convolution_convert_fusion.1 = bf16[1792,2432]{1,0:T(8,128)(2,1)} fusion(bf16[256,2432]{1,0:T(8,128)(2,1)S(1)} %get-tuple-element.181, bf16[256,2432]{1,0:T(8,128)(2,1)S(1)} %copy-done.59, bf16[256,1792]{1,0:T(8,128)(2,1)S(1)} %collective-permute-done.5.rows_ref, bf16[256,1792]{1,0:T(8,128)(2,1)S(1)} %multiply_convert_fusion.4.rows_ref), kind=kOutput, calls=%fused_computation.1 | convolution fusion | flops 4475748352 | bytes 13041664 | tf_op jit(solution)/shard_map/dot_general | solution.py:23
  338.6 6.8 %fusion.81 = f32[256,1792]{1,0:T(8,128)S(1)} fusion(bf16[256,2432]{1,0:T(8,128)(2,1)S(1)} %copy-done.39, bf16[1792,2432]{1,0:T(8,128)(2,1)} %bitcast.339), kind=kOutput, calls=%fused_computation.216 | convolution fusion | flops 2231369728 | bytes 11796480 | tf_op jit(solution)/shard_map/dot_general | solution.py:23
  349.0 7.5 %convolution_convert_fusion = bf16[1792,2432]{1,0:T(8,128)(2,1)S(1)} fusion(bf16[512,2432]{1,0:T(8,128)(2,1)} %pad_maximum_fusion, bf16[256,1792]{1,0:T(8,128)(2,1)S(1)} %collective-permute-done.5.rows_ref, bf16[256,1792]{1,0:T(8,128)(2,1)S(1)} %multiply_convert_fusion.4.rows_ref), kind=kOutput, calls=%fused_computation | convolution fusion | flops 4470767616 | bytes 13041664 | tf_op jit(solution)/shard_map/dot_general | solution.py:23
  365.5 7.4 %convolution_add_fusion = f32[256,1792]{1,0:T(8,128)S(1)} fusion(f32[256,1792]{1,0:T(8,128)} %fusion.82, bf16[256,2432]{1,0:T(8,128)(2,1)S(1)} %copy-done.37, bf16[1792,2432]{1,0:T(8,128)(2,1)} %bitcast.344), kind=kOutput, calls=%fused_computation.21 | convolution fusion | flops 2231828480 | bytes 13631488 | tf_op jit(solution)/shard_map/dot_general | solution.py:23
  372.9 8.8 %collective-permute-done.14 = bf16[256,1792]{1,0:T(8,128)(2,1)S(1)} collective-permute-done((bf16[256,1792]{1,0:T(8,128)(2,1)S(1)}, bf16[256,1792]{1,0:T(8,128)(2,1)S(1)}, u32[]{:S(2)}, u32[]{:S(2)}) %collective-permute-start.14) | collective-permute-done | bytes 917536 | tf_op jit(solution)/shard_map/ppermute | solution.py:64
  389.8 14.9 %collective-permute-done.16 = bf16[256,1792]{1,0:T(8,128)(2,1)S(1)} collective-permute-done((bf16[256,1792]{1,0:T(8,128)(2,1)S(1)}, bf16[256,1792]{1,0:T(8,128)(2,1)S(1)}, u32[]{:S(2)}, u32[]{:S(2)}) %collective-permute-start.16) | collective-permute-done | bytes 917536 | tf_op jit(solution)/shard_map/ppermute | solution.py:64
  416.4 21.7 %collective-permute-done.18 = bf16[2,2,152,1792]{3,2,1,0:T(8,128)(2,1)} collective-permute-done((bf16[2,2,152,1792]{3,2,1,0:T(8,128)(2,1)}, bf16[2,2,152,1792]{3,2,1,0:T(8,128)(2,1)}, u32[]{:S(2)}, u32[]{:S(2)}) %collective-permute-start.18) | collective-permute-done | bytes 2179104 | tf_op jit(solution)/shard_map/ppermute | solution.py:111
  445.5 11.7 %shard_map.250 = (bf16[2,2,128,1280]{3,2,1,0:T(8,128)(2,1)}, f32[2,8,896]{2,1,0:T(8,128)}) custom-call(s32[1]{0:T(128)} %bitcast.3.y_ref, bf16[2,2,128,1280]{3,2,1,0:T(8,128)(2,1)} %bitcast.310, f32[2,2,128,896]{3,2,1,0:T(8,128)} %bitcast.348, f32[8,896]{1,0:T(8,128)} %copy-done.6, s32[2,256,1]{2,1,0:T(8,128)} %copy-done.5, s32[2,1,256]{2,1,0:T(1,128)} %copy-done.7), custom_call_target="tpu_custom_call" | custom-call | tf_op jit(solution)/shard_map/pallas_call | solution.py:367
  469.8 6.7 %add_convert_fusion = bf16[1792,1280]{1,0:T(8,128)(2,1)} fusion(f32[1792,8]{1,0:T(8,128)} %bitcast.374, bf16[512,1280]{1,0:T(8,128)(2,1)} %bitcast.383, f32[1792]{0:T(1024)S(1)} %copy-done.48, f32[512]{0:T(512)S(1)} %add_rsqrt_fusion, bf16[256,1792]{1,0:T(8,128)(2,1)} %bitcast.359, bf16[256,1792]{1,0:T(8,128)(2,1)S(1)} %bitcast.318), kind=kOutput, calls=%fused_computation.3 | convolution fusion | flops 2359820288 | bytes 7799808 | tf_op jit(solution)/shard_map/dot_general | solution.py:23
  503.5 9.4 %collective-permute-done.20 = bf16[2,2,56,1792]{3,2,1,0:T(8,128)(2,1)} collective-permute-done((bf16[2,2,56,1792]{3,2,1,0:T(8,128)(2,1)}, bf16[2,2,56,1792]{3,2,1,0:T(8,128)(2,1)}, u32[]{:S(2)}, u32[]{:S(2)}) %collective-permute-start.20) | collective-permute-done | bytes 802848 | tf_op jit(solution)/shard_map/ppermute | solution.py:111
  519.0 15.9 %collective-permute-done.26 = bf16[2,112,2432]{2,1,0:T(8,128)(2,1)S(1)} collective-permute-done((bf16[2,112,2432]{2,1,0:T(8,128)(2,1)}, bf16[2,112,2432]{2,1,0:T(8,128)(2,1)S(1)}, u32[]{:S(2)}, u32[]{:S(2)}) %collective-permute-start.26) | collective-permute-done | bytes 1089568 | tf_op jit(solution)/shard_map/ppermute | solution.py:111
  538.8 34.5 %collective-permute-done.25 = bf16[152,1792]{1,0:T(8,128)(2,1)S(1)} collective-permute-done((bf16[152,1792]{1,0:T(8,128)(2,1)S(1)}, bf16[152,1792]{1,0:T(8,128)(2,1)S(1)}, u32[]{:S(2)}, u32[]{:S(2)}) %collective-permute-start.25) | collective-permute-done | bytes 544800 | tf_op jit(solution)/shard_map/ppermute | solution.py:111
  584.6 17.5 %collective-permute-done.28 = bf16[112,2432]{1,0:T(8,128)(2,1)S(1)} collective-permute-done((bf16[112,2432]{1,0:T(8,128)(2,1)S(1)}, bf16[112,2432]{1,0:T(8,128)(2,1)S(1)}, u32[]{:S(2)}, u32[]{:S(2)}) %collective-permute-start.28) | collective-permute-done | bytes 544800 | tf_op jit(solution)/shard_map/ppermute | solution.py:111
  605.9 6.4 collective-permute-done.27
  625.5 6.0 collective-permute-done.32
  (337 shorter events, 217.7 us)
Async XLA Ops:
  7.2 110.7 %all-gather.4.cloned.1.call-start = ((), (), s32[]{:S(2)}) async-start(), calls=%async_computation.2 | async-start | bytes 18382848 | tf_op jit(solution)/shard_map/all_gather | solution.py:456
  9.0 10.5 %collective-permute-start.2 = (bf16[56,1792]{1,0:T(8,128)(2,1)}, bf16[56,1792]{1,0:T(8,128)(2,1)S(1)}, u32[]{:S(2)}, u32[]{:S(2)}) collective-permute-start(bf16[56,1792]{1,0:T(8,128)(2,1)} %dynamic-slice_bitcast_fusion.4), channel_id=1, source_target_pairs={{0,8},{1,9},{2,10},{3,11},{4,12},{5,13},{6,14},{7,15},{24,16},{25,... | collective-permute-start | bytes 602120 | tf_op jit(solution)/shard_map/ppermute | solution.py:156
  20.6 205.2 %all-gather.6.cloned.1.call-start = ((), (), s32[]{:S(2)}) async-start(), calls=%async_computation.5 | async-start | bytes 18522112 | tf_op jit(solution)/shard_map/all_gather | solution.py:456
  20.7 22.4 %collective-permute-start.4 = (bf16[152,1792]{1,0:T(8,128)(2,1)S(1)}, bf16[152,1792]{1,0:T(8,128)(2,1)S(1)}, u32[]{:S(2)}, u32[]{:S(2)}) collective-permute-start(bf16[152,1792]{1,0:T(8,128)(2,1)S(1)} %dynamic-slice_bitcast_fusion.3), channel_id=1, source_target_pairs={{0,8},{1,9},{2,10},{3,11},{4,12},{5,13},{6,14},{7,15},{24,16},{25,... | collective-permute-start | bytes 1634312 | tf_op jit(solution)/shard_map/ppermute | solution.py:156
  44.3 452.9 %reduce-scatter.3.cloned.1.call-start = ((), (), s32[]{:S(2)}) async-start(), calls=%async_computation.3 | async-start | bytes 9261056 | tf_op jit(solution)/shard_map/reduce_scatter | solution.py:671
  44.6 40.7 %collective-permute-start.1 = (bf16[2,128,1792]{2,1,0:T(8,128)(2,1)S(1)}, bf16[2,128,1792]{2,1,0:T(8,128)(2,1)}, u32[]{:S(2)}, u32[]{:S(2)}) collective-permute-start(bf16[2,128,1792]{2,1,0:T(8,128)(2,1)S(1)} %bitcast.373), channel_id=1, source_target_pairs={{0,16},{16,0},{1,17},{17,1},{2,18},{18,2},{3,19},{19,3},{4,20},{20... | collective-permute-start | bytes 2752520 | tf_op jit(solution)/shard_map/ppermute | solution.py:64
  64.9 20.5 %collective-permute-start = (s32[2,128]{1,0:T(2,128)S(1)}, s32[2,128]{1,0:T(2,128)S(1)}, u32[]{:S(2)}, u32[]{:S(2)}) collective-permute-start(s32[2,128]{1,0:T(2,128)S(1)} %bitcast.385), channel_id=1, source_target_pairs={{0,16},{16,0},{1,17},{17,1},{2,18},{18,2},{3,19},{19,3},{4,20},{20... | collective-permute-start | bytes 3080 | tf_op jit(solution)/shard_map/ppermute | solution.py:64
  135.8 33.4 %collective-permute-start.3 = (bf16[256,1792]{1,0:T(8,128)(2,1)S(1)}, bf16[256,1792]{1,0:T(8,128)(2,1)S(1)}, u32[]{:S(2)}, u32[]{:S(2)}) collective-permute-start(bf16[256,1792]{1,0:T(8,128)(2,1)S(1)} %convolution_convert_fusion.6), channel_id=1, source_target_pairs={{0,16},{16,0},{1,17},{17,1},{2,18},{18,2},{3,19},{19,3},{4,20},{20... | collective-permute-start | bytes 2752520 | tf_op jit(solution)/shard_map/ppermute | solution.py:64
  171.1 22.2 %collective-permute-start.5 = (bf16[256,1792]{1,0:T(8,128)(2,1)S(1)}, bf16[256,1792]{1,0:T(8,128)(2,1)S(1)}, u32[]{:S(2)}, u32[]{:S(2)}) collective-permute-start(bf16[256,1792]{1,0:T(8,128)(2,1)S(1)} %multiply_convert_fusion.4.rows_ref), channel_id=1, source_target_pairs={{0,16},{16,0},{1,17},{17,1},{2,18},{18,2},{3,19},{19,3},{4,20},{20... | collective-permute-start | bytes 2752520 | tf_op jit(solution)/shard_map/ppermute | solution.py:64
  248.5 27.7 %collective-permute-start.6 = (bf16[256,1792]{1,0:T(8,128)(2,1)}, bf16[256,1792]{1,0:T(8,128)(2,1)}, u32[]{:S(2)}, u32[]{:S(2)}) collective-permute-start(bf16[256,1792]{1,0:T(8,128)(2,1)} %convolution_convert_fusion.5), channel_id=1, source_target_pairs={{0,16},{16,0},{1,17},{17,1},{2,18},{18,2},{3,19},{19,3},{4,20},{20... | collective-permute-start | bytes 2752520 | tf_op jit(solution)/shard_map/ppermute | solution.py:64
  281.0 10.3 %collective-permute-start.7 = (f32[1,1]{1,0:T(1,128)}, f32[1,1]{1,0:T(1,128)}, u32[]{:S(2)}, u32[]{:S(2)}) collective-permute-start(f32[1,1]{1,0:T(1,128)} %bitcast.67), channel_id=1, source_target_pairs={{0,1},{1,0},{2,3},{3,2},{4,5},{5,4},{6,7},{7,6},{8,9},{9,8},{10,11... | collective-permute-start | bytes 20 | tf_op jit(solution)/shard_map/ppermute | solution.py:193
  281.1 25.0 %collective-permute-start.11 = (bf16[256,1792]{1,0:T(8,128)(2,1)S(1)}, bf16[256,1792]{1,0:T(8,128)(2,1)S(1)}, u32[]{:S(2)}, u32[]{:S(2)}) collective-permute-start(bf16[256,1792]{1,0:T(8,128)(2,1)S(1)} %multiply_convert_fusion.5), channel_id=1, source_target_pairs={{0,16},{16,0},{1,17},{17,1},{2,18},{18,2},{3,19},{19,3},{4,20},{20... | collective-permute-start | bytes 2752520 | tf_op jit(solution)/shard_map/ppermute | solution.py:64
  316.7 17.6 %collective-permute-start.12 = (bf16[2,2,2,152,1792]{4,3,2,1,0:T(8,128)(2,1)}, bf16[2,2,2,152,1792]{4,3,2,1,0:T(8,128)(2,1)}, u32[]{:S(2)}, u32[]{:S(2)}) collective-permute-start(bf16[2,2,2,152,1792]{4,3,2,1,0:T(8,128)(2,1)} %dynamic-slice_bitcast_fusion.1), channel_id=1, source_target_pairs={{0,1},{1,0},{2,3},{3,2},{4,5},{5,4},{6,7},{7,6},{8,9},{9,8},{10,11... | collective-permute-start | bytes 13074440 | tf_op jit(solution)/shard_map/ppermute | solution.py:111
  334.2 288.1 %reduce-scatter.5.cloned.1.call-start = ((), (), s32[]{:S(2)}) async-start(), calls=%async_computation.4 | async-start | bytes 4874240 | tf_op jit(solution)/shard_map/reduce_scatter | solution.py:734
  358.9 14.0 %collective-permute-start.13 = (bf16[2,2,2,112,2432]{4,3,2,1,0:T(8,128)(2,1)}, bf16[2,2,2,112,2432]{4,3,2,1,0:T(8,128)(2,1)}, u32[]{:S(2)}, u32[]{:S(2)}) collective-permute-start(bf16[2,2,2,112,2432]{4,3,2,1,0:T(8,128)(2,1)} %dynamic-slice_bitcast_fusion), channel_id=1, source_target_pairs={{0,1},{1,0},{2,3},{3,2},{4,5},{5,4},{6,7},{7,6},{8,9},{9,8},{10,11... | collective-permute-start | bytes 13074440 | tf_op jit(solution)/shard_map/ppermute | solution.py:111
  359.4 22.3 %collective-permute-start.14 = (bf16[256,1792]{1,0:T(8,128)(2,1)S(1)}, bf16[256,1792]{1,0:T(8,128)(2,1)S(1)}, u32[]{:S(2)}, u32[]{:S(2)}) collective-permute-start(bf16[256,1792]{1,0:T(8,128)(2,1)S(1)} %copy-done.58), channel_id=1, source_target_pairs={{0,16},{16,0},{1,17},{17,1},{2,18},{18,2},{3,19},{19,3},{4,20},{20... | collective-permute-start | bytes 2752520 | tf_op jit(solution)/shard_map/ppermute | solution.py:64
  364.2 73.9 %collective-permute-start.18 = (bf16[2,2,152,1792]{3,2,1,0:T(8,128)(2,1)}, bf16[2,2,152,1792]{3,2,1,0:T(8,128)(2,1)}, u32[]{:S(2)}, u32[]{:S(2)}) collective-permute-start(bf16[2,2,152,1792]{3,2,1,0:T(8,128)(2,1)} %fusion.1), channel_id=1, source_target_pairs={{0,2},{1,3},{2,0},{3,1},{4,6},{5,7},{6,4},{7,5},{8,10},{9,11},{10,... | collective-permute-start | bytes 6537224 | tf_op jit(solution)/shard_map/ppermute | solution.py:111
  383.1 21.6 %collective-permute-start.16 = (bf16[256,1792]{1,0:T(8,128)(2,1)S(1)}, bf16[256,1792]{1,0:T(8,128)(2,1)S(1)}, u32[]{:S(2)}, u32[]{:S(2)}) collective-permute-start(bf16[256,1792]{1,0:T(8,128)(2,1)S(1)} %get-tuple-element.206), channel_id=1, source_target_pairs={{0,16},{16,0},{1,17},{17,1},{2,18},{18,2},{3,19},{19,3},{4,20},{20... | collective-permute-start | bytes 2752520 | tf_op jit(solution)/shard_map/ppermute | solution.py:64
  409.7 33.3 %collective-permute-start.17 = (bf16[2,2,2,56,1792]{4,3,2,1,0:T(8,128)(2,1)}, bf16[2,2,2,56,1792]{4,3,2,1,0:T(8,128)(2,1)}, u32[]{:S(2)}, u32[]{:S(2)}) collective-permute-start(bf16[2,2,2,56,1792]{4,3,2,1,0:T(8,128)(2,1)} %dynamic-slice_bitcast_fusion.2), channel_id=1, source_target_pairs={{0,1},{1,0},{2,3},{3,2},{4,5},{5,4},{6,7},{7,6},{8,9},{9,8},{10,11... | collective-permute-start | bytes 4816904 | tf_op jit(solution)/shard_map/ppermute | solution.py:111
  409.7 79.8 %collective-permute-start.15 = (bf16[2,2,112,2432]{3,2,1,0:T(8,128)(2,1)}, bf16[2,2,112,2432]{3,2,1,0:T(8,128)(2,1)}, u32[]{:S(2)}, u32[]{:S(2)}) collective-permute-start(bf16[2,2,112,2432]{3,2,1,0:T(8,128)(2,1)} %fusion), channel_id=1, source_target_pairs={{0,2},{1,3},{2,0},{3,1},{4,6},{5,7},{6,4},{7,5},{8,10},{9,11},{10,... | collective-permute-start | bytes 6537224 | tf_op jit(solution)/shard_map/ppermute | solution.py:111
  441.5 60.1 %collective-permute-start.21 = (bf16[2,152,1792]{2,1,0:T(8,128)(2,1)}, bf16[2,152,1792]{2,1,0:T(8,128)(2,1)}, u32[]{:S(2)}, u32[]{:S(2)}) collective-permute-start(bf16[2,152,1792]{2,1,0:T(8,128)(2,1)} %fusion.13), channel_id=1, source_target_pairs={{0,4},{1,5},{2,6},{3,7},{4,0},{5,1},{6,2},{7,3},{8,12},{9,13},{10,... | collective-permute-start | bytes 3268616 | tf_op jit(solution)/shard_map/ppermute | solution.py:111
  461.9 20.2 %collective-permute-start.19 = (bf16[256,1792]{1,0:T(8,128)(2,1)}, bf16[256,1792]{1,0:T(8,128)(2,1)}, u32[]{:S(2)}, u32[]{:S(2)}) collective-permute-start(bf16[256,1792]{1,0:T(8,128)(2,1)} %get-tuple-element.229), channel_id=1, source_target_pairs={{0,16},{16,0},{1,17},{17,1},{2,18},{18,2},{3,19},{19,3},{4,20},{20... | collective-permute-start | bytes 2752520 | tf_op jit(solution)/shard_map/ppermute | solution.py:64
  492.9 42.1 %collective-permute-start.26 = (bf16[2,112,2432]{2,1,0:T(8,128)(2,1)}, bf16[2,112,2432]{2,1,0:T(8,128)(2,1)S(1)}, u32[]{:S(2)}, u32[]{:S(2)}) collective-permute-start(bf16[2,112,2432]{2,1,0:T(8,128)(2,1)} %fusion.12), channel_id=1, source_target_pairs={{0,4},{1,5},{2,6},{3,7},{4,0},{5,1},{6,2},{7,3},{8,12},{9,13},{10,... | collective-permute-start | bytes 3268616 | tf_op jit(solution)/shard_map/ppermute | solution.py:111
  494.4 18.6 %collective-permute-start.20 = (bf16[2,2,56,1792]{3,2,1,0:T(8,128)(2,1)}, bf16[2,2,56,1792]{3,2,1,0:T(8,128)(2,1)}, u32[]{:S(2)}, u32[]{:S(2)}) collective-permute-start(bf16[2,2,56,1792]{3,2,1,0:T(8,128)(2,1)} %fusion.27), channel_id=1, source_target_pairs={{0,2},{1,3},{2,0},{3,1},{4,6},{5,7},{6,4},{7,5},{8,10},{9,11},{10,... | collective-permute-start | bytes 2408456 | tf_op jit(solution)/shard_map/ppermute | solution.py:111
  513.0 60.3 %collective-permute-start.25 = (bf16[152,1792]{1,0:T(8,128)(2,1)S(1)}, bf16[152,1792]{1,0:T(8,128)(2,1)S(1)}, u32[]{:S(2)}, u32[]{:S(2)}) collective-permute-start(bf16[152,1792]{1,0:T(8,128)(2,1)S(1)} %fusion.33), channel_id=1, source_target_pairs={{0,8},{1,9},{2,10},{3,11},{4,12},{5,13},{6,14},{7,15},{8,0},{9,1},... | collective-permute-start | bytes 1634312 | tf_op jit(solution)/shard_map/ppermute | solution.py:111
  517.0 59.7 %collective-permute-start.24 = (bf16[112,2432]{1,0:T(8,128)(2,1)S(1)}, bf16[112,2432]{1,0:T(8,128)(2,1)S(1)}, u32[]{:S(2)}, u32[]{:S(2)}) collective-permute-start(bf16[112,2432]{1,0:T(8,128)(2,1)S(1)} %copy-done.44), channel_id=1, source_target_pairs={{0,16},{16,0},{1,17},{17,1},{2,18},{18,2},{3,19},{19,3},{4,20},{20... | collective-permute-start | bytes 1634312 | tf_op jit(solution)/shard_map/ppermute | solution.py:64
  518.2 58.5 %collective-permute-start.23 = (bf16[2,56,1792]{2,1,0:T(8,128)(2,1)S(1)}, bf16[2,56,1792]{2,1,0:T(8,128)(2,1)S(1)}, u32[]{:S(2)}, u32[]{:S(2)}) collective-permute-start(bf16[2,56,1792]{2,1,0:T(8,128)(2,1)S(1)} %fusion.36), channel_id=1, source_target_pairs={{0,4},{1,5},{2,6},{3,7},{4,0},{5,1},{6,2},{7,3},{8,12},{9,13},{10,... | collective-permute-start | bytes 1204232 | tf_op jit(solution)/shard_map/ppermute | solution.py:111
  536.6 65.5 %collective-permute-start.28 = (bf16[112,2432]{1,0:T(8,128)(2,1)S(1)}, bf16[112,2432]{1,0:T(8,128)(2,1)S(1)}, u32[]{:S(2)}, u32[]{:S(2)}) collective-permute-start(bf16[112,2432]{1,0:T(8,128)(2,1)S(1)} %fusion.32), channel_id=1, source_target_pairs={{0,8},{1,9},{2,10},{3,11},{4,12},{5,13},{6,14},{7,15},{8,0},{9,1},... | collective-permute-start | bytes 1634312 | tf_op jit(solution)/shard_map/ppermute | solution.py:111
  577.9 34.4 %collective-permute-start.27 = (bf16[56,1792]{1,0:T(8,128)(2,1)S(1)}, bf16[56,1792]{1,0:T(8,128)(2,1)S(1)}, u32[]{:S(2)}, u32[]{:S(2)}) collective-permute-start(bf16[56,1792]{1,0:T(8,128)(2,1)S(1)} %fusion.46), channel_id=1, source_target_pairs={{0,8},{1,9},{2,10},{3,11},{4,12},{5,13},{6,14},{7,15},{8,0},{9,1},... | collective-permute-start | bytes 602120 | tf_op jit(solution)/shard_map/ppermute | solution.py:111
  602.6 18.1 %collective-permute-start.34 = (bf16[152,1792]{1,0:T(8,128)(2,1)S(1)}, bf16[152,1792]{1,0:T(8,128)(2,1)S(1)}, u32[]{:S(2)}, u32[]{:S(2)}) collective-permute-start(bf16[152,1792]{1,0:T(8,128)(2,1)S(1)} %get-tuple-element.386), channel_id=1, source_target_pairs={{0,8},{1,9},{2,10},{3,11},{4,12},{5,13},{6,14},{7,15},{8,0},{9,1},... | collective-permute-start | bytes 1634312 | tf_op jit(solution)/shard_map/ppermute | solution.py:185
  604.5 17.8 %collective-permute-start.33 = (bf16[112,2432]{1,0:T(8,128)(2,1)S(1)}, bf16[112,2432]{1,0:T(8,128)(2,1)S(1)}, u32[]{:S(2)}, u32[]{:S(2)}) collective-permute-start(bf16[112,2432]{1,0:T(8,128)(2,1)S(1)} %fusion.29), channel_id=1, source_target_pairs={{0,16},{16,0},{1,17},{17,1},{2,18},{18,2},{3,19},{19,3},{4,20},{20... | collective-permute-start | bytes 1634312 | tf_op jit(solution)/shard_map/ppermute | solution.py:64
  622.7 9.9 %collective-permute-start.30 = (bf16[112,1280]{1,0:T(8,128)(2,1)}, bf16[112,1280]{1,0:T(8,128)(2,1)S(1)}, u32[]{:S(2)}, u32[]{:S(2)}) collective-permute-start(bf16[112,1280]{1,0:T(8,128)(2,1)} %reduce-scatter.5.cloned.1.call-done), channel_id=1, source_target_pairs={{0,16},{16,0},{1,17},{17,1},{2,18},{18,2},{3,19},{19,3},{4,20},{20... | collective-permute-start | bytes 860168 | tf_op jit(solution)/shard_map/ppermute | solution.py:64
  (77 other events, 865.0 us)
Sparse Core Ops, SparseCore 0:
  20.7 97.1 all-gather.3
  120.0 105.6 all-gather.5
  334.4 144.7 reduce-scatter.2
  482.9 106.6 reduce-scatter.4
